TPU v7x, 256 devices: a whole 4x4x8 slice. The times are simulated.
256 devices in a mesh: seq: 32 (over x, z), fsdp: 8 (over y, core).
Axes of the slice: x: 4, y: 4, z: 8, core: 2. Of those that a mesh axis runs over, the one named last changes fastest.
Arguments:
- frames: bfloat16 [8, 4096, 1536], P('fsdp', 'seq'), may hold values from -6 to 6
- lengths: int32 [8, 4], P('fsdp'), may hold values from 1 to 2048, 4096 in all within a row
- offsets: int32 [8, 33], P('fsdp'), may hold values from 0 to 4096, as said below
- w_in: bfloat16 [1536, 3072], P('fsdp'), may hold values from -0.15625 to 0.15625
- kernel: float32 [31, 1536], replicated, may hold values from -1 to 1
- cotangent: bfloat16 [8, 8192, 1536], P('fsdp', 'seq'), may hold values from -6 to 6
Outputs:
- owner_output: bfloat16 [8, 8192, 1536], P('fsdp', 'seq')
- frame_grad: bfloat16 [8, 4096, 1536], P('fsdp', 'seq')
- w_grad: float32 [1536, 3072], P(('seq', 'fsdp'))
Inputs may be any that keep to these rules, and one draw needn't show every extreme that they name: Row g: device i of seq owns the frames offsets[g, i] to offsets[g, i + 1] - 1; offsets[g, 0] = 0 and offsets[g, 32] = 4096; each device owns 128 // 4 to 256 frames, beginning within 64 of i * 128; in every group one device owns exactly 256. `lengths`: each row sums to 4096; its largest entry is exactly 2048.
All inputs are finite; a program needn't handle non-finite values.
Results may differ from a plain program's by a relative error of at most 0.025.
Values may be sent and summed in bfloat16 or wider, within the bound.
No kernel may reach another device: no remote copies, remote signals or barrier semaphores. Data moves between devices by JAX's collectives and lax.ppermute only.
A program may use at most 128 MiB of HBM per device.

v0:
```python
import math

import jax
import jax.numpy as jnp
from jax import lax
from jax.sharding import PartitionSpec as P

epsilon = 1e-05


def passed_along(value, axis, steps):
    count = lax.axis_size(axis)
    initial, last = (max(0, -steps), min(count, count - steps))
    return lax.ppermute(value, axis, [(source, source + steps) for source in range(initial, last)])


def normalize_rows(values):
    values = values.astype(jnp.float32)
    center = jnp.mean(values, axis=-1, keepdims=True)
    shifted = values - center
    scale_inv = lax.rsqrt(jnp.mean(shifted * shifted, axis=-1, keepdims=True) + epsilon)
    return (shifted * scale_inv, scale_inv)


def norm_backward(upstream, normed, scale_inv):
    first_mean = jnp.mean(upstream, axis=-1, keepdims=True)
    second_mean = jnp.mean(upstream * normed, axis=-1, keepdims=True)
    return scale_inv * (upstream - first_mean - normed * second_mean)


def depthwise(window, kernel, labels, row_count):
    tap_count = kernel.shape[0]
    half_width = tap_count // 2
    centre = labels[half_width : half_width + row_count]
    result = jnp.zeros((row_count, kernel.shape[1]), jnp.float32)
    for tap_index in range(tap_count):
        same_utt = (labels[tap_index : tap_index + row_count] == centre).astype(jnp.float32)
        result = (
            result
            + kernel[tap_index]
            * window[tap_index : tap_index + row_count].astype(jnp.float32)
            * same_utt[:, None]
        )
    return result


def depthwise_back(window, kernel, labels, row_count):
    tap_count = kernel.shape[0]
    half_width = tap_count // 2
    centre = labels[half_width : half_width + row_count]
    result = jnp.zeros((row_count, kernel.shape[1]), jnp.float32)
    for tap_index in range(tap_count):
        tap_row = 2 * half_width - tap_index
        same_utt = (labels[tap_row : tap_row + row_count] == centre).astype(jnp.float32)
        result = (
            result + kernel[tap_index] * window[tap_row : tap_row + row_count] * same_utt[:, None]
        )
    return result


def finish(d_glu, values, gates, hidden, normed, scale_inv, backward_product):
    d_mixed = jnp.concatenate(
        [d_glu * gates, d_glu * values * gates * (1.0 - gates)], axis=1
    ).astype(jnp.bfloat16)
    d_hidden = backward_product(d_mixed)
    d_rows = norm_backward(d_hidden, normed, scale_inv).astype(jnp.bfloat16)
    partial_sum = lax.dot_general(
        hidden, d_mixed, (((0,), (0,)), ((), ())), preferred_element_type=jnp.float32
    )
    return (d_rows, partial_sum)


def on_device(frames, lengths, offsets, w_in, kernel, cotangent):
    rows_in = frames[0]
    per_device = rows_in.shape[0]
    model_width = rows_in.shape[1]
    capacity = 2 * per_device
    seq_count = lax.axis_size("seq")
    group_count = lax.axis_size("fsdp")
    device = lax.axis_index("seq")
    frame_total = seq_count * per_device
    half_width = kernel.shape[0] // 2
    bounds_row = offsets[0]
    start_row = bounds_row[device]
    owned_load = bounds_row[device + 1] - start_row
    base_row = (device - 1) * per_device
    utt_bounds = jnp.cumsum(lengths[0])[:-1]
    slot_index = jnp.arange(capacity, dtype=jnp.int32)
    owned = (slot_index < owned_load)[:, None]
    bf_zero = jnp.zeros((), jnp.bfloat16)
    cot_rows = jnp.where(owned, cotangent[0], bf_zero)

    def backward_product(d_mixed):
        return lax.dot_general(
            d_mixed,
            lax.all_gather(w_in, "fsdp", axis=0, tiled=True),
            (((1,), (1,)), ((), ())),
            preferred_element_type=jnp.float32,
        )

    from_prev = passed_along(rows_in, "seq", 1)
    from_next = passed_along(rows_in, "seq", -1)
    gathered = jnp.concatenate([from_prev, rows_in, from_next, jnp.zeros_like(rows_in)], axis=0)
    window_rows = capacity + 2 * half_width
    rows_window = lax.dynamic_slice_in_dim(
        gathered, start_row - half_width - base_row, window_rows, 0
    )
    positions = start_row - half_width + jnp.arange(window_rows, dtype=jnp.int32)
    labels = jnp.sum((positions[:, None] >= utt_bounds[None, :]).astype(jnp.int32), axis=1)
    inside = (positions >= 0) & (positions < frame_total)
    labels = jnp.where(inside, labels, -1)
    normed, scale_inv = normalize_rows(rows_window)
    hidden = normed.astype(jnp.bfloat16)
    projected = jnp.dot(
        hidden, lax.all_gather(w_in, "fsdp", axis=0, tiled=True), preferred_element_type=jnp.float32
    )
    values = projected[:, :model_width]
    gates = jax.nn.sigmoid(projected[:, model_width:])
    glu_out = (values * gates).astype(jnp.bfloat16)
    conv = depthwise(glu_out, kernel, labels, capacity)
    conv_normed, conv_inv = normalize_rows(conv)
    gate_out = jax.nn.sigmoid(conv_normed)
    output = conv_normed * gate_out
    owner_output = jnp.where(owned, output.astype(jnp.bfloat16), bf_zero)
    upstream = cot_rows.astype(jnp.float32)
    d_normed = upstream * (gate_out + output * (1.0 - gate_out))
    d_conv = jnp.where(owned, norm_backward(d_normed, conv_normed, conv_inv), 0.0)
    tail_rows = lax.dynamic_slice_in_dim(d_conv, owned_load - half_width, half_width, 0)
    head_rows = d_conv[:half_width]
    left_part = passed_along(tail_rows.astype(jnp.bfloat16), "seq", 1).astype(tail_rows.dtype)
    right_part = passed_along(head_rows.astype(jnp.bfloat16), "seq", -1).astype(head_rows.dtype)
    edge_zeros = jnp.zeros((half_width, model_width), jnp.float32)
    d_window = jnp.concatenate([left_part, d_conv, edge_zeros], axis=0)
    right_placed = lax.dynamic_update_slice_in_dim(
        jnp.zeros((window_rows, model_width), jnp.float32), right_part, half_width + owned_load, 0
    )
    d_window = d_window + right_placed
    d_glu = jnp.where(owned, depthwise_back(d_window, kernel, labels, capacity), 0.0)
    inner_end = half_width + capacity
    d_rows, partial_sum = finish(
        d_glu,
        values[half_width:inner_end],
        gates[half_width:inner_end],
        hidden[half_width:inner_end],
        normed[half_width:inner_end],
        scale_inv[half_width:inner_end],
        backward_product,
    )
    placed = lax.dynamic_update_slice_in_dim(
        jnp.zeros((4 * per_device, model_width), jnp.bfloat16), d_rows, start_row - base_row, 0
    )
    back_prev = passed_along(placed[:per_device], "seq", -1)
    back_next = passed_along(placed[2 * per_device : 3 * per_device], "seq", 1)
    frame_grad = (
        placed[per_device : 2 * per_device].astype(jnp.float32)
        + back_prev.astype(jnp.float32)
        + back_next.astype(jnp.float32)
    ).astype(jnp.bfloat16)
    rounded = lax.optimization_barrier(partial_sum.astype(jnp.bfloat16)).astype(jnp.float32)
    seq_summed = lax.psum_scatter(
        rounded.astype(jnp.bfloat16), "seq", scatter_dimension=0, tiled=True
    )
    summed = lax.psum_scatter(seq_summed, "fsdp", scatter_dimension=0, tiled=True).astype(
        jnp.float32
    )
    w_grad = summed * (1.0 / math.sqrt(group_count * frame_total))
    return (owner_output[None], frame_grad[None], w_grad)


def solution(mesh):
    return jax.shard_map(
        on_device,
        mesh=mesh,
        in_specs=(
            P("fsdp", "seq", None),
            P("fsdp", None),
            P("fsdp", None),
            P("fsdp", None),
            P(),
            P("fsdp", "seq", None),
        ),
        out_specs=(P("fsdp", "seq", None), P("fsdp", "seq", None), P(("seq", "fsdp"), None)),
        check_vma=False,
    )
```

profile of v0, /device:TPU:1, one launch (start us, length us, event | category | flops | bytes accessed | tf_op | source)
XLA Modules:
  0.0 390.6 jit_solution(15712493318630391508)
XLA Ops:
  8.0 4.4 %collective-permute-start = (bf16[128,1536]{1,0:T(8,128)(2,1)}, bf16[128,1536]{1,0:T(8,128)(2,1)S(1)}, u32[]{:S(2)}, u32[]{:S(2)}) collective-permute-start(bf16[128,1536]{1,0:T(8,128)(2,1)} %bitcast.21), channel_id=1, source_target_pairs={{0,8},{8,16},{16,24},{24,32},{32,40},{40,48},{48,56},{56,64},{64,7... | collective-permute-start | bytes 1179656 | tf_op jit(solution)/shard_map/ppermute | solution.py:14
  18.1 1.6 slice_reduce_fusion.29
  21.3 1.8 slice_reduce_fusion.30
  25.8 1.5 fusion.1
  27.4 43.4 %all-gather.2.cloned.1.call-done = bf16[1536,3072]{1,0:T(8,128)(2,1)} async-done(((bf16[192,3072]{1,0:T(8,128)(2,1)}), bf16[1536,3072]{1,0:T(8,128)(2,1)}) %all-gather.2.cloned.1.call-update) | async-done | bytes 9437200 | tf_op jit(solution)/shard_map/all_gather | solution.py:115
  70.8 5.4 %fusion.90 = f32[286,3072]{1,0:T(8,128)S(1)} fusion(bf16[286,1536]{1,0:T(8,128)(2,1)S(1)} %get-tuple-element.52, bf16[1536,3072]{1,0:T(8,128)(2,1)} %all-gather.2.cloned.1.call-done), kind=kOutput, calls=%fused_computation.223 | convolution fusion | flops 2699034624 | bytes 13830144 | tf_op jit(solution)/shard_map/dot_general | solution.py:114
  76.3 2.1 fusion.6
  79.0 13.3 %fusion.86 = (f32[256]{0:T(256)S(1)}, f32[256,1536]{1,0:T(8,128)S(1)}) fusion(f32[256]{0:T(256)S(1)} %get-tuple-element.82, bf16[286,1536]{1,0:T(8,128)(2,1)S(1)} %get-tuple-element.46, f32[1536]{0:T(1024)S(1)} %get-tuple-element.36, f32[256]{0:T(256)S(1)} %get-tuple-element.54, f32[1536]{0:T(1024)S(1)} %get-tuple-element.37, f32[256]{0:T(256)S(1)} %get-tuple-element.55, ...), kind=kLoop, calls=%fused_computation.220 | loop fusion | flops 48365312 | bytes 26174464 | tf_op jit(solution)/shard_map/reduce_sum | solution.py:19
  93.4 1.7 fusion.84
  97.4 3.2 collective-permute-start.2
  101.3 1.5 collective-permute-start.3
  102.8 1.6 maximum_maximum_fusion
  104.4 1.7 collective-permute-done.3
  106.9 10.6 %multiply_convert_fusion.1 = (bf16[256,1536]{1,0:T(8,128)(2,1)S(1)}, f32[256,1536]{1,0:T(8,128)S(1)}) fusion(f32[286,1536]{1,0:T(8,128)} %get-tuple-element.45, f32[256]{0:T(256)} %copy-done.37, f32[286,1536]{1,0:T(8,128)S(1)} %add.319, f32[1536]{0:T(1024)} %copy-done.26, f32[256]{0:T(256)} %copy-done.46, f32[1536]{0:T(1024)} %copy-done.27, ...), kind=kLoop, calls=%fused_computation.115 | loop fusion | flops 36962304 | bytes 52912384 | tf_op jit(solution)/shard_map/convert
  117.5 2.3 fusion.10
  120.7 5.2 %convolution_convert_fusion = bf16[1536,3072]{1,0:T(8,128)(2,1)} fusion(bf16[256,1536]{1,0:T(8,128)(2,1)S(1)} %fusion.10, bf16[256,1536]{1,0:T(8,128)(2,1)S(1)} %get-tuple-element.38, bf16[286,1536]{1,0:T(8,128)(2,1)S(1)} %copy-done.6), kind=kOutput, calls=%fused_computation | convolution fusion | flops 2423783424 | bytes 11796480 | tf_op jit(solution)/shard_map/dot_general | solution.py:67
  128.1 2.1 select_bitcast_fusion
  130.2 5.9 %fusion.83 = (f32[256]{0:T(256)S(1)}, f32[256]{0:T(256)S(1)}, f32[256,1536]{1,0:T(8,128)S(1)}) fusion(f32[286,1536]{1,0:T(8,128)S(1)} %copy-done.3, bf16[1536,3072]{1,0:T(8,128)(2,1)} %all-gather.2.cloned.1.call-done, bf16[256,1536]{1,0:T(8,128)(2,1)} %copy-done.8, bf16[256,1536]{1,0:T(8,128)(2,1)} %copy-done.9), kind=kOutput, calls=%fused_computation.218 | convolution fusion | flops 2420243968 | bytes 14157824 | tf_op jit(solution)/shard_map/dot_general | solution.py:94
  138.5 4.0 %dynamic_update_slice.7 = bf16[512,1536]{1,0:T(8,128)(2,1)S(1)} dynamic-update-slice(bf16[512,1536]{1,0:T(8,128)(2,1)S(1)} %broadcast_in_dim.45, bf16[256,1536]{1,0:T(8,128)(2,1)S(1)} %copy-done.4, s32[]{:T(128)S(6)} %select_n.46, s32[]{:T(128)} %constant.22.clone.1) | dynamic-update-slice | bytes 1572868 | tf_op jit(solution)/shard_map/dynamic_update_slice | solution.py:149
  143.9 4.0 %collective-permute-start.5 = (bf16[128,1536]{1,0:T(8,128)(2,1)S(1)}, bf16[128,1536]{1,0:T(8,128)(2,1)S(1)}, u32[]{:S(2)}, u32[]{:S(2)}) collective-permute-start(bf16[128,1536]{1,0:T(8,128)(2,1)S(1)} %get-tuple-element.48), channel_id=1, source_target_pairs={{0,8},{8,16},{16,24},{24,32},{32,40},{40,48},{48,56},{56,64},{64,7... | collective-permute-start | bytes 1179656 | tf_op jit(solution)/shard_map/ppermute | solution.py:14
  147.9 209.2 %reduce-scatter.4.cloned.1.call-done = bf16[48,3072]{1,0:T(8,128)(2,1)} async-done(((bf16[1536,3072]{1,0:T(8,128)(2,1)}), bf16[48,3072]{1,0:T(8,128)(2,1)}) %reduce-scatter.4.cloned.1.call-update) | async-done | bytes 294928 | tf_op jit(solution)/shard_map/reduce_scatter | solution.py:160
  357.1 19.1 %fusion = bf16[8,3072]{1,0:T(8,128)(2,1)S(1)} fusion(bf16[48,3072]{1,0:T(8,128)(2,1)} %reduce-scatter.4.cloned.1.call-done), kind=kCustom, calls=%all-reduce-scatter | all-reduce-scatter fusion | flops 196609 | bytes 345088
  376.2 3.5 collective-permute-start.6
  379.7 1.8 collective-permute-start.7
  (160 shorter events, 21.2 us)
Async XLA Ops:
  7.2 63.6 %all-gather.2.cloned.1.call-start = ((), (), s32[]{:S(2)}) async-start(), calls=%async_computation.1 | async-start | bytes 10616832 | tf_op jit(solution)/shard_map/all_gather | solution.py:115
  7.9 349.2 %reduce-scatter.4.cloned.1.call-start = ((), (), s32[]{:S(2)}) async-start(), calls=%async_computation.2 | async-start | bytes 9732096 | tf_op jit(solution)/shard_map/reduce_scatter | solution.py:160
  8.0 16.0 %collective-permute-start = (bf16[128,1536]{1,0:T(8,128)(2,1)}, bf16[128,1536]{1,0:T(8,128)(2,1)S(1)}, u32[]{:S(2)}, u32[]{:S(2)}) collective-permute-start(bf16[128,1536]{1,0:T(8,128)(2,1)} %bitcast.21), channel_id=1, source_target_pairs={{0,8},{8,16},{16,24},{24,32},{32,40},{40,48},{48,56},{56,64},{64,7... | collective-permute-start | bytes 1179656 | tf_op jit(solution)/shard_map/ppermute | solution.py:14
  12.4 12.1 %collective-permute-start.1 = (bf16[128,1536]{1,0:T(8,128)(2,1)}, bf16[128,1536]{1,0:T(8,128)(2,1)S(1)}, u32[]{:S(2)}, u32[]{:S(2)}) collective-permute-start(bf16[128,1536]{1,0:T(8,128)(2,1)} %bitcast.22), channel_id=1, source_target_pairs={{8,0},{16,8},{24,16},{32,24},{40,32},{48,40},{56,48},{64,56},{72,6... | collective-permute-start | bytes 1179656 | tf_op jit(solution)/shard_map/ppermute | solution.py:14
  19.8 58.9 %copy-start.16 = (f32[1536]{0:T(1024)}, f32[1536]{0:T(1024)S(1)}, u32[]{:S(2)}) copy-start(f32[1536]{0:T(1024)S(1)} %get-tuple-element.26) | copy-start | bytes 18436
  19.8 58.9 %copy-start.17 = (f32[1536]{0:T(1024)}, f32[1536]{0:T(1024)S(1)}, u32[]{:S(2)}) copy-start(f32[1536]{0:T(1024)S(1)} %get-tuple-element.27) | copy-start | bytes 18436
  19.8 58.9 %copy-start.18 = (f32[1536]{0:T(1024)}, f32[1536]{0:T(1024)S(1)}, u32[]{:S(2)}) copy-start(f32[1536]{0:T(1024)S(1)} %get-tuple-element.28) | copy-start | bytes 18436
  19.8 58.9 %copy-start.19 = (f32[1536]{0:T(1024)}, f32[1536]{0:T(1024)S(1)}, u32[]{:S(2)}) copy-start(f32[1536]{0:T(1024)S(1)} %get-tuple-element.29) | copy-start | bytes 18436
  19.8 58.9 %copy-start.20 = (f32[1536]{0:T(1024)}, f32[1536]{0:T(1024)S(1)}, u32[]{:S(2)}) copy-start(f32[1536]{0:T(1024)S(1)} %get-tuple-element.30) | copy-start | bytes 18436
  19.8 58.9 %copy-start.21 = (f32[1536]{0:T(1024)}, f32[1536]{0:T(1024)S(1)}, u32[]{:S(2)}) copy-start(f32[1536]{0:T(1024)S(1)} %get-tuple-element.31) | copy-start | bytes 18436
  19.8 58.9 %copy-start.22 = (f32[1536]{0:T(1024)}, f32[1536]{0:T(1024)S(1)}, u32[]{:S(2)}) copy-start(f32[1536]{0:T(1024)S(1)} %get-tuple-element.32) | copy-start | bytes 18436
  19.8 58.9 %copy-start.23 = (f32[1536]{0:T(1024)}, f32[1536]{0:T(1024)S(1)}, u32[]{:S(2)}) copy-start(f32[1536]{0:T(1024)S(1)} %get-tuple-element.33) | copy-start | bytes 18436
  19.8 58.9 %copy-start.24 = (f32[1536]{0:T(1024)}, f32[1536]{0:T(1024)S(1)}, u32[]{:S(2)}) copy-start(f32[1536]{0:T(1024)S(1)} %get-tuple-element.34) | copy-start | bytes 18436
  19.9 58.9 %copy-start.25 = (f32[1536]{0:T(1024)}, f32[1536]{0:T(1024)S(1)}, u32[]{:S(2)}) copy-start(f32[1536]{0:T(1024)S(1)} %get-tuple-element.35) | copy-start | bytes 18436
  19.9 58.9 %copy-start.26 = (f32[1536]{0:T(1024)}, f32[1536]{0:T(1024)S(1)}, u32[]{:S(2)}) copy-start(f32[1536]{0:T(1024)S(1)} %get-tuple-element.36) | copy-start | bytes 18436
  19.9 58.9 %copy-start.27 = (f32[1536]{0:T(1024)}, f32[1536]{0:T(1024)S(1)}, u32[]{:S(2)}) copy-start(f32[1536]{0:T(1024)S(1)} %get-tuple-element.37) | copy-start | bytes 18436
  20.0 58.8 %copy-start.35 = (f32[256]{0:T(256)}, f32[256]{0:T(256)S(1)}, u32[]{:S(2)}) copy-start(f32[256]{0:T(256)S(1)} %get-tuple-element.81) | copy-start | bytes 3076
  20.0 58.8 %copy-start.36 = (f32[256]{0:T(256)}, f32[256]{0:T(256)S(1)}, u32[]{:S(2)}) copy-start(f32[256]{0:T(256)S(1)} %get-tuple-element.82) | copy-start | bytes 3076
  97.4 5.3 %collective-permute-start.2 = (bf16[15,1536]{1,0:T(8,128)(2,1)S(1)}, bf16[15,1536]{1,0:T(8,128)(2,1)S(1)}, u32[]{:S(2)}, u32[]{:S(2)}) collective-permute-start(bf16[15,1536]{1,0:T(8,128)(2,1)S(1)} %get-tuple-element.50), channel_id=1, source_target_pairs={{0,8},{8,16},{16,24},{24,32},{32,40},{40,48},{48,56},{56,64},{64,7... | collective-permute-start | bytes 138248 | tf_op jit(solution)/shard_map/ppermute | solution.py:14
  101.3 4.8 %collective-permute-start.3 = (bf16[15,1536]{1,0:T(8,128)(2,1)S(1)}, bf16[15,1536]{1,0:T(8,128)(2,1)S(1)}, u32[]{:S(2)}, u32[]{:S(2)}) collective-permute-start(bf16[15,1536]{1,0:T(8,128)(2,1)S(1)} %get-tuple-element.49), channel_id=1, source_target_pairs={{8,0},{16,8},{24,16},{32,24},{40,32},{48,40},{56,48},{64,56},{72,6... | collective-permute-start | bytes 138248 | tf_op jit(solution)/shard_map/ppermute | solution.py:14
  142.6 239.0 %collective-permute-start.4 = (bf16[128,1536]{1,0:T(8,128)(2,1)S(1)}, bf16[128,1536]{1,0:T(8,128)(2,1)S(1)}, u32[]{:S(2)}, u32[]{:S(2)}) collective-permute-start(bf16[128,1536]{1,0:T(8,128)(2,1)S(1)} %get-tuple-element.47), channel_id=1, source_target_pairs={{8,0},{16,8},{24,16},{32,24},{40,32},{48,40},{56,48},{64,56},{72,6... | collective-permute-start | bytes 1179656 | tf_op jit(solution)/shard_map/ppermute | solution.py:14
  143.9 237.7 %collective-permute-start.5 = (bf16[128,1536]{1,0:T(8,128)(2,1)S(1)}, bf16[128,1536]{1,0:T(8,128)(2,1)S(1)}, u32[]{:S(2)}, u32[]{:S(2)}) collective-permute-start(bf16[128,1536]{1,0:T(8,128)(2,1)S(1)} %get-tuple-element.48), channel_id=1, source_target_pairs={{0,8},{8,16},{16,24},{24,32},{32,40},{40,48},{48,56},{56,64},{64,7... | collective-permute-start | bytes 1179656 | tf_op jit(solution)/shard_map/ppermute | solution.py:14
  376.2 6.5 %collective-permute-start.6 = (bf16[8,3072]{1,0:T(8,128)(2,1)S(1)}, bf16[8,3072]{1,0:T(8,128)(2,1)S(1)}, u32[]{:S(2)}, u32[]{:S(2)}) collective-permute-start(bf16[8,3072]{1,0:T(8,128)(2,1)S(1)} %fusion), channel_id=1, source_target_pairs={{0,1},{1,2},{2,3},{3,4},{4,5},{5,6},{6,7},{8,9},{9,10},{10,11},{11... | collective-permute-start | bytes 147464
  379.7 3.0 collective-permute-start.7
  (40 other events, 1379.4 us)
Sparse Core Ops, SparseCore 0:
  9.8 60.9 all-gather.1
  126.1 230.9 reduce-scatter.3
where the time goes:
time: 393 us; the launch traced here: 391 us
  waiting for transfers between devices  256 us (65%)
  other arithmetic  43.6 us (11%)
  starting transfers between devices  21 us (5%)
  blocking collectives  19.1 us (5%)
  between operations  18.5 us (5%)
  matrix products  16.5 us (4%)
  local copies, waits for them, and re-layouts  15.9 us (4%)
    reduce_scatter x1, waiting for transfers between devices, on_device(): lax.psum_scatter(rounded.astype(jnp.bfloat16), 'seq', scatter_dimension=0...  209 us
    all_gather x1, waiting for transfers between devices, on_device(): lax.all_gather(w_in, 'fsdp', axis=0, tiled=True)  43.4 us
    unnamed x1, blocking collectives  19.1 us
    ppermute x6, starting transfers between devices, passed_along(): lax.ppermute(value, axis, [(source, source + steps) for source in range(i...  15.6 us
    reduce_sum x2, other arithmetic, normalize_rows(): center = jnp.mean(values, axis=-1, keepdims=True)  14.2 us
    another operation x3, other arithmetic  13.7 us
  transfers between devices with their start and end apart: 10, of which 5 were waited for; matrix products, arithmetic and copies ran while one was open for 12% of the time, Pallas kernels for 0%

commit v1 on v0

--- a/solution.py
+++ b/solution.py
@@ -84,7 +84,9 @@
     start_row = bounds_row[device]
     owned_load = bounds_row[device + 1] - start_row
     base_row = (device - 1) * per_device
-    utt_bounds = jnp.cumsum(lengths[0])[:-1]
+    first_end = lengths[0, 0]
+    second_end = first_end + lengths[0, 1]
+    utt_bounds = jnp.stack([first_end, second_end, second_end + lengths[0, 2]])
     slot_index = jnp.arange(capacity, dtype=jnp.int32)
     owned = (slot_index < owned_load)[:, None]
     bf_zero = jnp.zeros((), jnp.bfloat16)

time: 393 us -> 392 us (level)
  transfers between devices with their start and end apart: 10 -> 10, of which waited for: 5 -> 4; matrix products, arithmetic and copies ran while one was open for 12% -> 12% of each run, Pallas kernels for 0% -> 0%
where the time goes in v1:
time: 392 us; the launch traced here: 391 us
  waiting for transfers between devices  254 us (65%)
  other arithmetic  43.5 us (11%)
  starting transfers between devices  21.1 us (5%)
  between operations  20.5 us (5%)
  blocking collectives  19.2 us (5%)
  matrix products  16.5 us (4%)
  local copies, waits for them, and re-layouts  15.6 us (4%)
    reduce_scatter x1, waiting for transfers between devices, on_device(): lax.psum_scatter(rounded.astype(jnp.bfloat16), 'seq', scatter_dimension=0...  209 us
    all_gather x1, waiting for transfers between devices, on_device(): lax.all_gather(w_in, 'fsdp', axis=0, tiled=True)  42.5 us
    unnamed x1, blocking collectives  19.2 us
    ppermute x6, starting transfers between devices, passed_along(): lax.ppermute(value, axis, [(source, source + steps) for source in range(i...  15.7 us
    reduce_sum x2, other arithmetic, normalize_rows(): center = jnp.mean(values, axis=-1, keepdims=True)  14.2 us
    another operation x2, other arithmetic  12.9 us
  transfers between devices with their start and end apart: 10, of which 4 were waited for; matrix products, arithmetic and copies ran while one was open for 12% of the time, Pallas kernels for 0%

profile of v1, /device:TPU:1, one launch (start us, length us, event | category | flops | bytes accessed | tf_op | source)
XLA Modules:
  0.0 390.5 jit_solution(2730120736717077136)
XLA Ops:
  8.0 4.4 %collective-permute-start = (bf16[128,1536]{1,0:T(8,128)(2,1)}, bf16[128,1536]{1,0:T(8,128)(2,1)S(1)}, u32[]{:S(2)}, u32[]{:S(2)}) collective-permute-start(bf16[128,1536]{1,0:T(8,128)(2,1)} %bitcast.21), channel_id=1, source_target_pairs={{0,8},{8,16},{16,24},{24,32},{32,40},{40,48},{48,56},{56,64},{64,7... | collective-permute-start | bytes 1179656 | tf_op jit(solution)/shard_map/ppermute | solution.py:14
  13.7 1.4 constant_dynamic-slice_fusion.1
  21.3 1.5 slice_reduce_fusion.29
  26.8 1.5 fusion.1
  28.3 42.5 %all-gather.2.cloned.1.call-done = bf16[1536,3072]{1,0:T(8,128)(2,1)} async-done(((bf16[192,3072]{1,0:T(8,128)(2,1)}), bf16[1536,3072]{1,0:T(8,128)(2,1)}) %all-gather.2.cloned.1.call-update) | async-done | bytes 9437200 | tf_op jit(solution)/shard_map/all_gather | solution.py:117
  70.8 5.4 %fusion.91 = f32[286,3072]{1,0:T(8,128)S(1)} fusion(bf16[286,1536]{1,0:T(8,128)(2,1)S(1)} %get-tuple-element.52, bf16[1536,3072]{1,0:T(8,128)(2,1)} %all-gather.2.cloned.1.call-done), kind=kOutput, calls=%fused_computation.224 | convolution fusion | flops 2699034624 | bytes 13830144 | tf_op jit(solution)/shard_map/dot_general | solution.py:116
  76.3 2.1 fusion.6
  79.0 13.3 %fusion.86 = (f32[256]{0:T(256)S(1)}, f32[256,1536]{1,0:T(8,128)S(1)}) fusion(f32[256]{0:T(256)S(1)} %get-tuple-element.82, bf16[286,1536]{1,0:T(8,128)(2,1)S(1)} %get-tuple-element.46, f32[1536]{0:T(1024)S(1)} %get-tuple-element.36, f32[256]{0:T(256)S(1)} %get-tuple-element.54, f32[1536]{0:T(1024)S(1)} %get-tuple-element.37, f32[256]{0:T(256)S(1)} %get-tuple-element.55, ...), kind=kLoop, calls=%fused_computation.220 | loop fusion | flops 48365312 | bytes 26174464 | tf_op jit(solution)/shard_map/reduce_sum | solution.py:19
  93.5 1.7 fusion.84
  97.4 3.2 collective-permute-start.2
  101.3 1.5 collective-permute-start.3
  102.8 1.6 maximum_maximum_fusion
  104.5 1.7 collective-permute-done.3
  107.0 10.6 %multiply_convert_fusion.1 = (bf16[256,1536]{1,0:T(8,128)(2,1)S(1)}, f32[256,1536]{1,0:T(8,128)S(1)}) fusion(f32[286,1536]{1,0:T(8,128)} %get-tuple-element.45, f32[256]{0:T(256)} %copy-done.38, f32[286,1536]{1,0:T(8,128)S(1)} %add.329, f32[1536]{0:T(1024)} %copy-done.27, f32[256]{0:T(256)} %copy-done.47, f32[1536]{0:T(1024)} %copy-done.28, ...), kind=kLoop, calls=%fused_computation.115 | loop fusion | flops 36962304 | bytes 52912384 | tf_op jit(solution)/shard_map/convert
  117.6 2.3 fusion.10
  120.8 5.2 %convolution_convert_fusion = bf16[1536,3072]{1,0:T(8,128)(2,1)} fusion(bf16[256,1536]{1,0:T(8,128)(2,1)S(1)} %fusion.10, bf16[256,1536]{1,0:T(8,128)(2,1)S(1)} %get-tuple-element.38, bf16[286,1536]{1,0:T(8,128)(2,1)S(1)} %copy-done.6), kind=kOutput, calls=%fused_computation | convolution fusion | flops 2423783424 | bytes 11796480 | tf_op jit(solution)/shard_map/dot_general | solution.py:67
  128.2 2.1 select_bitcast_fusion
  130.2 5.9 %fusion.83 = (f32[256]{0:T(256)S(1)}, f32[256]{0:T(256)S(1)}, f32[256,1536]{1,0:T(8,128)S(1)}) fusion(f32[286,1536]{1,0:T(8,128)S(1)} %copy-done.3, bf16[1536,3072]{1,0:T(8,128)(2,1)} %all-gather.2.cloned.1.call-done, bf16[256,1536]{1,0:T(8,128)(2,1)} %copy-done.8, bf16[256,1536]{1,0:T(8,128)(2,1)} %copy-done.9), kind=kOutput, calls=%fused_computation.218 | convolution fusion | flops 2420243968 | bytes 14157824 | tf_op jit(solution)/shard_map/dot_general | solution.py:96
  138.6 4.0 %dynamic_update_slice.7 = bf16[512,1536]{1,0:T(8,128)(2,1)S(1)} dynamic-update-slice(bf16[512,1536]{1,0:T(8,128)(2,1)S(1)} %broadcast_in_dim.45, bf16[256,1536]{1,0:T(8,128)(2,1)S(1)} %copy-done.4, s32[]{:T(128)S(6)} %select_n.46, s32[]{:T(128)} %constant.20.clone.1) | dynamic-update-slice | bytes 1572868 | tf_op jit(solution)/shard_map/dynamic_update_slice | solution.py:151
  143.9 4.0 %collective-permute-start.5 = (bf16[128,1536]{1,0:T(8,128)(2,1)S(1)}, bf16[128,1536]{1,0:T(8,128)(2,1)S(1)}, u32[]{:S(2)}, u32[]{:S(2)}) collective-permute-start(bf16[128,1536]{1,0:T(8,128)(2,1)S(1)} %get-tuple-element.48), channel_id=1, source_target_pairs={{0,8},{8,16},{16,24},{24,32},{32,40},{40,48},{48,56},{56,64},{64,7... | collective-permute-start | bytes 1179656 | tf_op jit(solution)/shard_map/ppermute | solution.py:14
  148.0 208.9 %reduce-scatter.4.cloned.1.call-done = bf16[48,3072]{1,0:T(8,128)(2,1)} async-done(((bf16[1536,3072]{1,0:T(8,128)(2,1)}), bf16[48,3072]{1,0:T(8,128)(2,1)}) %reduce-scatter.4.cloned.1.call-update) | async-done | bytes 294928 | tf_op jit(solution)/shard_map/reduce_scatter | solution.py:162
  356.9 19.2 %fusion = bf16[8,3072]{1,0:T(8,128)(2,1)S(1)} fusion(bf16[48,3072]{1,0:T(8,128)(2,1)} %reduce-scatter.4.cloned.1.call-done), kind=kCustom, calls=%all-reduce-scatter | all-reduce-scatter fusion | flops 196609 | bytes 345088
  376.1 3.5 collective-permute-start.6
  379.7 1.8 collective-permute-start.7
  (162 shorter events, 20.8 us)
Async XLA Ops:
  7.2 63.6 %all-gather.2.cloned.1.call-start = ((), (), s32[]{:S(2)}) async-start(), calls=%async_computation.1 | async-start | bytes 10616832 | tf_op jit(solution)/shard_map/all_gather | solution.py:117
  7.9 348.9 %reduce-scatter.4.cloned.1.call-start = ((), (), s32[]{:S(2)}) async-start(), calls=%async_computation.2 | async-start | bytes 9732096 | tf_op jit(solution)/shard_map/reduce_scatter | solution.py:162
  8.0 17.4 %collective-permute-start = (bf16[128,1536]{1,0:T(8,128)(2,1)}, bf16[128,1536]{1,0:T(8,128)(2,1)S(1)}, u32[]{:S(2)}, u32[]{:S(2)}) collective-permute-start(bf16[128,1536]{1,0:T(8,128)(2,1)} %bitcast.21), channel_id=1, source_target_pairs={{0,8},{8,16},{16,24},{24,32},{32,40},{40,48},{48,56},{56,64},{64,7... | collective-permute-start | bytes 1179656 | tf_op jit(solution)/shard_map/ppermute | solution.py:14
  12.4 13.0 %collective-permute-start.1 = (bf16[128,1536]{1,0:T(8,128)(2,1)}, bf16[128,1536]{1,0:T(8,128)(2,1)S(1)}, u32[]{:S(2)}, u32[]{:S(2)}) collective-permute-start(bf16[128,1536]{1,0:T(8,128)(2,1)} %bitcast.22), channel_id=1, source_target_pairs={{8,0},{16,8},{24,16},{32,24},{40,32},{48,40},{56,48},{64,56},{72,6... | collective-permute-start | bytes 1179656 | tf_op jit(solution)/shard_map/ppermute | solution.py:14
  22.8 55.9 %copy-start.17 = (f32[1536]{0:T(1024)}, f32[1536]{0:T(1024)S(1)}, u32[]{:S(2)}) copy-start(f32[1536]{0:T(1024)S(1)} %get-tuple-element.26) | copy-start | bytes 18436
  22.8 55.9 %copy-start.18 = (f32[1536]{0:T(1024)}, f32[1536]{0:T(1024)S(1)}, u32[]{:S(2)}) copy-start(f32[1536]{0:T(1024)S(1)} %get-tuple-element.27) | copy-start | bytes 18436
  22.8 55.9 %copy-start.19 = (f32[1536]{0:T(1024)}, f32[1536]{0:T(1024)S(1)}, u32[]{:S(2)}) copy-start(f32[1536]{0:T(1024)S(1)} %get-tuple-element.28) | copy-start | bytes 18436
  22.8 55.9 %copy-start.20 = (f32[1536]{0:T(1024)}, f32[1536]{0:T(1024)S(1)}, u32[]{:S(2)}) copy-start(f32[1536]{0:T(1024)S(1)} %get-tuple-element.29) | copy-start | bytes 18436
  22.8 55.9 %copy-start.21 = (f32[1536]{0:T(1024)}, f32[1536]{0:T(1024)S(1)}, u32[]{:S(2)}) copy-start(f32[1536]{0:T(1024)S(1)} %get-tuple-element.30) | copy-start | bytes 18436
  22.8 55.9 %copy-start.22 = (f32[1536]{0:T(1024)}, f32[1536]{0:T(1024)S(1)}, u32[]{:S(2)}) copy-start(f32[1536]{0:T(1024)S(1)} %get-tuple-element.31) | copy-start | bytes 18436
  22.8 55.9 %copy-start.23 = (f32[1536]{0:T(1024)}, f32[1536]{0:T(1024)S(1)}, u32[]{:S(2)}) copy-start(f32[1536]{0:T(1024)S(1)} %get-tuple-element.32) | copy-start | bytes 18436
  22.8 55.9 %copy-start.24 = (f32[1536]{0:T(1024)}, f32[1536]{0:T(1024)S(1)}, u32[]{:S(2)}) copy-start(f32[1536]{0:T(1024)S(1)} %get-tuple-element.33) | copy-start | bytes 18436
  22.9 55.9 %copy-start.25 = (f32[1536]{0:T(1024)}, f32[1536]{0:T(1024)S(1)}, u32[]{:S(2)}) copy-start(f32[1536]{0:T(1024)S(1)} %get-tuple-element.34) | copy-start | bytes 18436
  22.9 55.9 %copy-start.26 = (f32[1536]{0:T(1024)}, f32[1536]{0:T(1024)S(1)}, u32[]{:S(2)}) copy-start(f32[1536]{0:T(1024)S(1)} %get-tuple-element.35) | copy-start | bytes 18436
  22.9 55.9 %copy-start.27 = (f32[1536]{0:T(1024)}, f32[1536]{0:T(1024)S(1)}, u32[]{:S(2)}) copy-start(f32[1536]{0:T(1024)S(1)} %get-tuple-element.36) | copy-start | bytes 18436
  22.9 55.9 %copy-start.28 = (f32[1536]{0:T(1024)}, f32[1536]{0:T(1024)S(1)}, u32[]{:S(2)}) copy-start(f32[1536]{0:T(1024)S(1)} %get-tuple-element.37) | copy-start | bytes 18436
  23.0 55.8 %copy-start.36 = (f32[256]{0:T(256)}, f32[256]{0:T(256)S(1)}, u32[]{:S(2)}) copy-start(f32[256]{0:T(256)S(1)} %get-tuple-element.81) | copy-start | bytes 3076
  23.0 55.8 %copy-start.37 = (f32[256]{0:T(256)}, f32[256]{0:T(256)S(1)}, u32[]{:S(2)}) copy-start(f32[256]{0:T(256)S(1)} %get-tuple-element.82) | copy-start | bytes 3076
  97.4 5.4 %collective-permute-start.2 = (bf16[15,1536]{1,0:T(8,128)(2,1)S(1)}, bf16[15,1536]{1,0:T(8,128)(2,1)S(1)}, u32[]{:S(2)}, u32[]{:S(2)}) collective-permute-start(bf16[15,1536]{1,0:T(8,128)(2,1)S(1)} %get-tuple-element.50), channel_id=1, source_target_pairs={{0,8},{8,16},{16,24},{24,32},{32,40},{40,48},{48,56},{56,64},{64,7... | collective-permute-start | bytes 138248 | tf_op jit(solution)/shard_map/ppermute | solution.py:14
  101.3 4.8 %collective-permute-start.3 = (bf16[15,1536]{1,0:T(8,128)(2,1)S(1)}, bf16[15,1536]{1,0:T(8,128)(2,1)S(1)}, u32[]{:S(2)}, u32[]{:S(2)}) collective-permute-start(bf16[15,1536]{1,0:T(8,128)(2,1)S(1)} %get-tuple-element.49), channel_id=1, source_target_pairs={{8,0},{16,8},{24,16},{32,24},{40,32},{48,40},{56,48},{64,56},{72,6... | collective-permute-start | bytes 138248 | tf_op jit(solution)/shard_map/ppermute | solution.py:14
  142.7 238.8 %collective-permute-start.4 = (bf16[128,1536]{1,0:T(8,128)(2,1)S(1)}, bf16[128,1536]{1,0:T(8,128)(2,1)S(1)}, u32[]{:S(2)}, u32[]{:S(2)}) collective-permute-start(bf16[128,1536]{1,0:T(8,128)(2,1)S(1)} %get-tuple-element.47), channel_id=1, source_target_pairs={{8,0},{16,8},{24,16},{32,24},{40,32},{48,40},{56,48},{64,56},{72,6... | collective-permute-start | bytes 1179656 | tf_op jit(solution)/shard_map/ppermute | solution.py:14
  143.9 237.6 %collective-permute-start.5 = (bf16[128,1536]{1,0:T(8,128)(2,1)S(1)}, bf16[128,1536]{1,0:T(8,128)(2,1)S(1)}, u32[]{:S(2)}, u32[]{:S(2)}) collective-permute-start(bf16[128,1536]{1,0:T(8,128)(2,1)S(1)} %get-tuple-element.48), channel_id=1, source_target_pairs={{0,8},{8,16},{16,24},{24,32},{32,40},{40,48},{48,56},{56,64},{64,7... | collective-permute-start | bytes 1179656 | tf_op jit(solution)/shard_map/ppermute | solution.py:14
  376.1 6.5 %collective-permute-start.6 = (bf16[8,3072]{1,0:T(8,128)(2,1)S(1)}, bf16[8,3072]{1,0:T(8,128)(2,1)S(1)}, u32[]{:S(2)}, u32[]{:S(2)}) collective-permute-start(bf16[8,3072]{1,0:T(8,128)(2,1)S(1)} %fusion), channel_id=1, source_target_pairs={{0,1},{1,2},{2,3},{3,4},{4,5},{5,6},{6,7},{8,9},{9,10},{10,11},{11... | collective-permute-start | bytes 147464
  379.7 3.0 collective-permute-start.7
  (41 other events, 1338.2 us)
Sparse Core Ops, SparseCore 0:
  9.9 60.9 all-gather.1
  126.1 230.6 reduce-scatter.3

commit v2 on v0

v2 whole, which is shorter than its diff:
```python
import functools
import math

import jax
import jax.numpy as jnp
from jax import lax
from jax.experimental import pallas as pl
from jax.experimental.pallas import tpu as pltpu
from jax.sharding import PartitionSpec as P

epsilon = 1e-05
bf16 = jnp.bfloat16
f32 = jnp.float32
LANES = 128
BLOCK = 32
SEQ = ("x", "z")
CHIP = 2
NEAR = 3


def passed_along(value, axis, steps):
    count = lax.axis_size(axis)
    initial, last = (max(0, -steps), min(count, count - steps))
    return lax.ppermute(value, axis, [(source, source + steps) for source in range(initial, last)])


def normalize_rows(values):
    values = values.astype(f32)
    center = jnp.mean(values, axis=-1, keepdims=True)
    shifted = values - center
    scale_inv = lax.rsqrt(jnp.mean(shifted * shifted, axis=-1, keepdims=True) + epsilon)
    return (shifted * scale_inv, scale_inv)


def shifted_copies(source, copies, rows):
    copies[0, :rows] = source
    for shift in range(1, 8):
        copies[shift, :rows] = pltpu.roll(source, rows - shift, 0)


def tap_sum(copies, mask_ref, ker_ref, lanes, row, mask_row, count, flip, masked):
    tap_count = ker_ref.shape[0]
    total = jnp.zeros((count, LANES), f32)
    for tap in range(tap_count):
        tile, shift = divmod(tap + 1, 8)
        weight = ker_ref[pl.ds(tap_count - 1 - tap if flip else tap, 1), lanes]
        term = weight * copies[shift, pl.ds(row + 8 * tile, count), :]
        if masked:
            term = term * mask_ref[tap, pl.ds(mask_row, count), :]
        total = total + term
    return total


def centred(values):
    inverse = 1.0 / values.shape[-1]
    center = jnp.sum(values, axis=-1, keepdims=True) * inverse
    shifted = values - center
    variance = jnp.sum(shifted * shifted, axis=-1, keepdims=True) * inverse
    scale_inv = lax.rsqrt(variance + epsilon)
    return shifted * scale_inv, scale_inv


def started(copies):
    for copy in copies:
        copy.start()
    return copies


def pair_copies(core_ref, pieces, target, sem, first):
    copies = []
    half = len(pieces) // 2
    rows = target.shape[0] // CHIP
    for index, piece in enumerate(pieces):
        count = piece.shape[0]
        core = core_ref[0] if index < half else 1 - core_ref[0]
        start = pl.multiple_of(core * rows + (index % half) * count, 16)
        copies.append(
            pltpu.make_async_copy(piece, target.at[pl.ds(start, count), :], sem.at[first + index])
        )
    return copies


def chip_copies(core_ref, pieces, w_buf, sem):
    copies = []
    first = 0
    for chip in range(w_buf.shape[0]):
        count = 2 if chip < NEAR else 4
        copies.append(pair_copies(core_ref, pieces[first : first + count], w_buf.at[chip], sem, first))
        first += count
    return copies


def part_kernel(halo, at_ref, core_ref, prev_ref, rows_ref, next_ref, *rest):
    piece_count = len(rest) - 4
    pieces = rest[:piece_count]
    hid_ref, part_ref, w_buf, sem = rest[piece_count:]
    chips = w_buf.shape[0]
    depth = w_buf.shape[1]
    copies = chip_copies(core_ref, pieces, w_buf, sem)
    for chip in range(chips):
        started(copies[chip])

    def normalize(source, first, count, target):
        @pl.loop(0, count // 16)
        def _(block):
            taken = pl.ds(pl.multiple_of(first + block * 16, 16), 16)
            put = pl.ds(pl.multiple_of(target + block * 16, 16), 16)
            hid_ref[put, :] = centred(source[taken, :].astype(f32))[0].astype(bf16)

    rows = rows_ref.shape[0]
    normalize(prev_ref, 0, halo, 0)
    normalize(rows_ref, 0, rows, halo)
    normalize(next_ref, next_ref.shape[0] - halo, halo, halo + rows)

    for chip in range(chips):
        for copy in copies[chip]:
            copy.wait()

    @pl.loop(0, part_ref.shape[1] // 256)
    def _(block):
        at = pl.ds(pl.multiple_of(block * 256, 256), 256)
        total = jnp.zeros((hid_ref.shape[0], 256), f32)
        for chip in range(chips):
            lanes = pl.ds(pl.multiple_of(at_ref[chip] * depth, LANES), depth)
            total = total + jnp.dot(
                hid_ref[:, lanes], w_buf[chip, :, at], preferred_element_type=f32
            )
        part_ref[:, at] = total


def main_kernel(rows, edge, bounds_ref, at_ref, core_ref, hid_ref, part_ref, up_ref, ker_ref, *rest):
    piece_count = len(rest) - 11
    pieces = rest[:piece_count]
    out_ref, dm_ref, shares_ref, w_buf, val, gate, glu, conv, copies_buf, mask_ref, sem = rest[piece_count:]
    width = hid_ref.shape[1]
    window = rows + 4 * edge
    wide = rows + 2 * edge
    tap_count = ker_ref.shape[0]
    half_width = tap_count // 2
    copies = started(pair_copies(core_ref, pieces, w_buf, sem, 0))
    depth = w_buf.shape[0]
    far = pl.ds(pl.multiple_of(at_ref[at_ref.shape[0] - 1] * depth, LANES), depth)
    base = bounds_ref[0]
    last = bounds_ref[1]
    ends = [bounds_ref[index] for index in range(2, bounds_ref.shape[0])]

    def crossed(first, count):
        found = jnp.bool_(False)
        for end in ends:
            found = found | ((end > first - half_width) & (end < first + count + half_width))
        return found

    @pl.when(crossed(base, wide))
    def _():
        @pl.loop(0, wide // 8)
        def _(block):
            row = pl.multiple_of(block * 8, 8)
            position = base + row + lax.broadcasted_iota(jnp.int32, (8, LANES), 0)
            low = jnp.zeros((8, LANES), jnp.int32)
            high = jnp.full((8, LANES), last, jnp.int32)
            for end in ends:
                low = jnp.where(position >= end, jnp.maximum(low, end), low)
                high = jnp.where(position < end, jnp.minimum(high, end), high)
            low = low - position + half_width
            high = high - position + half_width
            for tap in range(tap_count):
                mask_ref[tap, pl.ds(row, 8), :] = jnp.where((low <= tap) & (high > tap), 1.0, 0.0).astype(f32)

    for copy in copies:
        copy.wait()

    @pl.loop(0, width // 256)
    def _(block):
        at = pl.ds(pl.multiple_of(block * 256, 256), 256)
        gate_at = pl.ds(pl.multiple_of(block * 256 + width, 256), 256)
        values = part_ref[:, at] + jnp.dot(hid_ref[:, far], w_buf[:, at], preferred_element_type=f32)
        gates = jax.nn.sigmoid(
            part_ref[:, gate_at]
            + jnp.dot(hid_ref[:, far], w_buf[:, gate_at], preferred_element_type=f32)
        )
        val[:, at] = values[2 * edge : 2 * edge + rows]
        gate[:, at] = gates[2 * edge : 2 * edge + rows]
        glu[:, at] = (values * gates).astype(bf16).astype(f32)

    @pl.loop(0, width // LANES)
    def _(block):
        lanes = pl.ds(pl.multiple_of(block * LANES, LANES), LANES)
        shifted_copies(glu[:, lanes], copies_buf, window)

        @pl.loop(0, wide // BLOCK)
        def _(step):
            row = pl.multiple_of(step * BLOCK, BLOCK)
            cut = crossed(base + row, BLOCK)

            @pl.when(jnp.logical_not(cut))
            def _():
                conv[pl.ds(row, BLOCK), lanes] = tap_sum(
                    copies_buf, mask_ref, ker_ref, lanes, row, row, BLOCK, False, False
                )

            @pl.when(cut)
            def _():
                conv[pl.ds(row, BLOCK), lanes] = tap_sum(
                    copies_buf, mask_ref, ker_ref, lanes, row, row, BLOCK, False, True
                )

    @pl.loop(0, wide // 16)
    def _(block):
        at = pl.ds(pl.multiple_of(block * 16, 16), 16)
        normed, scale_inv = centred(conv[at, :])
        gates = jax.nn.sigmoid(normed)
        output = normed * gates

        @pl.when((block >= edge // 16) & (block < (edge + rows) // 16))
        def _():
            out_ref[pl.ds(pl.multiple_of(block * 16 - edge, 16), 16), :] = output.astype(bf16)

        d_normed = up_ref[at, :].astype(f32) * (gates + output * (1.0 - gates))
        conv[at, :] = back_through_norm(d_normed, normed, scale_inv)

    @pl.loop(0, width // LANES)
    def _(block):
        lanes = pl.ds(pl.multiple_of(block * LANES, LANES), LANES)
        gate_lanes = pl.ds(pl.multiple_of(block * LANES + width, LANES), LANES)
        shifted_copies(conv[:, lanes], copies_buf, wide)
        per_share = shares_ref.shape[2] // LANES
        share = lax.div(block, per_share)
        share_lanes = pl.ds(pl.multiple_of((block - share * per_share) * LANES, LANES), LANES)

        @pl.loop(0, rows // BLOCK)
        def _(step):
            row = pl.multiple_of(step * BLOCK, BLOCK)
            at = pl.ds(row, BLOCK)
            cut = crossed(base + edge + row, BLOCK)

            def finish(masked):
                d_glu = tap_sum(
                    copies_buf, mask_ref, ker_ref, lanes, row, row + edge, BLOCK, True, masked
                )
                gates = gate[at, lanes]
                d_values = d_glu * gates
                d_gates = (d_values * val[at, lanes] * (1.0 - gates)).astype(bf16)
                d_values = d_values.astype(bf16)
                dm_ref[at, lanes] = d_values
                dm_ref[at, gate_lanes] = d_gates
                shares_ref[share, at, share_lanes] = d_values
                shares_ref[share + shares_ref.shape[0] // 2, at, share_lanes] = d_gates

            @pl.when(jnp.logical_not(cut))
            def _():
                finish(False)

            @pl.when(cut)
            def _():
                finish(True)


def back_through_norm(upstream, normed, scale_inv):
    inverse = 1.0 / normed.shape[-1]
    first_mean = jnp.sum(upstream, axis=-1, keepdims=True) * inverse
    second_mean = jnp.sum(upstream * normed, axis=-1, keepdims=True) * inverse
    return scale_inv * (upstream - first_mean - normed * second_mean)


def frame_kernel(at_ref, core_ref, rows_ref, dm_ref, *rest):
    piece_count = len(rest) - 4
    pieces = rest[:piece_count]
    grad_ref, w_buf, d_hidden, sem = rest[piece_count:]
    rows, width = rows_ref.shape
    chips, depth = w_buf.shape[:2]
    copies = chip_copies(core_ref, pieces, w_buf, sem)
    for chip in range(chips):
        started(copies[chip])
    for chip in range(chips):
        for copy in copies[chip]:
            copy.wait()
        lanes = pl.ds(pl.multiple_of(at_ref[chip] * depth, LANES), depth)
        d_hidden[:, lanes] = lax.dot_general(
            dm_ref[...], w_buf[chip], (((1,), (1,)), ((), ())), preferred_element_type=f32
        )

    @pl.loop(0, rows // 16)
    def _(block):
        at = pl.ds(pl.multiple_of(block * 16, 16), 16)
        normed, scale_inv = centred(rows_ref[at, :].astype(f32))
        grad_ref[at, :] = back_through_norm(d_hidden[at, :], normed, scale_inv).astype(bf16)


VMEM = pl.BlockSpec(memory_space=pltpu.VMEM)
SMEM = pl.BlockSpec(memory_space=pltpu.SMEM)
ANY = pl.BlockSpec(memory_space=pltpu.HBM)


def limit(mib):
    return pltpu.CompilerParams(vmem_limit_bytes=mib * 1024 * 1024)


def run_part(chips, core, from_prev, rows_in, from_next, pieces, halo):
    rows, width = rows_in.shape
    big = rows + 2 * halo
    depth = pieces[0].shape[0] * CHIP
    mixed_width = pieces[0].shape[1]
    return pl.pallas_call(
        functools.partial(part_kernel, halo),
        out_shape=(
            jax.ShapeDtypeStruct((big, width), bf16),
            jax.ShapeDtypeStruct((big, mixed_width), f32),
        ),
        in_specs=[SMEM, SMEM, VMEM, VMEM, VMEM] + [ANY] * len(pieces),
        out_specs=(VMEM, VMEM),
        scratch_shapes=[
            pltpu.VMEM((chips.shape[0], depth, mixed_width), bf16),
            pltpu.SemaphoreType.DMA((len(pieces),)),
        ],
        compiler_params=limit(44),
        cost_estimate=pl.CostEstimate(flops=2 * 10**9, bytes_accessed=8 * 10**6, transcendentals=0),
        name="forward_part",
    )(chips, core, from_prev, rows_in, from_next, *pieces)


def run_main(bounds, chips, core, hidden, part, upstream, kernel, pieces, rows, edge, shares):
    big, width = hidden.shape
    wide = upstream.shape[0]
    taps = kernel.shape[0]
    depth = sum(piece.shape[0] for piece in pieces)
    return pl.pallas_call(
        functools.partial(main_kernel, rows, edge),
        out_shape=(
            jax.ShapeDtypeStruct((rows, width), bf16),
            jax.ShapeDtypeStruct((rows, 2 * width), bf16),
            jax.ShapeDtypeStruct((shares, rows, 2 * width // shares), bf16),
        ),
        in_specs=[SMEM, SMEM, SMEM, VMEM, VMEM, VMEM, VMEM] + [ANY] * len(pieces),
        out_specs=(VMEM, VMEM, VMEM),
        scratch_shapes=[
            pltpu.VMEM((depth, 2 * width), bf16),
            pltpu.VMEM((rows, width), f32),
            pltpu.VMEM((rows, width), f32),
            pltpu.VMEM((big, width), f32),
            pltpu.VMEM((wide, width), f32),
            pltpu.VMEM((8, big, LANES), f32),
            pltpu.VMEM((taps, wide, LANES), f32),
            pltpu.SemaphoreType.DMA((len(pieces),)),
        ],
        compiler_params=limit(44),
        cost_estimate=pl.CostEstimate(flops=6 * 10**9, bytes_accessed=12 * 10**6, transcendentals=0),
        name="main",
    )(bounds, chips, core, hidden, part, upstream, kernel, *pieces)


def run_frame(chips, core, rows_in, d_mixed, pieces):
    rows, width = rows_in.shape
    return pl.pallas_call(
        frame_kernel,
        out_shape=jax.ShapeDtypeStruct((rows, width), bf16),
        in_specs=[SMEM, SMEM, VMEM, VMEM] + [ANY] * len(pieces),
        out_specs=VMEM,
        scratch_shapes=[
            pltpu.VMEM((chips.shape[0], width // chips.shape[0], 2 * width), bf16),
            pltpu.VMEM((rows, width), f32),
            pltpu.SemaphoreType.DMA((len(pieces),)),
        ],
        compiler_params=limit(58),
        cost_estimate=pl.CostEstimate(flops=2 * 10**9, bytes_accessed=11 * 10**6, transcendentals=0),
        name="frame_back",
    )(chips, core, rows_in, d_mixed, *pieces)


def ring(value, axis, steps):
    count = lax.axis_size(axis)
    return lax.ppermute(value, axis, [(i, (i + steps) % count) for i in range(count)])


def other_core(value):
    return lax.ppermute(value, "c", [(0, 1), (1, 0)])


def weight_blocks(w_in):
    half = w_in.shape[0] // 2
    below, above = ring(w_in, "y", 1), ring(w_in, "y", -1)
    return below, above, [ring(below[:half], "y", 1), ring(above[half:], "y", -1)]


def exchange_edges(rows_in, cot_rows, bounds_row, device, edge):
    rows, width = rows_in.shape
    halo = 2 * edge
    sent = rows // 2 + edge
    load = bounds_row[device + 1] - bounds_row[device]
    slot = jnp.arange(cot_rows.shape[0], dtype=jnp.int32)[:, None]
    own = jnp.where(slot < load, cot_rows, jnp.zeros((), cot_rows.dtype))
    padded = jnp.concatenate([jnp.zeros((sent, width), own.dtype), own], axis=0)
    last_rows = lax.dynamic_slice_in_dim(padded, load, sent, 0)
    upwards = jnp.concatenate([rows_in[rows - halo :], last_rows], axis=0)
    downwards = jnp.concatenate([own[:sent], rows_in[:halo]], axis=0)
    return own, passed_along(upwards, SEQ, 1), passed_along(downwards, SEQ, -1)


def upstream_window(own, from_prev, from_next, bounds_row, device, rows, edge):
    came, width = from_prev.shape
    start_row = bounds_row[device]
    load = bounds_row[device + 1] - start_row
    joined = jnp.concatenate([from_prev, own, jnp.zeros((came, width), own.dtype)], axis=0)
    joined = lax.dynamic_update_slice_in_dim(joined, from_next, came + load, 0)
    first = rows * device - edge - (start_row - came)
    return lax.dynamic_slice_in_dim(joined, first, rows + 2 * edge, 0)


def owner_slots(out_rows, bounds_row, device):
    rows, width = out_rows.shape
    half = rows // 2
    from_prev = passed_along(out_rows[half:], SEQ, 1)
    from_next = passed_along(out_rows[:half], SEQ, -1)
    start_row = bounds_row[device]
    load = bounds_row[device + 1] - start_row
    joined = jnp.concatenate(
        [from_prev, out_rows, from_next, jnp.zeros((rows, width), out_rows.dtype)], axis=0
    )
    placed = lax.dynamic_slice_in_dim(joined, start_row - (rows * device - half), 2 * rows, 0)
    slot = jnp.arange(2 * rows, dtype=jnp.int32)[:, None]
    return jnp.where(slot < load, placed, jnp.zeros((), placed.dtype))


def by_receiver(hidden):
    width = hidden.shape[1]
    xs, zs, ys = lax.axis_size("x"), lax.axis_size("z"), lax.axis_size("y")
    kept = width // (xs * zs * ys)
    place = jnp.arange(width, dtype=jnp.int32)
    rest, row = place // kept, place % kept
    x, rest = rest % xs, rest // xs
    z, y = rest % zs, rest // zs
    feature = ((x * zs + z) * ys + y) * kept + row
    chosen = (place[:, None] == feature[None, :]).astype(bf16)
    return jnp.dot(hidden, chosen, preferred_element_type=f32).astype(bf16)


def hidden_blocks(hidden):
    return [ring(hidden, "x", -1), ring(hidden, "x", 2), ring(hidden, "x", 1), hidden]


def all_hidden(blocks):
    count = lax.axis_size("x")
    blocks = jnp.stack(blocks)
    others = other_core(blocks)
    core = lax.axis_index("c")
    both = jnp.stack(
        [jnp.where(core == 0, blocks, others), jnp.where(core == 0, others, blocks)], axis=1
    )
    twice = jnp.concatenate([both, both], axis=0)
    first = (count - 1 - lax.axis_index("x")) % count
    ordered = lax.dynamic_slice_in_dim(twice, first, count, 0)
    return ordered.reshape(-1, blocks.shape[-1])


def weight_gradient(hidden_all, mixed_share, frame_total, group_count):
    width = hidden_all.shape[1]
    share = mixed_share.shape[1]
    ys = lax.axis_size("y")
    y = lax.axis_index("y")
    taken = width // ys

    def product(steps):
        columns = lax.dynamic_slice_in_dim(hidden_all, taken * ((y + steps) % ys), taken, 1)
        return lax.dot_general(
            columns, mixed_share, (((0,), (0,)), ((), ())), preferred_element_type=f32
        )

    from_far = ring(product(2).astype(bf16), "y", 2).astype(f32)
    from_below = ring(product(1).astype(bf16), "y", 1).astype(f32)
    from_above = ring(product(3).astype(bf16), "y", -1).astype(f32)
    own, from_far = lax.optimization_barrier((product(0), from_far))
    summed = (own + from_far + from_below + from_above).astype(bf16)
    last = ("z", "x", "c")
    receivers = lax.axis_size(last)
    pieces = summed.reshape(receivers, taken // receivers, share)
    pieces = lax.all_to_all(pieces, last, 0, 0, tiled=True).astype(f32)
    pieces = jnp.sum(pieces.reshape(lax.axis_size("z"), -1, taken // receivers, share), axis=0)
    w_grad = jnp.swapaxes(pieces, 0, 1).reshape(taken // receivers, -1)
    return w_grad * (1.0 / math.sqrt(group_count * frame_total))


def on_device(frames, lengths, offsets, w_in, kernel, cotangent):
    rows_in = frames[0]
    rows, width = rows_in.shape
    half_width = kernel.shape[0] // 2
    edge = half_width + 1
    halo = 2 * edge
    seq_count = lax.axis_size(SEQ)
    device = lax.axis_index(SEQ)
    frame_total = seq_count * rows
    bounds_row = offsets[0]
    chip = lax.axis_index("y")
    chips = lax.axis_size("y")
    core = lax.axis_index("c").reshape(1)
    below, above, far = weight_blocks(w_in)
    own_other = other_core(w_in)
    own, from_prev, from_next = exchange_edges(
        rows_in, cotangent[0], bounds_row, device, edge
    )
    upstream = upstream_window(own, from_prev, from_next, bounds_row, device, rows, edge)
    rows_late, own_other = lax.optimization_barrier((rows_in, own_other))
    near = [w_in, own_other, below, other_core(below), above, other_core(above)]
    order = jnp.stack([chip, (chip + chips - 1) % chips, (chip + 1) % chips, (chip + 2) % chips])

    hidden_sent = by_receiver(normalize_rows(rows_late)[0].astype(bf16))
    hidden_sent, _, _ = lax.optimization_barrier(
        (hidden_sent, from_prev[:8, :LANES], from_next[:8, :LANES])
    )
    blocks = hidden_blocks(hidden_sent)

    bounds = [rows * device - edge, jnp.int32(frame_total)]
    utt_end = jnp.int32(0)
    for utt in range(lengths.shape[1] - 1):
        utt_end = utt_end + lengths[0, utt]
        bounds.append(utt_end)
    bounds = jnp.stack(bounds).astype(jnp.int32)

    hidden, part = run_part(order[:3], core, from_prev, rows_in, from_next, near, halo)
    far, _, _ = lax.optimization_barrier((far, upstream[:8, :LANES], part[:8, :LANES]))
    far = far + [other_core(piece) for piece in far]
    shares = lax.axis_size(("x", "c"))
    output, d_mixed, d_shares = run_main(
        bounds, order, core, hidden, part, upstream, kernel, far, rows, edge, shares
    )
    blocks, d_shares = lax.optimization_barrier((blocks, d_shares))
    hidden_all = all_hidden(blocks)
    mixed_share = lax.all_to_all(d_shares, ("x", "c"), 0, 0, tiled=True)
    mixed_share = mixed_share.reshape(shares * rows, -1)
    frame_grad = run_frame(order, core, rows_in, d_mixed, near + far)
    w_grad = weight_gradient(hidden_all, mixed_share, frame_total, chips * CHIP)
    owner_output = owner_slots(output, bounds_row, device)
    return (owner_output[None], frame_grad[None], w_grad)


def solution(mesh):
    seq_count, group_count = mesh.devices.shape
    ys, xs = group_count // CHIP, 4
    devices = mesh.devices.reshape(xs, seq_count // xs, ys, CHIP)
    groups = ("y", "c")
    return jax.shard_map(
        on_device,
        mesh=jax.sharding.Mesh(devices, ("x", "z", "y", "c")),
        in_specs=(
            P(groups, SEQ, None),
            P(groups, None),
            P(groups, None),
            P(groups, None),
            P(),
            P(groups, SEQ, None),
        ),
        out_specs=(P(groups, SEQ, None), P(groups, SEQ, None), P((*SEQ, *groups), None)),
        check_vma=False,
    )
```

time: 393 us -> 153 us (0.39)
  waiting for transfers between devices: 256 us -> 31.8 us
  Pallas kernels: 0 us -> 34.3 us
  other arithmetic: 43.6 us -> 11.9 us
  starting transfers between devices: 21 us -> 44.2 us
  blocking collectives: 19.1 us -> 0 us
  between operations: 18.5 us -> 5.97 us
  matrix products: 16.5 us -> 9.65 us
    reduce_scatter x1 -> x0, waiting for transfers between devices: 209 us -> none  [on_device(): lax.psum_scatter(rounded.astype(jnp.bfloat16), 'seq', scatter_dimension=0...]
    all_gather x1 -> x0, waiting for transfers between devices: 43.4 us -> none  [on_device(): lax.all_gather(w_in, 'fsdp', axis=0, tiled=True)]
    pallas_call x0 -> x3, Pallas kernels: none -> 34.3 us  [the longest x1 14.8 us: run_main(): pl.pallas_call(functools.partial(main_kernel, rows, edge), out_shape=(jax...]
    ppermute x0 -> x16, starting transfers between devices: none -> 21.4 us  [the longest x10 13.4 us: ring(): lax.ppermute(value, axis, [(i, (i + steps) % count) for i in range(count)])]
    unnamed x1 -> x0, blocking collectives: 19.1 us -> none
    ppermute x0 -> x16, waiting for transfers between devices: none -> 18.3 us  [the longest x10 18.3 us: ring(): lax.ppermute(value, axis, [(i, (i + steps) % count) for i in range(count)])]
    all_to_all x0 -> x2, starting transfers between devices: none -> 16.6 us  [the longest x1 12.4 us: weight_gradient(): pieces = lax.all_to_all(pieces, last, 0, 0, tiled=True).astype(f32)]
    reduce_sum x2 -> x1, other arithmetic: 14.2 us -> 0.14 us  [normalize_rows(): center = jnp.mean(values, axis=-1, keepdims=True)]
  transfers between devices with their start and end apart: 10 -> 22, of which waited for: 5 -> 7; matrix products, arithmetic and copies ran while one was open for 12% -> 19% of each run, Pallas kernels for 0% -> 23%
where the time goes in v2:
time: 153 us; the launch traced here: 152 us
  starting transfers between devices  44.2 us (29%)
  Pallas kernels  34.3 us (22%)
  waiting for transfers between devices  31.8 us (21%)
  local copies, waits for them, and re-layouts  14.6 us (10%)
  other arithmetic  11.9 us (8%)
  matrix products  9.65 us (6%)
  between operations  5.97 us (4%)
    ppermute x10, waiting for transfers between devices, ring(): lax.ppermute(value, axis, [(i, (i + steps) % count) for i in range(count)])  18.3 us
    pallas_call x1, Pallas kernels, run_main(): pl.pallas_call(functools.partial(main_kernel, rows, edge), out_shape=(jax...  14.8 us
    ppermute x10, starting transfers between devices, ring(): lax.ppermute(value, axis, [(i, (i + steps) % count) for i in range(count)])  13.4 us
    all_to_all x1, starting transfers between devices, weight_gradient(): pieces = lax.all_to_all(pieces, last, 0, 0, tiled=True).astype(f32)  12.4 us
    pallas_call x1, Pallas kernels, run_frame(): pl.pallas_call(frame_kernel, out_shape=jax.ShapeDtypeStruct((rows, width)...  10.1 us
    pallas_call x1, Pallas kernels, run_part(): pl.pallas_call(functools.partial(part_kernel, halo), out_shape=(jax.Shape...  9.41 us
    ppermute x6, starting transfers between devices, other_core(): return lax.ppermute(value, 'c', [(0, 1), (1, 0)])  7.96 us
    dot_general x4, matrix products, product(): lax.dot_general(columns, mixed_share, (((0,), (0,)), ((), ())), preferred...  7.58 us
  transfers between devices with their start and end apart: 22, of which 7 were waited for; matrix products, arithmetic and copies ran while one was open for 19% of the time, Pallas kernels for 23%

profile of v2, /device:TPU:1, one launch (start us, length us, event | category | flops | bytes accessed | tf_op | source)
XLA Modules:
  0.0 152.4 jit_solution(17533652165226981389)
XLA Ops:
  0.6 3.3 %collective-permute-start.2 = (bf16[192,3072]{1,0:T(8,128)(2,1)}, bf16[192,3072]{1,0:T(8,128)(2,1)}, u32[]{:S(2)}, u32[]{:S(2)}) collective-permute-start(bf16[192,3072]{1,0:T(8,128)(2,1)} %rest_0_.3), channel_id=1, source_target_pairs={{0,1},{1,0},{2,3},{3,2},{4,5},{5,4},{6,7},{7,6},{8,9},{9,8},{10,11... | collective-permute-start | bytes 3538952 | tf_op jit(solution)/shard_map/ppermute | solution.py:375
  4.0 2.7 %collective-permute-start.5 = (bf16[192,3072]{1,0:T(8,128)(2,1)}, bf16[192,3072]{1,0:T(8,128)(2,1)S(1)}, u32[]{:S(2)}, u32[]{:S(2)}) collective-permute-start(bf16[192,3072]{1,0:T(8,128)(2,1)} %rest_0_.3), channel_id=1, source_target_pairs={{0,6},{2,0},{4,2},{6,4},{1,7},{3,1},{5,3},{7,5},{8,14},{10,8},{12,... | collective-permute-start | bytes 3538952 | tf_op jit(solution)/shard_map/ppermute | solution.py:371
  13.3 1.9 %collective-permute-start = (bf16[112,1536]{1,0:T(8,128)(2,1)}, bf16[112,1536]{1,0:T(8,128)(2,1)S(1)}, u32[]{:S(2)}, u32[]{:S(2)}) collective-permute-start(bf16[112,1536]{1,0:T(8,128)(2,1)} %pad_maximum_fusion.1), channel_id=1, source_target_pairs={{0,8},{8,16},{16,24},{24,32},{32,40},{40,48},{48,56},{56,64},{64,7... | collective-permute-start | bytes 1032200 | tf_op jit(solution)/shard_map/ppermute | solution.py:24
  22.2 2.6 %maximum_maximum_fusion = bf16[480,1536]{1,0:T(8,128)(2,1)} fusion(bf16[256,1536]{1,0:T(8,128)(2,1)} %copy-done.14, bf16[112,1536]{1,0:T(8,128)(2,1)S(1)} %collective-permute-done.prev_ref, bf16[480]{0:T(512)(128)(2,1)S(1)} %pad.15.clone), kind=kLoop, calls=%fused_computation.14 | loop fusion | flops 4423680 | bytes 2606016 | tf_op jit(solution)/shard_map/concatenate | solution.py:402
  24.8 2.2 %collective-permute-done.1.next_ref = bf16[112,1536]{1,0:T(8,128)(2,1)S(1)} collective-permute-done((bf16[112,1536]{1,0:T(8,128)(2,1)}, bf16[112,1536]{1,0:T(8,128)(2,1)S(1)}, u32[]{:S(2)}, u32[]{:S(2)}) %collective-permute-start.1) | collective-permute-done | bytes 344096 | tf_op jit(solution)/shard_map/ppermute | solution.py:24
  27.0 2.8 %dynamic_update_slice.3 = bf16[480,1536]{1,0:T(8,128)(2,1)} dynamic-update-slice(bf16[480,1536]{1,0:T(8,128)(2,1)} %maximum_maximum_fusion, bf16[112,1536]{1,0:T(8,128)(2,1)S(1)} %collective-permute-done.1.next_ref, s32[]{:T(128)S(6)} %select_n.141, s32[]{:T(128)} %constant.128.clone.1) | dynamic-update-slice | bytes 688132 | tf_op jit(solution)/shard_map/dynamic_update_slice | solution.py:403
  29.8 3.1 %collective-permute-done.3.rest_2_ = bf16[192,3072]{1,0:T(8,128)(2,1)S(1)} collective-permute-done((bf16[192,3072]{1,0:T(8,128)(2,1)}, bf16[192,3072]{1,0:T(8,128)(2,1)S(1)}, u32[]{:S(2)}, u32[]{:S(2)}) %collective-permute-start.3) | collective-permute-done | bytes 1179680 | tf_op jit(solution)/shard_map/ppermute | solution.py:371
  33.1 2.7 %collective-permute-start.8 = (bf16[96,3072]{1,0:T(8,128)(2,1)S(1)}, bf16[96,3072]{1,0:T(8,128)(2,1)S(1)}, u32[]{:S(2)}, u32[]{:S(2)}) collective-permute-start(bf16[96,3072]{1,0:T(8,128)(2,1)S(1)} %slice.56), channel_id=1, source_target_pairs={{0,6},{2,0},{4,2},{6,4},{1,7},{3,1},{5,3},{7,5},{8,14},{10,8},{12,... | collective-permute-start | bytes 1769480 | tf_op jit(solution)/shard_map/ppermute | solution.py:371
  38.8 9.4 %collective-permute-done.7.rest_0_.rest_6_ = bf16[96,3072]{1,0:T(8,128)(2,1)S(1)} collective-permute-done((bf16[96,3072]{1,0:T(8,128)(2,1)S(1)}, bf16[96,3072]{1,0:T(8,128)(2,1)S(1)}, u32[]{:S(2)}, u32[]{:S(2)}) %collective-permute-start.7) | collective-permute-done | bytes 589856 | tf_op jit(solution)/shard_map/ppermute | solution.py:371
  50.2 2.1 %fusion.5 = bf16[128,1536]{1,0:T(8,128)(2,1)S(1)} fusion(s32[1536]{0:T(1024)S(1)} %fusion.34, bf16[128,1536]{1,0:T(8,128)(2,1)S(1)} %bitcast.43, f32[128]{0:T(128)S(1)} %add_rsqrt_fusion, f32[128]{0:T(128)S(1)} %broadcast_multiply_fusion.1), kind=kOutput, calls=%fused_computation.10 | convolution fusion | flops 607322112 | bytes 793600 | tf_op jit(solution)/shard_map/dot_general | solution.py:433
  52.3 2.4 %collective-permute-start.13 = (bf16[128,1536]{1,0:T(8,128)(2,1)S(1)}, bf16[128,1536]{1,0:T(8,128)(2,1)S(1)}, u32[]{:S(2)}, u32[]{:S(2)}) collective-permute-start(bf16[128,1536]{1,0:T(8,128)(2,1)S(1)} %fusion.5), channel_id=1, source_target_pairs={{0,192},{64,0},{128,64},{192,128},{1,193},{65,1},{129,65},{193,129... | collective-permute-start | bytes 1179656 | tf_op jit(solution)/shard_map/ppermute | solution.py:371
  55.5 9.4 %forward_part.1 = (bf16[192,1536]{1,0:T(8,128)(2,1)S(1)}, f32[192,3072]{1,0:T(8,128)}) custom-call(s32[3]{0:T(128)S(1)} %pad_add_fusion.1.at_ref, s32[1]{0:T(128)} %bitcast.10.core_ref, bf16[112,1536]{1,0:T(8,128)(2,1)S(1)} %collective-permute-done.prev_ref, bf16[128,1536]{1,0:T(8,128)(2,1)S(1)} %bitcast.44, ...), custom_call_target="tpu_custom_call" | custom-call | flops 2000000000 | bytes 8000000 | tf_op jit(solution)/shard_map/forward_part/pallas_call | solution.py:303
  65.1 2.0 %copy-done.12 = f32[192,3072]{1,0:T(8,128)S(1)} copy-done((f32[192,3072]{1,0:T(8,128)S(1)}, f32[192,3072]{1,0:T(8,128)}, u32[]{:S(2)}) %copy-start.12) | copy-done | bytes 2359320
  67.1 14.8 %main.1 = (bf16[128,1536]{1,0:T(8,128)(2,1)S(1)}, bf16[128,3072]{1,0:T(8,128)(2,1)S(1)}, bf16[8,128,384]{2,1,0:T(8,128)(2,1)}) custom-call(s32[5]{0:T(128)S(1)} %stack.56.bounds_ref, s32[4]{0:T(128)S(1)} %pad_add_fusion.at_ref, s32[1]{0:T(128)} %bitcast.10.core_ref, bf16[192,1536]{1,0:T(8,128)(2,1)S(1)} %get-tuple-element.20.hid_ref, ...), custom_call_target="tpu_custom_call" | custom-call | flops 6000000000 | bytes 12000000 | tf_op jit(solution)/shard_map/main/pallas_call | solution.py:326
  85.4 4.2 %all-to-all-start = ((bf16[8,128,384]{2,1,0:T(8,128)(2,1)}), bf16[8,128,384]{2,1,0:T(8,128)(2,1)}, u32[]{:S(2)}, u32[]{:S(2)}) async-start(bf16[8,128,384]{2,1,0:T(8,128)(2,1)} %get-tuple-element.32), calls=%async_computation | async-start | bytes 1572864 | tf_op jit(solution)/shard_map/all_to_all | solution.py:526
  93.0 1.9 %copy.10 = bf16[4,2,128,1536]{3,2,1,0:T(8,128)(2,1)} copy(bf16[4,2,128,1536]{3,2,0,1:T(8,128)(2,1)S(1)} %fusion.3) | data formatting | bytes 6291456 | tf_op jit(solution)/shard_map/dynamic_slice | solution.py:450
  94.9 7.0 %all-to-all-done = bf16[8,128,384]{2,1,0:T(8,128)(2,1)} async-done(((bf16[8,128,384]{2,1,0:T(8,128)(2,1)}), bf16[8,128,384]{2,1,0:T(8,128)(2,1)}, u32[]{:S(2)}, u32[]{:S(2)}) %all-to-all-start) | async-done | bytes 786464 | tf_op jit(solution)/shard_map/all_to_all | solution.py:526
  101.9 2.1 %convolution_convert_fusion = bf16[384,384]{1,0:T(8,128)(2,1)S(1)} fusion(bf16[1024,384]{1,0:T(8,128)(2,1)} %bitcast.24, bf16[1024,1536]{1,0:T(8,128)(2,1)} %bitcast.45, s32[]{:T(128)S(6)} %select_n.160), kind=kOutput, calls=%fused_computation.15 | convolution fusion | flops 302137344 | bytes 1867780 | tf_op jit(solution)/shard_map/dot_general | solution.py:463
  104.0 3.3 %collective-permute-start.19 = (bf16[384,384]{1,0:T(8,128)(2,1)S(1)}, bf16[384,384]{1,0:T(8,128)(2,1)S(1)}, u32[]{:S(2)}, u32[]{:S(2)}) collective-permute-start(bf16[384,384]{1,0:T(8,128)(2,1)S(1)} %convolution_convert_fusion), channel_id=1, source_target_pairs={{0,6},{2,0},{4,2},{6,4},{1,7},{3,1},{5,3},{7,5},{8,14},{10,8},{12,... | collective-permute-start | bytes 884744 | tf_op jit(solution)/shard_map/ppermute | solution.py:371
  107.4 2.0 %convolution_convert_fusion.1 = bf16[384,384]{1,0:T(8,128)(2,1)S(1)} fusion(bf16[1024,384]{1,0:T(8,128)(2,1)} %bitcast.24, bf16[1024,1536]{1,0:T(8,128)(2,1)} %bitcast.46, s32[]{:T(128)S(6)} %select_n.159), kind=kOutput, calls=%fused_computation.16 | convolution fusion | flops 302137344 | bytes 1867780 | tf_op jit(solution)/shard_map/dot_general | solution.py:463
  117.4 5.8 %collective-permute-done.17 = bf16[384,384]{1,0:T(8,128)(2,1)S(1)} collective-permute-done((bf16[384,384]{1,0:T(8,128)(2,1)S(1)}, bf16[384,384]{1,0:T(8,128)(2,1)S(1)}, u32[]{:S(2)}, u32[]{:S(2)}) %collective-permute-start.17) | collective-permute-done | bytes 294944 | tf_op jit(solution)/shard_map/ppermute | solution.py:371
  124.2 12.4 %all-to-all-start.1 = ((bf16[64,6,384]{2,1,0:T(8,128)(2,1)}), bf16[64,6,384]{2,1,0:T(8,128)(2,1)S(1)}, u32[]{:S(2)}, u32[]{:S(2)}) async-start(bf16[64,6,384]{2,1,0:T(8,128)(2,1)} %reshape.132), calls=%async_computation.1 | async-start | bytes 786432 | tf_op jit(solution)/shard_map/all_to_all | solution.py:475
  136.6 10.1 %frame_back.1 = bf16[128,1536]{1,0:T(8,128)(2,1)} custom-call(s32[4]{0:T(128)} %copy-done.11, s32[1]{0:T(128)} %bitcast.10.core_ref, bf16[128,1536]{1,0:T(8,128)(2,1)} %bitcast.40, bf16[128,3072]{1,0:T(8,128)(2,1)} %copy-done.6, bf16[192,3072]{1,0:T(8,128)(2,1)} %rest_0_.3, bf16[192,3072]{1,0:T(8,128)(2,1)} %collective-permute-done.2.rest_1_, ...), custom_call_target="tpu_custom_call" | custom-call | flops 2000000000 | bytes 11000000 | tf_op jit(solution)/shard_map/frame_back/pallas_call | solution.py:353
  148.2 3.5 %all-to-all-done.1 = bf16[64,6,384]{2,1,0:T(8,128)(2,1)S(1)} async-done(((bf16[64,6,384]{2,1,0:T(8,128)(2,1)}), bf16[64,6,384]{2,1,0:T(8,128)(2,1)S(1)}, u32[]{:S(2)}, u32[]{:S(2)}) %all-to-all-start.1) | async-done | bytes 294944 | tf_op jit(solution)/shard_map/all_to_all | solution.py:475
  (108 shorter events, 32.9 us)
Async XLA Ops:
  0.6 37.8 %collective-permute-start.2 = (bf16[192,3072]{1,0:T(8,128)(2,1)}, bf16[192,3072]{1,0:T(8,128)(2,1)}, u32[]{:S(2)}, u32[]{:S(2)}) collective-permute-start(bf16[192,3072]{1,0:T(8,128)(2,1)} %rest_0_.3), channel_id=1, source_target_pairs={{0,1},{1,0},{2,3},{3,2},{4,5},{5,4},{6,7},{7,6},{8,9},{9,8},{10,11... | collective-permute-start | bytes 3538952 | tf_op jit(solution)/shard_map/ppermute | solution.py:375
  4.0 28.9 %collective-permute-start.3 = (bf16[192,3072]{1,0:T(8,128)(2,1)}, bf16[192,3072]{1,0:T(8,128)(2,1)S(1)}, u32[]{:S(2)}, u32[]{:S(2)}) collective-permute-start(bf16[192,3072]{1,0:T(8,128)(2,1)} %rest_0_.3), channel_id=1, source_target_pairs={{0,2},{2,4},{4,6},{6,0},{1,3},{3,5},{5,7},{7,1},{8,10},{10,12},{12... | collective-permute-start | bytes 3538952 | tf_op jit(solution)/shard_map/ppermute | solution.py:371
  4.0 29.1 %collective-permute-start.5 = (bf16[192,3072]{1,0:T(8,128)(2,1)}, bf16[192,3072]{1,0:T(8,128)(2,1)S(1)}, u32[]{:S(2)}, u32[]{:S(2)}) collective-permute-start(bf16[192,3072]{1,0:T(8,128)(2,1)} %rest_0_.3), channel_id=1, source_target_pairs={{0,6},{2,0},{4,2},{6,4},{1,7},{3,1},{5,3},{7,5},{8,14},{10,8},{12,... | collective-permute-start | bytes 3538952 | tf_op jit(solution)/shard_map/ppermute | solution.py:371
  13.3 9.0 %collective-permute-start = (bf16[112,1536]{1,0:T(8,128)(2,1)}, bf16[112,1536]{1,0:T(8,128)(2,1)S(1)}, u32[]{:S(2)}, u32[]{:S(2)}) collective-permute-start(bf16[112,1536]{1,0:T(8,128)(2,1)} %pad_maximum_fusion.1), channel_id=1, source_target_pairs={{0,8},{8,16},{16,24},{24,32},{32,40},{40,48},{48,56},{56,64},{64,7... | collective-permute-start | bytes 1032200 | tf_op jit(solution)/shard_map/ppermute | solution.py:24
  15.9 11.2 %collective-permute-start.1 = (bf16[112,1536]{1,0:T(8,128)(2,1)}, bf16[112,1536]{1,0:T(8,128)(2,1)S(1)}, u32[]{:S(2)}, u32[]{:S(2)}) collective-permute-start(bf16[112,1536]{1,0:T(8,128)(2,1)} %pad_maximum_fusion.2), channel_id=1, source_target_pairs={{8,0},{16,8},{24,16},{32,24},{40,32},{48,40},{56,48},{64,56},{72,6... | collective-permute-start | bytes 1032200 | tf_op jit(solution)/shard_map/ppermute | solution.py:24
  21.4 43.6 %copy-start.11 = (s32[4]{0:T(128)}, s32[4]{0:T(128)S(1)}, u32[]{:S(2)}) copy-start(s32[4]{0:T(128)S(1)} %pad_add_fusion.at_ref) | copy-start | bytes 52
  32.9 22.6 %copy-start.1 = (bf16[192,3072]{1,0:T(8,128)(2,1)}, bf16[192,3072]{1,0:T(8,128)(2,1)S(1)}, u32[]{:S(2)}) copy-start(bf16[192,3072]{1,0:T(8,128)(2,1)S(1)} %collective-permute-done.3.rest_2_) | copy-start | bytes 3538948
  33.0 15.3 %collective-permute-start.7 = (bf16[96,3072]{1,0:T(8,128)(2,1)S(1)}, bf16[96,3072]{1,0:T(8,128)(2,1)S(1)}, u32[]{:S(2)}, u32[]{:S(2)}) collective-permute-start(bf16[96,3072]{1,0:T(8,128)(2,1)S(1)} %slice.55), channel_id=1, source_target_pairs={{0,2},{2,4},{4,6},{6,0},{1,3},{3,5},{5,7},{7,1},{8,10},{10,12},{12... | collective-permute-start | bytes 1769480 | tf_op jit(solution)/shard_map/ppermute | solution.py:371
  33.1 15.1 %collective-permute-start.8 = (bf16[96,3072]{1,0:T(8,128)(2,1)S(1)}, bf16[96,3072]{1,0:T(8,128)(2,1)S(1)}, u32[]{:S(2)}, u32[]{:S(2)}) collective-permute-start(bf16[96,3072]{1,0:T(8,128)(2,1)S(1)} %slice.56), channel_id=1, source_target_pairs={{0,6},{2,0},{4,2},{6,4},{1,7},{3,1},{5,3},{7,5},{8,14},{10,8},{12,... | collective-permute-start | bytes 1769480 | tf_op jit(solution)/shard_map/ppermute | solution.py:371
  35.8 18.8 %collective-permute-start.4 = (bf16[192,3072]{1,0:T(8,128)(2,1)S(1)}, bf16[192,3072]{1,0:T(8,128)(2,1)S(1)}, u32[]{:S(2)}, u32[]{:S(2)}) collective-permute-start(bf16[192,3072]{1,0:T(8,128)(2,1)S(1)} %collective-permute-done.3.rest_2_), channel_id=1, source_target_pairs={{0,1},{1,0},{2,3},{3,2},{4,5},{5,4},{6,7},{7,6},{8,9},{9,8},{10,11... | collective-permute-start | bytes 3538952 | tf_op jit(solution)/shard_map/ppermute | solution.py:375
  37.3 17.6 %collective-permute-start.6 = (bf16[192,3072]{1,0:T(8,128)(2,1)S(1)}, bf16[192,3072]{1,0:T(8,128)(2,1)S(1)}, u32[]{:S(2)}, u32[]{:S(2)}) collective-permute-start(bf16[192,3072]{1,0:T(8,128)(2,1)S(1)} %collective-permute-done.5.rest_4_), channel_id=1, source_target_pairs={{0,1},{1,0},{2,3},{3,2},{4,5},{5,4},{6,7},{7,6},{8,9},{9,8},{10,11... | collective-permute-start | bytes 3538952 | tf_op jit(solution)/shard_map/ppermute | solution.py:375
  48.2 16.7 %collective-permute-start.9 = (bf16[96,3072]{1,0:T(8,128)(2,1)S(1)}, bf16[96,3072]{1,0:T(8,128)(2,1)S(1)}, u32[]{:S(2)}, u32[]{:S(2)}) collective-permute-start(bf16[96,3072]{1,0:T(8,128)(2,1)S(1)} %collective-permute-done.7.rest_0_.rest_6_), channel_id=1, source_target_pairs={{0,1},{1,0},{2,3},{3,2},{4,5},{5,4},{6,7},{7,6},{8,9},{9,8},{10,11... | collective-permute-start | bytes 1769480 | tf_op jit(solution)/shard_map/ppermute | solution.py:375
  50.1 14.9 %collective-permute-start.10 = (bf16[96,3072]{1,0:T(8,128)(2,1)S(1)}, bf16[96,3072]{1,0:T(8,128)(2,1)S(1)}, u32[]{:S(2)}, u32[]{:S(2)}) collective-permute-start(bf16[96,3072]{1,0:T(8,128)(2,1)S(1)} %collective-permute-done.8.rest_1_.rest_7_), channel_id=1, source_target_pairs={{0,1},{1,0},{2,3},{3,2},{4,5},{5,4},{6,7},{7,6},{8,9},{9,8},{10,11... | collective-permute-start | bytes 1769480 | tf_op jit(solution)/shard_map/ppermute | solution.py:375
  52.3 29.7 %collective-permute-start.13 = (bf16[128,1536]{1,0:T(8,128)(2,1)S(1)}, bf16[128,1536]{1,0:T(8,128)(2,1)S(1)}, u32[]{:S(2)}, u32[]{:S(2)}) collective-permute-start(bf16[128,1536]{1,0:T(8,128)(2,1)S(1)} %fusion.5), channel_id=1, source_target_pairs={{0,192},{64,0},{128,64},{192,128},{1,193},{65,1},{129,65},{193,129... | collective-permute-start | bytes 1179656 | tf_op jit(solution)/shard_map/ppermute | solution.py:371
  54.7 27.3 %collective-permute-start.14 = (bf16[128,1536]{1,0:T(8,128)(2,1)S(1)}, bf16[128,1536]{1,0:T(8,128)(2,1)S(1)}, u32[]{:S(2)}, u32[]{:S(2)}) collective-permute-start(bf16[128,1536]{1,0:T(8,128)(2,1)S(1)} %fusion.5), channel_id=1, source_target_pairs={{0,128},{64,192},{128,0},{192,64},{1,129},{65,193},{129,1},{193,65... | collective-permute-start | bytes 1179656 | tf_op jit(solution)/shard_map/ppermute | solution.py:371
  54.9 27.1 %collective-permute-start.15 = (bf16[128,1536]{1,0:T(8,128)(2,1)S(1)}, bf16[128,1536]{1,0:T(8,128)(2,1)S(1)}, u32[]{:S(2)}, u32[]{:S(2)}) collective-permute-start(bf16[128,1536]{1,0:T(8,128)(2,1)S(1)} %fusion.5), channel_id=1, source_target_pairs={{0,64},{64,128},{128,192},{192,0},{1,65},{65,129},{129,193},{193,1... | collective-permute-start | bytes 1179656 | tf_op jit(solution)/shard_map/ppermute | solution.py:371
  83.2 6.3 %collective-permute-start.16 = (bf16[4,128,1536]{2,1,0:T(8,128)(2,1)S(1)}, bf16[4,128,1536]{2,1,0:T(8,128)(2,1)}, u32[]{:S(2)}, u32[]{:S(2)}) collective-permute-start(bf16[4,128,1536]{2,1,0:T(8,128)(2,1)S(1)} %pad_maximum_fusion), channel_id=1, source_target_pairs={{0,1},{1,0},{2,3},{3,2},{4,5},{5,4},{6,7},{7,6},{8,9},{9,8},{10,11... | collective-permute-start | bytes 4718600 | tf_op jit(solution)/shard_map/ppermute | solution.py:375
  85.4 16.5 %all-to-all-start = ((bf16[8,128,384]{2,1,0:T(8,128)(2,1)}), bf16[8,128,384]{2,1,0:T(8,128)(2,1)}, u32[]{:S(2)}, u32[]{:S(2)}) async-start(bf16[8,128,384]{2,1,0:T(8,128)(2,1)} %get-tuple-element.32), calls=%async_computation | async-start | bytes 1572864 | tf_op jit(solution)/shard_map/all_to_all | solution.py:526
  104.0 19.2 %collective-permute-start.19 = (bf16[384,384]{1,0:T(8,128)(2,1)S(1)}, bf16[384,384]{1,0:T(8,128)(2,1)S(1)}, u32[]{:S(2)}, u32[]{:S(2)}) collective-permute-start(bf16[384,384]{1,0:T(8,128)(2,1)S(1)} %convolution_convert_fusion), channel_id=1, source_target_pairs={{0,6},{2,0},{4,2},{6,4},{1,7},{3,1},{5,3},{7,5},{8,14},{10,8},{12,... | collective-permute-start | bytes 884744 | tf_op jit(solution)/shard_map/ppermute | solution.py:371
  109.3 13.9 %collective-permute-start.18 = (bf16[384,384]{1,0:T(8,128)(2,1)S(1)}, bf16[384,384]{1,0:T(8,128)(2,1)S(1)}, u32[]{:S(2)}, u32[]{:S(2)}) collective-permute-start(bf16[384,384]{1,0:T(8,128)(2,1)S(1)} %convolution_convert_fusion.1), channel_id=1, source_target_pairs={{0,2},{2,4},{4,6},{6,0},{1,3},{3,5},{5,7},{7,1},{8,10},{10,12},{12... | collective-permute-start | bytes 884744 | tf_op jit(solution)/shard_map/ppermute | solution.py:371
  111.2 12.0 %collective-permute-start.17 = (bf16[384,384]{1,0:T(8,128)(2,1)S(1)}, bf16[384,384]{1,0:T(8,128)(2,1)S(1)}, u32[]{:S(2)}, u32[]{:S(2)}) collective-permute-start(bf16[384,384]{1,0:T(8,128)(2,1)S(1)} %convolution_convert_fusion.2), channel_id=1, source_target_pairs={{0,4},{2,6},{4,0},{6,2},{1,5},{3,7},{5,1},{7,3},{8,12},{10,14},{12... | collective-permute-start | bytes 884744 | tf_op jit(solution)/shard_map/ppermute | solution.py:371
  112.5 34.2 %collective-permute-start.11 = (bf16[64,1536]{1,0:T(8,128)(2,1)S(1)}, bf16[64,1536]{1,0:T(8,128)(2,1)S(1)}, u32[]{:S(2)}, u32[]{:S(2)}) collective-permute-start(bf16[64,1536]{1,0:T(8,128)(2,1)S(1)} %get-tuple-element.40), channel_id=1, source_target_pairs={{0,8},{8,16},{16,24},{24,32},{32,40},{40,48},{48,56},{56,64},{64,7... | collective-permute-start | bytes 589832 | tf_op jit(solution)/shard_map/ppermute | solution.py:24
  114.3 32.4 %collective-permute-start.12 = (bf16[64,1536]{1,0:T(8,128)(2,1)S(1)}, bf16[64,1536]{1,0:T(8,128)(2,1)S(1)}, u32[]{:S(2)}, u32[]{:S(2)}) collective-permute-start(bf16[64,1536]{1,0:T(8,128)(2,1)S(1)} %get-tuple-element.39), channel_id=1, source_target_pairs={{8,0},{16,8},{24,16},{32,24},{40,32},{48,40},{56,48},{64,56},{72,6... | collective-permute-start | bytes 589832 | tf_op jit(solution)/shard_map/ppermute | solution.py:24
  124.2 27.5 %all-to-all-start.1 = ((bf16[64,6,384]{2,1,0:T(8,128)(2,1)}), bf16[64,6,384]{2,1,0:T(8,128)(2,1)S(1)}, u32[]{:S(2)}, u32[]{:S(2)}) async-start(bf16[64,6,384]{2,1,0:T(8,128)(2,1)} %reshape.132), calls=%async_computation.1 | async-start | bytes 786432 | tf_op jit(solution)/shard_map/all_to_all | solution.py:475
  (20 other events, 164.2 us)

commit v3 on v2

--- a/solution.py
+++ b/solution.py
@@ -40,15 +40,15 @@
 
 def tap_sum(copies, mask_ref, ker_ref, lanes, row, mask_row, count, flip, masked):
     tap_count = ker_ref.shape[0]
-    total = jnp.zeros((count, LANES), f32)
+    totals = [jnp.zeros((count, LANES), f32)] * 2
     for tap in range(tap_count):
         tile, shift = divmod(tap + 1, 8)
         weight = ker_ref[pl.ds(tap_count - 1 - tap if flip else tap, 1), lanes]
         term = weight * copies[shift, pl.ds(row + 8 * tile, count), :]
         if masked:
             term = term * mask_ref[tap, pl.ds(mask_row, count), :]
-        total = total + term
-    return total
+        totals[tap % 2] = totals[tap % 2] + term
+    return totals[0] + totals[1]
 
 
 def centred(values):
@@ -128,7 +128,7 @@
         part_ref[:, at] = total
 
 
-def main_kernel(rows, edge, bounds_ref, at_ref, core_ref, hid_ref, part_ref, up_ref, ker_ref, *rest):
+def main_kernel(rows, edge, bounds_ref, at_ref, core_ref, corner_ref, hid_ref, part_ref, up_ref, ker_ref, *rest):
     piece_count = len(rest) - 11
     pieces = rest[:piece_count]
     out_ref, dm_ref, shares_ref, w_buf, val, gate, glu, conv, copies_buf, mask_ref, sem = rest[piece_count:]
@@ -318,7 +318,7 @@
     )(chips, core, from_prev, rows_in, from_next, *pieces)
 
 
-def run_main(bounds, chips, core, hidden, part, upstream, kernel, pieces, rows, edge, shares):
+def run_main(bounds, chips, core, corner, hidden, part, upstream, kernel, pieces, rows, edge, shares):
     big, width = hidden.shape
     wide = upstream.shape[0]
     taps = kernel.shape[0]
@@ -330,7 +330,7 @@
             jax.ShapeDtypeStruct((rows, 2 * width), bf16),
             jax.ShapeDtypeStruct((shares, rows, 2 * width // shares), bf16),
         ),
-        in_specs=[SMEM, SMEM, SMEM, VMEM, VMEM, VMEM, VMEM] + [ANY] * len(pieces),
+        in_specs=[SMEM, SMEM, SMEM, VMEM, VMEM, VMEM, VMEM, VMEM] + [ANY] * len(pieces),
         out_specs=(VMEM, VMEM, VMEM),
         scratch_shapes=[
             pltpu.VMEM((depth, 2 * width), bf16),
@@ -345,7 +345,7 @@
         compiler_params=limit(44),
         cost_estimate=pl.CostEstimate(flops=6 * 10**9, bytes_accessed=12 * 10**6, transcendentals=0),
         name="main",
-    )(bounds, chips, core, hidden, part, upstream, kernel, *pieces)
+    )(bounds, chips, core, corner, hidden, part, upstream, kernel, *pieces)
 
 
 def run_frame(chips, core, rows_in, d_mixed, pieces):
@@ -502,9 +502,6 @@
     order = jnp.stack([chip, (chip + chips - 1) % chips, (chip + 1) % chips, (chip + 2) % chips])
 
     hidden_sent = by_receiver(normalize_rows(rows_late)[0].astype(bf16))
-    hidden_sent, _, _ = lax.optimization_barrier(
-        (hidden_sent, from_prev[:8, :LANES], from_next[:8, :LANES])
-    )
     blocks = hidden_blocks(hidden_sent)
 
     bounds = [rows * device - edge, jnp.int32(frame_total)]
@@ -515,11 +512,11 @@
     bounds = jnp.stack(bounds).astype(jnp.int32)
 
     hidden, part = run_part(order[:3], core, from_prev, rows_in, from_next, near, halo)
-    far, _, _ = lax.optimization_barrier((far, upstream[:8, :LANES], part[:8, :LANES]))
+    far, corner = lax.optimization_barrier((far, part[:8, :LANES]))
     far = far + [other_core(piece) for piece in far]
     shares = lax.axis_size(("x", "c"))
     output, d_mixed, d_shares = run_main(
-        bounds, order, core, hidden, part, upstream, kernel, far, rows, edge, shares
+        bounds, order, core, corner, hidden, part, upstream, kernel, far, rows, edge, shares
     )
     blocks, d_shares = lax.optimization_barrier((blocks, d_shares))
     hidden_all = all_hidden(blocks)

time: 153 us -> 150 us (0.980)
  local copies, waits for them, and re-layouts: 14.6 us -> 10.4 us
  starting transfers between devices: 44.2 us -> 48.2 us
  waiting for transfers between devices: 31.8 us -> 28.1 us
  other arithmetic: 11.9 us -> 14.2 us
    unnamed x44, local copies, waits for them, and re-layouts: 3.84 us -> 0.81 us
    ppermute x4, waiting for transfers between devices: 3 us -> 0.01 us  [passed_along(): lax.ppermute(value, axis, [(source, source + steps) for source in range(i...]
    ppermute x4, starting transfers between devices: 6.27 us -> 8.59 us  [passed_along(): lax.ppermute(value, axis, [(source, source + steps) for source in range(i...]
    all_to_all x1, waiting for transfers between devices: 7.01 us -> 8.62 us  [on_device(): mixed_share = lax.all_to_all(d_shares, ('x', 'c'), 0, 0, tiled=True)]
  transfers between devices with their start and end apart: 22 -> 22, of which waited for: 7 -> 6; matrix products, arithmetic and copies ran while one was open for 19% -> 19% of each run, Pallas kernels for 23% -> 23%
where the time goes in v3:
time: 150 us; the launch traced here: 149 us
  starting transfers between devices  48.2 us (32%)
  Pallas kernels  33.6 us (22%)
  waiting for transfers between devices  28.1 us (19%)
  other arithmetic  14.2 us (9%)
  local copies, waits for them, and re-layouts  10.4 us (7%)
  matrix products  9.04 us (6%)
  between operations  5.77 us (4%)
    ppermute x10, waiting for transfers between devices, ring(): lax.ppermute(value, axis, [(i, (i + steps) % count) for i in range(count)])  16.9 us
    pallas_call x1, Pallas kernels, run_main(): pl.pallas_call(functools.partial(main_kernel, rows, edge), out_shape=(jax...  14.7 us
    ppermute x10, starting transfers between devices, ring(): lax.ppermute(value, axis, [(i, (i + steps) % count) for i in range(count)])  14.3 us
    all_to_all x1, starting transfers between devices, weight_gradient(): pieces = lax.all_to_all(pieces, last, 0, 0, tiled=True).astype(f32)  13 us
    pallas_call x1, Pallas kernels, run_frame(): pl.pallas_call(frame_kernel, out_shape=jax.ShapeDtypeStruct((rows, width)...  10.1 us
    pallas_call x1, Pallas kernels, run_part(): pl.pallas_call(functools.partial(part_kernel, halo), out_shape=(jax.Shape...  8.93 us
    all_to_all x1, waiting for transfers between devices, on_device(): mixed_share = lax.all_to_all(d_shares, ('x', 'c'), 0, 0, tiled=True)  8.62 us
    ppermute x4, starting transfers between devices, passed_along(): lax.ppermute(value, axis, [(source, source + steps) for source in range(i...  8.59 us
  transfers between devices with their start and end apart: 22, of which 6 were waited for; matrix products, arithmetic and copies ran while one was open for 19% of the time, Pallas kernels for 23%

profile of v3, /device:TPU:1, one launch (start us, length us, event | category | flops | bytes accessed | tf_op | source)
XLA Modules:
  0.0 149.4 jit_solution(13863344816409735065)
XLA Ops:
  0.6 2.2 %collective-permute-start = (bf16[192,3072]{1,0:T(8,128)(2,1)}, bf16[192,3072]{1,0:T(8,128)(2,1)S(1)}, u32[]{:S(2)}, u32[]{:S(2)}) collective-permute-start(bf16[192,3072]{1,0:T(8,128)(2,1)} %rest_0_.3), channel_id=1, source_target_pairs={{0,2},{2,4},{4,6},{6,0},{1,3},{3,5},{5,7},{7,1},{8,10},{10,12},{12... | collective-permute-start | bytes 3538952 | tf_op jit(solution)/shard_map/ppermute | solution.py:371
  4.4 2.8 %collective-permute-start.6 = (bf16[192,3072]{1,0:T(8,128)(2,1)}, bf16[192,3072]{1,0:T(8,128)(2,1)}, u32[]{:S(2)}, u32[]{:S(2)}) collective-permute-start(bf16[192,3072]{1,0:T(8,128)(2,1)} %rest_0_.3), channel_id=1, source_target_pairs={{0,1},{1,0},{2,3},{3,2},{4,5},{5,4},{6,7},{7,6},{8,9},{9,8},{10,11... | collective-permute-start | bytes 3538952 | tf_op jit(solution)/shard_map/ppermute | solution.py:375
  12.7 1.8 %collective-permute-start.4 = (bf16[112,1536]{1,0:T(8,128)(2,1)}, bf16[112,1536]{1,0:T(8,128)(2,1)S(1)}, u32[]{:S(2)}, u32[]{:S(2)}) collective-permute-start(bf16[112,1536]{1,0:T(8,128)(2,1)} %pad_maximum_fusion.1), channel_id=1, source_target_pairs={{0,8},{8,16},{16,24},{24,32},{32,40},{40,48},{48,56},{56,64},{64,7... | collective-permute-start | bytes 1032200 | tf_op jit(solution)/shard_map/ppermute | solution.py:24
  20.7 7.5 %collective-permute-done.rest_2_ = bf16[192,3072]{1,0:T(8,128)(2,1)S(1)} collective-permute-done((bf16[192,3072]{1,0:T(8,128)(2,1)}, bf16[192,3072]{1,0:T(8,128)(2,1)S(1)}, u32[]{:S(2)}, u32[]{:S(2)}) %collective-permute-start) | collective-permute-done | bytes 1179680 | tf_op jit(solution)/shard_map/ppermute | solution.py:371
  28.1 3.3 %collective-permute-start.7 = (bf16[192,3072]{1,0:T(8,128)(2,1)S(1)}, bf16[192,3072]{1,0:T(8,128)(2,1)}, u32[]{:S(2)}, u32[]{:S(2)}) collective-permute-start(bf16[192,3072]{1,0:T(8,128)(2,1)S(1)} %collective-permute-done.rest_2_), channel_id=1, source_target_pairs={{0,1},{1,0},{2,3},{3,2},{4,5},{5,4},{6,7},{7,6},{8,9},{9,8},{10,11... | collective-permute-start | bytes 3538952 | tf_op jit(solution)/shard_map/ppermute | solution.py:375
  31.6 2.8 %maximum_maximum_fusion = bf16[480,1536]{1,0:T(8,128)(2,1)} fusion(bf16[256,1536]{1,0:T(8,128)(2,1)} %copy-done.12, bf16[112,1536]{1,0:T(8,128)(2,1)S(1)} %collective-permute-done.4.prev_ref, bf16[480]{0:T(512)(128)(2,1)S(1)} %pad.15.clone), kind=kLoop, calls=%fused_computation.14 | loop fusion | flops 4423680 | bytes 2606016 | tf_op jit(solution)/shard_map/concatenate | solution.py:402
  34.4 2.8 %dynamic_update_slice.3 = bf16[480,1536]{1,0:T(8,128)(2,1)} dynamic-update-slice(bf16[480,1536]{1,0:T(8,128)(2,1)} %maximum_maximum_fusion, bf16[112,1536]{1,0:T(8,128)(2,1)S(1)} %collective-permute-done.5.next_ref, s32[]{:T(128)S(6)} %select_n.141, s32[]{:T(128)} %constant.128.clone.1) | dynamic-update-slice | bytes 688132 | tf_op jit(solution)/shard_map/dynamic_update_slice | solution.py:403
  38.3 1.8 %collective-permute-start.3 = (bf16[96,3072]{1,0:T(8,128)(2,1)S(1)}, bf16[96,3072]{1,0:T(8,128)(2,1)S(1)}, u32[]{:S(2)}, u32[]{:S(2)}) collective-permute-start(bf16[96,3072]{1,0:T(8,128)(2,1)S(1)} %slice.55), channel_id=1, source_target_pairs={{0,6},{2,0},{4,2},{6,4},{1,7},{3,1},{5,3},{7,5},{8,14},{10,8},{12,... | collective-permute-start | bytes 1769480 | tf_op jit(solution)/shard_map/ppermute | solution.py:371
  41.5 8.9 %forward_part.1 = (bf16[192,1536]{1,0:T(8,128)(2,1)S(1)}, f32[192,3072]{1,0:T(8,128)}) custom-call(s32[3]{0:T(128)S(1)} %pad_add_fusion.1.at_ref, s32[1]{0:T(128)} %bitcast.10.core_ref, bf16[112,1536]{1,0:T(8,128)(2,1)S(1)} %collective-permute-done.4.prev_ref, bf16[128,1536]{1,0:T(8,128)(2,1)S(1)} %bitcast.42, ...), custom_call_target="tpu_custom_call" | custom-call | flops 2000000000 | bytes 8000000 | tf_op jit(solution)/shard_map/forward_part/pallas_call | solution.py:303
  51.1 2.0 %collective-permute-done.1.rest_0_.rest_6_ = bf16[96,3072]{1,0:T(8,128)(2,1)S(1)} collective-permute-done((bf16[96,3072]{1,0:T(8,128)(2,1)S(1)}, bf16[96,3072]{1,0:T(8,128)(2,1)S(1)}, u32[]{:S(2)}, u32[]{:S(2)}) %collective-permute-start.1) | collective-permute-done | bytes 589856 | tf_op jit(solution)/shard_map/ppermute | solution.py:371
  54.8 2.1 %fusion.5 = bf16[128,1536]{1,0:T(8,128)(2,1)S(1)} fusion(s32[1536]{0:T(1024)S(1)} %fusion.34, bf16[128,1536]{1,0:T(8,128)(2,1)S(1)} %bitcast.44, f32[128]{0:T(128)S(1)} %add_rsqrt_fusion, f32[128]{0:T(128)S(1)} %broadcast_multiply_fusion.1), kind=kOutput, calls=%fused_computation.10 | convolution fusion | flops 607322112 | bytes 793600 | tf_op jit(solution)/shard_map/dot_general | solution.py:433
  56.8 2.6 %collective-permute-start.13 = (bf16[128,1536]{1,0:T(8,128)(2,1)S(1)}, bf16[128,1536]{1,0:T(8,128)(2,1)S(1)}, u32[]{:S(2)}, u32[]{:S(2)}) collective-permute-start(bf16[128,1536]{1,0:T(8,128)(2,1)S(1)} %fusion.5), channel_id=1, source_target_pairs={{0,192},{64,0},{128,64},{192,128},{1,193},{65,1},{129,65},{193,129... | collective-permute-start | bytes 1179656 | tf_op jit(solution)/shard_map/ppermute | solution.py:371
  60.6 14.7 %main.1 = (bf16[128,1536]{1,0:T(8,128)(2,1)S(1)}, bf16[128,3072]{1,0:T(8,128)(2,1)S(1)}, bf16[8,128,384]{2,1,0:T(8,128)(2,1)}) custom-call(s32[5]{0:T(128)S(1)} %stack.56.bounds_ref, s32[4]{0:T(128)S(1)} %pad_add_fusion.at_ref, s32[1]{0:T(128)} %bitcast.10.core_ref, f32[8,128]{1,0:T(8,128)S(1)} %slice.51.corner_ref, ...), custom_call_target="tpu_custom_call" | custom-call | flops 6000000000 | bytes 12000000 | tf_op jit(solution)/shard_map/main/pallas_call | solution.py:326
  75.3 5.0 %collective-permute-done.15 = bf16[128,1536]{1,0:T(8,128)(2,1)S(1)} collective-permute-done((bf16[128,1536]{1,0:T(8,128)(2,1)S(1)}, bf16[128,1536]{1,0:T(8,128)(2,1)S(1)}, u32[]{:S(2)}, u32[]{:S(2)}) %collective-permute-start.15) | collective-permute-done | bytes 393248 | tf_op jit(solution)/shard_map/ppermute | solution.py:371
  83.2 4.2 %all-to-all-start = ((bf16[8,128,384]{2,1,0:T(8,128)(2,1)}), bf16[8,128,384]{2,1,0:T(8,128)(2,1)}, u32[]{:S(2)}, u32[]{:S(2)}) async-start(bf16[8,128,384]{2,1,0:T(8,128)(2,1)} %get-tuple-element.34), calls=%async_computation | async-start | bytes 1572864 | tf_op jit(solution)/shard_map/all_to_all | solution.py:523
  91.2 8.6 %all-to-all-done = bf16[8,128,384]{2,1,0:T(8,128)(2,1)} async-done(((bf16[8,128,384]{2,1,0:T(8,128)(2,1)}), bf16[8,128,384]{2,1,0:T(8,128)(2,1)}, u32[]{:S(2)}, u32[]{:S(2)}) %all-to-all-start) | async-done | bytes 786464 | tf_op jit(solution)/shard_map/all_to_all | solution.py:523
  101.5 2.7 %collective-permute-start.19 = (bf16[384,384]{1,0:T(8,128)(2,1)S(1)}, bf16[384,384]{1,0:T(8,128)(2,1)S(1)}, u32[]{:S(2)}, u32[]{:S(2)}) collective-permute-start(bf16[384,384]{1,0:T(8,128)(2,1)S(1)} %convolution_convert_fusion), channel_id=1, source_target_pairs={{0,6},{2,0},{4,2},{6,4},{1,7},{3,1},{5,3},{7,5},{8,14},{10,8},{12,... | collective-permute-start | bytes 884744 | tf_op jit(solution)/shard_map/ppermute | solution.py:371
  106.1 1.8 %convolution_convert_fusion.2 = bf16[384,384]{1,0:T(8,128)(2,1)S(1)} fusion(bf16[1024,384]{1,0:T(8,128)(2,1)} %bitcast.24, bf16[1024,1536]{1,0:T(8,128)(2,1)S(1)} %bitcast.47, s32[]{:T(128)S(6)} %select_n.158), kind=kOutput, calls=%fused_computation.17 | convolution fusion | flops 302137344 | bytes 1867780 | tf_op jit(solution)/shard_map/dot_general | solution.py:463
  109.8 4.2 %collective-permute-start.11 = (bf16[64,1536]{1,0:T(8,128)(2,1)}, bf16[64,1536]{1,0:T(8,128)(2,1)}, u32[]{:S(2)}, u32[]{:S(2)}) collective-permute-start(bf16[64,1536]{1,0:T(8,128)(2,1)} %get-tuple-element.42), channel_id=1, source_target_pairs={{0,8},{8,16},{16,24},{24,32},{32,40},{40,48},{48,56},{56,64},{64,7... | collective-permute-start | bytes 589832 | tf_op jit(solution)/shard_map/ppermute | solution.py:24
  117.1 2.4 %collective-permute-done.17 = bf16[384,384]{1,0:T(8,128)(2,1)S(1)} collective-permute-done((bf16[384,384]{1,0:T(8,128)(2,1)S(1)}, bf16[384,384]{1,0:T(8,128)(2,1)S(1)}, u32[]{:S(2)}, u32[]{:S(2)}) %collective-permute-start.17) | collective-permute-done | bytes 294944 | tf_op jit(solution)/shard_map/ppermute | solution.py:371
  120.6 13.0 %all-to-all-start.1 = ((bf16[64,6,384]{2,1,0:T(8,128)(2,1)}), bf16[64,6,384]{2,1,0:T(8,128)(2,1)S(1)}, u32[]{:S(2)}, u32[]{:S(2)}) async-start(bf16[64,6,384]{2,1,0:T(8,128)(2,1)} %reshape.132), calls=%async_computation.1 | async-start | bytes 786432 | tf_op jit(solution)/shard_map/all_to_all | solution.py:475
  133.6 10.1 %frame_back.1 = bf16[128,1536]{1,0:T(8,128)(2,1)} custom-call(s32[4]{0:T(128)} %copy-done.9, s32[1]{0:T(128)} %bitcast.10.core_ref, bf16[128,1536]{1,0:T(8,128)(2,1)} %bitcast.40, bf16[128,3072]{1,0:T(8,128)(2,1)} %copy-done.4, bf16[192,3072]{1,0:T(8,128)(2,1)} %rest_0_.3, bf16[192,3072]{1,0:T(8,128)(2,1)} %collective-permute-done.6.rest_1_, ...), custom_call_target="tpu_custom_call" | custom-call | flops 2000000000 | bytes 11000000 | tf_op jit(solution)/shard_map/frame_back/pallas_call | solution.py:353
  143.7 2.4 %fusion.14 = bf16[1,256,1536]{2,1,0:T(8,128)(2,1)} fusion(s32[]{:T(128)S(6)} %select_n.143, bf16[64,1536]{1,0:T(8,128)(2,1)} %collective-permute-done.11, bf16[128,1536]{1,0:T(8,128)(2,1)S(1)} %get-tuple-element.26, bf16[64,1536]{1,0:T(8,128)(2,1)} %collective-permute-done.12, pred[256]{0:T(512)(128)(4,1)S(1)} %iota_compare_fusion.4, ...), kind=kLoop, calls=%fused_computation.32 | loop fusion | flops 3538944 | bytes 1573636 | tf_op jit(solution)/shard_map/broadcast_in_dim | solution.py:528
  146.1 2.5 %all-to-all-done.1 = bf16[64,6,384]{2,1,0:T(8,128)(2,1)S(1)} async-done(((bf16[64,6,384]{2,1,0:T(8,128)(2,1)}), bf16[64,6,384]{2,1,0:T(8,128)(2,1)S(1)}, u32[]{:S(2)}, u32[]{:S(2)}) %all-to-all-start.1) | async-done | bytes 294944 | tf_op jit(solution)/shard_map/all_to_all | solution.py:475
  (109 shorter events, 31.5 us)
Async XLA Ops:
  0.6 27.5 %collective-permute-start = (bf16[192,3072]{1,0:T(8,128)(2,1)}, bf16[192,3072]{1,0:T(8,128)(2,1)S(1)}, u32[]{:S(2)}, u32[]{:S(2)}) collective-permute-start(bf16[192,3072]{1,0:T(8,128)(2,1)} %rest_0_.3), channel_id=1, source_target_pairs={{0,2},{2,4},{4,6},{6,0},{1,3},{3,5},{5,7},{7,1},{8,10},{10,12},{12... | collective-permute-start | bytes 3538952 | tf_op jit(solution)/shard_map/ppermute | solution.py:371
  2.8 28.6 %collective-permute-start.2 = (bf16[192,3072]{1,0:T(8,128)(2,1)}, bf16[192,3072]{1,0:T(8,128)(2,1)S(1)}, u32[]{:S(2)}, u32[]{:S(2)}) collective-permute-start(bf16[192,3072]{1,0:T(8,128)(2,1)} %rest_0_.3), channel_id=1, source_target_pairs={{0,6},{2,0},{4,2},{6,4},{1,7},{3,1},{5,3},{7,5},{8,14},{10,8},{12,... | collective-permute-start | bytes 3538952 | tf_op jit(solution)/shard_map/ppermute | solution.py:371
  4.4 36.9 %collective-permute-start.6 = (bf16[192,3072]{1,0:T(8,128)(2,1)}, bf16[192,3072]{1,0:T(8,128)(2,1)}, u32[]{:S(2)}, u32[]{:S(2)}) collective-permute-start(bf16[192,3072]{1,0:T(8,128)(2,1)} %rest_0_.3), channel_id=1, source_target_pairs={{0,1},{1,0},{2,3},{3,2},{4,5},{5,4},{6,7},{7,6},{8,9},{9,8},{10,11... | collective-permute-start | bytes 3538952 | tf_op jit(solution)/shard_map/ppermute | solution.py:375
  12.7 18.9 %collective-permute-start.4 = (bf16[112,1536]{1,0:T(8,128)(2,1)}, bf16[112,1536]{1,0:T(8,128)(2,1)S(1)}, u32[]{:S(2)}, u32[]{:S(2)}) collective-permute-start(bf16[112,1536]{1,0:T(8,128)(2,1)} %pad_maximum_fusion.1), channel_id=1, source_target_pairs={{0,8},{8,16},{16,24},{24,32},{32,40},{40,48},{48,56},{56,64},{64,7... | collective-permute-start | bytes 1032200 | tf_op jit(solution)/shard_map/ppermute | solution.py:24
  15.3 19.2 %collective-permute-start.5 = (bf16[112,1536]{1,0:T(8,128)(2,1)}, bf16[112,1536]{1,0:T(8,128)(2,1)S(1)}, u32[]{:S(2)}, u32[]{:S(2)}) collective-permute-start(bf16[112,1536]{1,0:T(8,128)(2,1)} %pad_maximum_fusion.2), channel_id=1, source_target_pairs={{8,0},{16,8},{24,16},{32,24},{40,32},{48,40},{56,48},{64,56},{72,6... | collective-permute-start | bytes 1032200 | tf_op jit(solution)/shard_map/ppermute | solution.py:24
  28.1 13.3 %collective-permute-start.7 = (bf16[192,3072]{1,0:T(8,128)(2,1)S(1)}, bf16[192,3072]{1,0:T(8,128)(2,1)}, u32[]{:S(2)}, u32[]{:S(2)}) collective-permute-start(bf16[192,3072]{1,0:T(8,128)(2,1)S(1)} %collective-permute-done.rest_2_), channel_id=1, source_target_pairs={{0,1},{1,0},{2,3},{3,2},{4,5},{5,4},{6,7},{7,6},{8,9},{9,8},{10,11... | collective-permute-start | bytes 3538952 | tf_op jit(solution)/shard_map/ppermute | solution.py:375
  31.4 10.0 %collective-permute-start.8 = (bf16[192,3072]{1,0:T(8,128)(2,1)S(1)}, bf16[192,3072]{1,0:T(8,128)(2,1)}, u32[]{:S(2)}, u32[]{:S(2)}) collective-permute-start(bf16[192,3072]{1,0:T(8,128)(2,1)S(1)} %collective-permute-done.2.rest_4_), channel_id=1, source_target_pairs={{0,1},{1,0},{2,3},{3,2},{4,5},{5,4},{6,7},{7,6},{8,9},{9,8},{10,11... | collective-permute-start | bytes 3538952 | tf_op jit(solution)/shard_map/ppermute | solution.py:375
  31.6 29.0 %copy-start.9 = (s32[4]{0:T(128)}, s32[4]{0:T(128)S(1)}, u32[]{:S(2)}) copy-start(s32[4]{0:T(128)S(1)} %pad_add_fusion.at_ref) | copy-start | bytes 52
  37.2 15.8 %collective-permute-start.1 = (bf16[96,3072]{1,0:T(8,128)(2,1)S(1)}, bf16[96,3072]{1,0:T(8,128)(2,1)S(1)}, u32[]{:S(2)}, u32[]{:S(2)}) collective-permute-start(bf16[96,3072]{1,0:T(8,128)(2,1)S(1)} %slice.54), channel_id=1, source_target_pairs={{0,2},{2,4},{4,6},{6,0},{1,3},{3,5},{5,7},{7,1},{8,10},{10,12},{12... | collective-permute-start | bytes 1769480 | tf_op jit(solution)/shard_map/ppermute | solution.py:371
  38.3 14.7 %collective-permute-start.3 = (bf16[96,3072]{1,0:T(8,128)(2,1)S(1)}, bf16[96,3072]{1,0:T(8,128)(2,1)S(1)}, u32[]{:S(2)}, u32[]{:S(2)}) collective-permute-start(bf16[96,3072]{1,0:T(8,128)(2,1)S(1)} %slice.55), channel_id=1, source_target_pairs={{0,6},{2,0},{4,2},{6,4},{1,7},{3,1},{5,3},{7,5},{8,14},{10,8},{12,... | collective-permute-start | bytes 1769480 | tf_op jit(solution)/shard_map/ppermute | solution.py:371
  53.1 7.5 %collective-permute-start.9 = (bf16[96,3072]{1,0:T(8,128)(2,1)S(1)}, bf16[96,3072]{1,0:T(8,128)(2,1)S(1)}, u32[]{:S(2)}, u32[]{:S(2)}) collective-permute-start(bf16[96,3072]{1,0:T(8,128)(2,1)S(1)} %collective-permute-done.1.rest_0_.rest_6_), channel_id=1, source_target_pairs={{0,1},{1,0},{2,3},{3,2},{4,5},{5,4},{6,7},{7,6},{8,9},{9,8},{10,11... | collective-permute-start | bytes 1769480 | tf_op jit(solution)/shard_map/ppermute | solution.py:375
  54.4 6.2 %collective-permute-start.10 = (bf16[96,3072]{1,0:T(8,128)(2,1)S(1)}, bf16[96,3072]{1,0:T(8,128)(2,1)S(1)}, u32[]{:S(2)}, u32[]{:S(2)}) collective-permute-start(bf16[96,3072]{1,0:T(8,128)(2,1)S(1)} %collective-permute-done.3.rest_1_.rest_7_), channel_id=1, source_target_pairs={{0,1},{1,0},{2,3},{3,2},{4,5},{5,4},{6,7},{7,6},{8,9},{9,8},{10,11... | collective-permute-start | bytes 1769480 | tf_op jit(solution)/shard_map/ppermute | solution.py:375
  56.8 23.5 %copy-start.13 = (bf16[128,1536]{1,0:T(8,128)(2,1)}, bf16[128,1536]{1,0:T(8,128)(2,1)S(1)}, u32[]{:S(2)}) copy-start(bf16[128,1536]{1,0:T(8,128)(2,1)S(1)} %fusion.5) | copy-start | bytes 1179652
  56.8 18.5 %collective-permute-start.13 = (bf16[128,1536]{1,0:T(8,128)(2,1)S(1)}, bf16[128,1536]{1,0:T(8,128)(2,1)S(1)}, u32[]{:S(2)}, u32[]{:S(2)}) collective-permute-start(bf16[128,1536]{1,0:T(8,128)(2,1)S(1)} %fusion.5), channel_id=1, source_target_pairs={{0,192},{64,0},{128,64},{192,128},{1,193},{65,1},{129,65},{193,129... | collective-permute-start | bytes 1179656 | tf_op jit(solution)/shard_map/ppermute | solution.py:371
  59.4 15.9 %collective-permute-start.14 = (bf16[128,1536]{1,0:T(8,128)(2,1)S(1)}, bf16[128,1536]{1,0:T(8,128)(2,1)S(1)}, u32[]{:S(2)}, u32[]{:S(2)}) collective-permute-start(bf16[128,1536]{1,0:T(8,128)(2,1)S(1)} %fusion.5), channel_id=1, source_target_pairs={{0,128},{64,192},{128,0},{192,64},{1,129},{65,193},{129,1},{193,65... | collective-permute-start | bytes 1179656 | tf_op jit(solution)/shard_map/ppermute | solution.py:371
  59.9 20.5 %collective-permute-start.15 = (bf16[128,1536]{1,0:T(8,128)(2,1)S(1)}, bf16[128,1536]{1,0:T(8,128)(2,1)S(1)}, u32[]{:S(2)}, u32[]{:S(2)}) collective-permute-start(bf16[128,1536]{1,0:T(8,128)(2,1)S(1)} %fusion.5), channel_id=1, source_target_pairs={{0,64},{64,128},{128,192},{192,0},{1,65},{65,129},{129,193},{193,1... | collective-permute-start | bytes 1179656 | tf_op jit(solution)/shard_map/ppermute | solution.py:371
  81.8 5.6 %collective-permute-start.16 = (bf16[4,128,1536]{2,1,0:T(8,128)(2,1)}, bf16[4,128,1536]{2,1,0:T(8,128)(2,1)}, u32[]{:S(2)}, u32[]{:S(2)}) collective-permute-start(bf16[4,128,1536]{2,1,0:T(8,128)(2,1)} %pad_maximum_fusion), channel_id=1, source_target_pairs={{0,1},{1,0},{2,3},{3,2},{4,5},{5,4},{6,7},{7,6},{8,9},{9,8},{10,11... | collective-permute-start | bytes 4718600 | tf_op jit(solution)/shard_map/ppermute | solution.py:375
  83.2 16.6 %all-to-all-start = ((bf16[8,128,384]{2,1,0:T(8,128)(2,1)}), bf16[8,128,384]{2,1,0:T(8,128)(2,1)}, u32[]{:S(2)}, u32[]{:S(2)}) async-start(bf16[8,128,384]{2,1,0:T(8,128)(2,1)} %get-tuple-element.34), calls=%async_computation | async-start | bytes 1572864 | tf_op jit(solution)/shard_map/all_to_all | solution.py:523
  101.5 18.0 %collective-permute-start.19 = (bf16[384,384]{1,0:T(8,128)(2,1)S(1)}, bf16[384,384]{1,0:T(8,128)(2,1)S(1)}, u32[]{:S(2)}, u32[]{:S(2)}) collective-permute-start(bf16[384,384]{1,0:T(8,128)(2,1)S(1)} %convolution_convert_fusion), channel_id=1, source_target_pairs={{0,6},{2,0},{4,2},{6,4},{1,7},{3,1},{5,3},{7,5},{8,14},{10,8},{12,... | collective-permute-start | bytes 884744 | tf_op jit(solution)/shard_map/ppermute | solution.py:371
  106.0 13.6 %collective-permute-start.18 = (bf16[384,384]{1,0:T(8,128)(2,1)S(1)}, bf16[384,384]{1,0:T(8,128)(2,1)S(1)}, u32[]{:S(2)}, u32[]{:S(2)}) collective-permute-start(bf16[384,384]{1,0:T(8,128)(2,1)S(1)} %convolution_convert_fusion.1), channel_id=1, source_target_pairs={{0,2},{2,4},{4,6},{6,0},{1,3},{3,5},{5,7},{7,1},{8,10},{10,12},{12... | collective-permute-start | bytes 884744 | tf_op jit(solution)/shard_map/ppermute | solution.py:371
  107.8 11.7 %collective-permute-start.17 = (bf16[384,384]{1,0:T(8,128)(2,1)S(1)}, bf16[384,384]{1,0:T(8,128)(2,1)S(1)}, u32[]{:S(2)}, u32[]{:S(2)}) collective-permute-start(bf16[384,384]{1,0:T(8,128)(2,1)S(1)} %convolution_convert_fusion.2), channel_id=1, source_target_pairs={{0,4},{2,6},{4,0},{6,2},{1,5},{3,7},{5,1},{7,3},{8,12},{10,14},{12... | collective-permute-start | bytes 884744 | tf_op jit(solution)/shard_map/ppermute | solution.py:371
  109.8 33.8 %collective-permute-start.11 = (bf16[64,1536]{1,0:T(8,128)(2,1)}, bf16[64,1536]{1,0:T(8,128)(2,1)}, u32[]{:S(2)}, u32[]{:S(2)}) collective-permute-start(bf16[64,1536]{1,0:T(8,128)(2,1)} %get-tuple-element.42), channel_id=1, source_target_pairs={{0,8},{8,16},{16,24},{24,32},{32,40},{40,48},{48,56},{56,64},{64,7... | collective-permute-start | bytes 589832 | tf_op jit(solution)/shard_map/ppermute | solution.py:24
  114.0 29.6 %collective-permute-start.12 = (bf16[64,1536]{1,0:T(8,128)(2,1)}, bf16[64,1536]{1,0:T(8,128)(2,1)}, u32[]{:S(2)}, u32[]{:S(2)}) collective-permute-start(bf16[64,1536]{1,0:T(8,128)(2,1)} %get-tuple-element.41), channel_id=1, source_target_pairs={{8,0},{16,8},{24,16},{32,24},{40,32},{48,40},{56,48},{64,56},{72,6... | collective-permute-start | bytes 589832 | tf_op jit(solution)/shard_map/ppermute | solution.py:24
  120.6 28.1 %all-to-all-start.1 = ((bf16[64,6,384]{2,1,0:T(8,128)(2,1)}), bf16[64,6,384]{2,1,0:T(8,128)(2,1)S(1)}, u32[]{:S(2)}, u32[]{:S(2)}) async-start(bf16[64,6,384]{2,1,0:T(8,128)(2,1)} %reshape.132), calls=%async_computation.1 | async-start | bytes 786432 | tf_op jit(solution)/shard_map/all_to_all | solution.py:475
  (20 other events, 135.7 us)

commit v4 on v3

--- a/solution.py
+++ b/solution.py
@@ -375,12 +375,6 @@
     return lax.ppermute(value, "c", [(0, 1), (1, 0)])
 
 
-def weight_blocks(w_in):
-    half = w_in.shape[0] // 2
-    below, above = ring(w_in, "y", 1), ring(w_in, "y", -1)
-    return below, above, [ring(below[:half], "y", 1), ring(above[half:], "y", -1)]
-
-
 def exchange_edges(rows_in, cot_rows, bounds_row, device, edge):
     rows, width = rows_in.shape
     halo = 2 * edge
@@ -392,30 +386,44 @@
     last_rows = lax.dynamic_slice_in_dim(padded, load, sent, 0)
     upwards = jnp.concatenate([rows_in[rows - halo :], last_rows], axis=0)
     downwards = jnp.concatenate([own[:sent], rows_in[:halo]], axis=0)
-    return own, passed_along(upwards, SEQ, 1), passed_along(downwards, SEQ, -1)
-
-
-def upstream_window(own, from_prev, from_next, bounds_row, device, rows, edge):
+    came = sent + halo
+    first = rows * device - edge - (bounds_row[device] - came)
+    beside = jnp.zeros((came, width), own.dtype)
+    own_window = lax.dynamic_slice_in_dim(
+        jnp.concatenate([beside, own, beside], axis=0), first, rows + 2 * edge, 0
+    )
+    return passed_along(upwards, SEQ, 1), passed_along(downwards, SEQ, -1), own_window, first, load
+
+
+def upstream_window(own_window, from_prev, from_next, first, load):
     came, width = from_prev.shape
-    start_row = bounds_row[device]
-    load = bounds_row[device + 1] - start_row
-    joined = jnp.concatenate([from_prev, own, jnp.zeros((came, width), own.dtype)], axis=0)
-    joined = lax.dynamic_update_slice_in_dim(joined, from_next, came + load, 0)
-    first = rows * device - edge - (start_row - came)
-    return lax.dynamic_slice_in_dim(joined, first, rows + 2 * edge, 0)
-
-
-def owner_slots(out_rows, bounds_row, device):
+    wide = own_window.shape[0]
+    most = 2 * wide
+    behind = jnp.concatenate([from_prev, jnp.zeros((most - came, width), from_prev.dtype)], axis=0)
+    before = 3 * came
+    ahead = jnp.concatenate(
+        [
+            jnp.zeros((before, width), from_next.dtype),
+            from_next,
+            jnp.zeros((most - came, width), from_next.dtype),
+        ],
+        axis=0,
+    )
+    return (
+        lax.dynamic_slice_in_dim(behind, first, wide, 0)
+        + own_window
+        + lax.dynamic_slice_in_dim(ahead, first - came - load + before, wide, 0)
+    )
+
+
+def owner_slots(out_rows, from_prev, from_next, bounds_row, device):
     rows, width = out_rows.shape
-    half = rows // 2
-    from_prev = passed_along(out_rows[half:], SEQ, 1)
-    from_next = passed_along(out_rows[:half], SEQ, -1)
     start_row = bounds_row[device]
     load = bounds_row[device + 1] - start_row
     joined = jnp.concatenate(
         [from_prev, out_rows, from_next, jnp.zeros((rows, width), out_rows.dtype)], axis=0
     )
-    placed = lax.dynamic_slice_in_dim(joined, start_row - (rows * device - half), 2 * rows, 0)
+    placed = lax.dynamic_slice_in_dim(joined, start_row - (rows * device - rows // 2), 2 * rows, 0)
     slot = jnp.arange(2 * rows, dtype=jnp.int32)[:, None]
     return jnp.where(slot < load, placed, jnp.zeros((), placed.dtype))
 
@@ -491,17 +499,21 @@
     chip = lax.axis_index("y")
     chips = lax.axis_size("y")
     core = lax.axis_index("c").reshape(1)
-    below, above, far = weight_blocks(w_in)
     own_other = other_core(w_in)
-    own, from_prev, from_next = exchange_edges(
+    below, above = ring(w_in, "y", 1), ring(w_in, "y", -1)
+    from_prev, from_next, own_window, first, load = exchange_edges(
         rows_in, cotangent[0], bounds_row, device, edge
     )
-    upstream = upstream_window(own, from_prev, from_next, bounds_row, device, rows, edge)
     rows_late, own_other = lax.optimization_barrier((rows_in, own_other))
+    hidden_sent = by_receiver(normalize_rows(rows_late)[0].astype(bf16))
+    below, hidden_sent, from_prev, from_next = lax.optimization_barrier(
+        (below, hidden_sent, from_prev, from_next)
+    )
+    upstream = upstream_window(own_window, from_prev, from_next, first, load)
+    half = below.shape[0] // 2
+    far = [ring(below[:half], "y", 1), ring(above[half:], "y", -1)]
     near = [w_in, own_other, below, other_core(below), above, other_core(above)]
     order = jnp.stack([chip, (chip + chips - 1) % chips, (chip + 1) % chips, (chip + 2) % chips])
-
-    hidden_sent = by_receiver(normalize_rows(rows_late)[0].astype(bf16))
     blocks = hidden_blocks(hidden_sent)
 
     bounds = [rows * device - edge, jnp.int32(frame_total)]
@@ -512,19 +524,21 @@
     bounds = jnp.stack(bounds).astype(jnp.int32)
 
     hidden, part = run_part(order[:3], core, from_prev, rows_in, from_next, near, halo)
-    far, corner = lax.optimization_barrier((far, part[:8, :LANES]))
+    far, corner, blocks[1] = lax.optimization_barrier((far, part[:8, :LANES], blocks[1]))
     far = far + [other_core(piece) for piece in far]
     shares = lax.axis_size(("x", "c"))
     output, d_mixed, d_shares = run_main(
         bounds, order, core, corner, hidden, part, upstream, kernel, far, rows, edge, shares
     )
-    blocks, d_shares = lax.optimization_barrier((blocks, d_shares))
+    blocks, output = lax.optimization_barrier((blocks, output))
     hidden_all = all_hidden(blocks)
     mixed_share = lax.all_to_all(d_shares, ("x", "c"), 0, 0, tiled=True)
+    out_prev = passed_along(output[rows // 2 :], SEQ, 1)
+    out_next = passed_along(output[: rows // 2], SEQ, -1)
     mixed_share = mixed_share.reshape(shares * rows, -1)
     frame_grad = run_frame(order, core, rows_in, d_mixed, near + far)
+    owner_output = owner_slots(output, out_prev, out_next, bounds_row, device)
     w_grad = weight_gradient(hidden_all, mixed_share, frame_total, chips * CHIP)
-    owner_output = owner_slots(output, bounds_row, device)
     return (owner_output[None], frame_grad[None], w_grad)
 
 

time: 150 us -> 148 us (0.987)
  waiting for transfers between devices: 28.1 us -> 24.1 us
  local copies, waits for them, and re-layouts: 10.4 us -> 12.1 us
    ppermute x10, waiting for transfers between devices: 16.9 us -> 6.16 us  [ring(): lax.ppermute(value, axis, [(i, (i + steps) % count) for i in range(count)])]
    ppermute x4, waiting for transfers between devices: 0.01 us -> 6.76 us  [passed_along(): lax.ppermute(value, axis, [(source, source + steps) for source in range(i...]
    concatenate x1 -> x0, other arithmetic: 2.82 us -> none  [upstream_window(): jnp.concatenate([from_prev, own, jnp.zeros((came, width), own.dtype)], ax...]
    dynamic_update_slice x1 -> x0, local copies, waits for them, and re-layouts: 2.78 us -> none  [upstream_window(): joined = lax.dynamic_update_slice_in_dim(joined, from_next, came + load, 0)]
    unnamed x44 -> x36, local copies, waits for them, and re-layouts: 0.81 us -> 3.59 us
    add x0 -> x1, other arithmetic: none -> 2.31 us  [upstream_window(): lax.dynamic_slice_in_dim(behind, first, wide, 0) + own_window]
    slice x4, local copies, waits for them, and re-layouts: 1.51 us -> 3.25 us  [the longest x2 1.75 us: on_device(): far = [ring(below[:half], 'y', 1), ring(above[half:], 'y', -1)]]
  transfers between devices with their start and end apart: 22 -> 22, of which waited for: 6 -> 7; matrix products, arithmetic and copies ran while one was open for 19% -> 19% of each run, Pallas kernels for 23% -> 23%
where the time goes in v4:
time: 148 us
  starting transfers between devices  48.4 us (33%)
  Pallas kernels  34.4 us (23%)
  waiting for transfers between devices  24.1 us (16%)
  other arithmetic  13.3 us (9%)
  local copies, waits for them, and re-layouts  12.1 us (8%)
  matrix products  9.78 us (7%)
  between operations  5.68 us (4%)
    pallas_call x1, Pallas kernels, run_main(): pl.pallas_call(functools.partial(main_kernel, rows, edge), out_shape=(jax...  15.4 us
    ppermute x10, starting transfers between devices, ring(): lax.ppermute(value, axis, [(i, (i + steps) % count) for i in range(count)])  15.1 us
    all_to_all x1, starting transfers between devices, weight_gradient(): pieces = lax.all_to_all(pieces, last, 0, 0, tiled=True).astype(f32)  13.6 us
    pallas_call x1, Pallas kernels, run_frame(): pl.pallas_call(frame_kernel, out_shape=jax.ShapeDtypeStruct((rows, width)...  10.1 us
    pallas_call x1, Pallas kernels, run_part(): pl.pallas_call(functools.partial(part_kernel, halo), out_shape=(jax.Shape...  8.9 us
    all_to_all x1, waiting for transfers between devices, on_device(): mixed_share = lax.all_to_all(d_shares, ('x', 'c'), 0, 0, tiled=True)  8.63 us
    ppermute x4, starting transfers between devices, passed_along(): lax.ppermute(value, axis, [(source, source + steps) for source in range(i...  8.1 us
    ppermute x6, starting transfers between devices, other_core(): return lax.ppermute(value, 'c', [(0, 1), (1, 0)])  7.47 us
  transfers between devices with their start and end apart: 22, of which 7 were waited for; matrix products, arithmetic and copies ran while one was open for 19% of the time, Pallas kernels for 23%

profile of v4, /device:TPU:1, one launch (start us, length us, event | category | flops | bytes accessed | tf_op | source)
XLA Modules:
  0.0 147.7 jit_solution(7219787546957597334)
XLA Ops:
  0.6 2.2 %collective-permute-start = (bf16[192,3072]{1,0:T(8,128)(2,1)}, bf16[192,3072]{1,0:T(8,128)(2,1)S(1)}, u32[]{:S(2)}, u32[]{:S(2)}) collective-permute-start(bf16[192,3072]{1,0:T(8,128)(2,1)} %rest_0_.3), channel_id=1, source_target_pairs={{0,2},{2,4},{4,6},{6,0},{1,3},{3,5},{5,7},{7,1},{8,10},{10,12},{12... | collective-permute-start | bytes 3538952 | tf_op jit(solution)/shard_map/ppermute | solution.py:371
  4.1 2.9 %collective-permute-start.6 = (bf16[192,3072]{1,0:T(8,128)(2,1)}, bf16[192,3072]{1,0:T(8,128)(2,1)S(1)}, u32[]{:S(2)}, u32[]{:S(2)}) collective-permute-start(bf16[192,3072]{1,0:T(8,128)(2,1)} %rest_0_.3), channel_id=1, source_target_pairs={{0,6},{2,0},{4,2},{6,4},{1,7},{3,1},{5,3},{7,5},{8,14},{10,8},{12,... | collective-permute-start | bytes 3538952 | tf_op jit(solution)/shard_map/ppermute | solution.py:371
  9.6 2.1 %bitcast_select_fusion = bf16[256,1536]{1,0:T(8,128)(2,1)} fusion(bf16[1,256,1536]{2,1,0:T(8,128)(2,1)} %param.11, pred[256]{0:T(512)(128)(4,1)S(1)} %iota_compare_fusion.4), kind=kLoop, calls=%fused_computation.38 | loop fusion | flops 393216 | bytes 1573120 | tf_op jit(solution)/shard_map/jit(_where)/select_n | solution.py:384
  12.9 1.8 %collective-permute-start.2 = (bf16[112,1536]{1,0:T(8,128)(2,1)S(1)}, bf16[112,1536]{1,0:T(8,128)(2,1)S(1)}, u32[]{:S(2)}, u32[]{:S(2)}) collective-permute-start(bf16[112,1536]{1,0:T(8,128)(2,1)S(1)} %pad_maximum_fusion.1), channel_id=1, source_target_pairs={{0,8},{8,16},{16,24},{24,32},{32,40},{40,48},{48,56},{56,64},{64,7... | collective-permute-start | bytes 1032200 | tf_op jit(solution)/shard_map/ppermute | solution.py:24
  16.6 2.8 %fusion.5 = bf16[128,1536]{1,0:T(8,128)(2,1)} fusion(s32[1536]{0:T(1024)S(1)} %fusion.40, bf16[128,1536]{1,0:T(8,128)(2,1)S(1)} %bitcast.43, f32[128]{0:T(128)S(1)} %add_rsqrt_fusion, f32[128]{0:T(128)S(1)} %broadcast_multiply_fusion.1), kind=kOutput, calls=%fused_computation.10 | convolution fusion | flops 607322112 | bytes 793600 | tf_op jit(solution)/shard_map/dot_general | solution.py:441
  19.4 2.5 %collective-permute-done.2.prev_ref = bf16[112,1536]{1,0:T(8,128)(2,1)S(1)} collective-permute-done((bf16[112,1536]{1,0:T(8,128)(2,1)S(1)}, bf16[112,1536]{1,0:T(8,128)(2,1)S(1)}, u32[]{:S(2)}, u32[]{:S(2)}) %collective-permute-start.2) | collective-permute-done | bytes 344096 | tf_op jit(solution)/shard_map/ppermute | solution.py:24
  21.9 4.2 %collective-permute-done.3.next_ref = bf16[112,1536]{1,0:T(8,128)(2,1)S(1)} collective-permute-done((bf16[112,1536]{1,0:T(8,128)(2,1)S(1)}, bf16[112,1536]{1,0:T(8,128)(2,1)S(1)}, u32[]{:S(2)}, u32[]{:S(2)}) %collective-permute-start.3) | collective-permute-done | bytes 344096 | tf_op jit(solution)/shard_map/ppermute | solution.py:24
  26.1 2.0 %collective-permute-done.rest_2_ = bf16[192,3072]{1,0:T(8,128)(2,1)S(1)} collective-permute-done((bf16[192,3072]{1,0:T(8,128)(2,1)}, bf16[192,3072]{1,0:T(8,128)(2,1)S(1)}, u32[]{:S(2)}, u32[]{:S(2)}) %collective-permute-start) | collective-permute-done | bytes 1179680 | tf_op jit(solution)/shard_map/ppermute | solution.py:371
  28.2 3.3 %collective-permute-start.8 = (bf16[192,3072]{1,0:T(8,128)(2,1)S(1)}, bf16[192,3072]{1,0:T(8,128)(2,1)}, u32[]{:S(2)}, u32[]{:S(2)}) collective-permute-start(bf16[192,3072]{1,0:T(8,128)(2,1)S(1)} %collective-permute-done.rest_2_), channel_id=1, source_target_pairs={{0,1},{1,0},{2,3},{3,2},{4,5},{5,4},{6,7},{7,6},{8,9},{9,8},{10,11... | collective-permute-start | bytes 3538952 | tf_op jit(solution)/shard_map/ppermute | solution.py:375
  35.5 3.0 %collective-permute-start.7 = (bf16[96,3072]{1,0:T(8,128)(2,1)}, bf16[96,3072]{1,0:T(8,128)(2,1)}, u32[]{:S(2)}, u32[]{:S(2)}) collective-permute-start(bf16[96,3072]{1,0:T(8,128)(2,1)} %slice.55), channel_id=1, source_target_pairs={{0,6},{2,0},{4,2},{6,4},{1,7},{3,1},{5,3},{7,5},{8,14},{10,8},{12,... | collective-permute-start | bytes 1769480 | tf_op jit(solution)/shard_map/ppermute | solution.py:371
  41.6 8.9 %forward_part.1 = (bf16[192,1536]{1,0:T(8,128)(2,1)S(1)}, f32[192,3072]{1,0:T(8,128)}) custom-call(s32[3]{0:T(128)S(1)} %pad_add_fusion.at_ref, s32[1]{0:T(128)} %bitcast.9.core_ref, bf16[112,1536]{1,0:T(8,128)(2,1)S(1)} %collective-permute-done.2.prev_ref, bf16[128,1536]{1,0:T(8,128)(2,1)S(1)} %bitcast.44, ...), custom_call_target="tpu_custom_call" | custom-call | flops 2000000000 | bytes 8000000 | tf_op jit(solution)/shard_map/forward_part/pallas_call | solution.py:303
  58.1 2.3 %fusion.21.up_ref = bf16[160,1536]{1,0:T(8,128)(2,1)S(1)} fusion(s32[]{:T(128)S(6)} %select_n.149, bf16[112,1536]{1,0:T(8,128)(2,1)S(1)} %collective-permute-done.2.prev_ref, s32[]{:T(128)S(6)} %select_n.150, bf16[112,1536]{1,0:T(8,128)(2,1)S(1)} %broadcast_in_dim.40, bf16[256,1536]{1,0:T(8,128)(2,1)} %bitcast_select_fusion, s32[]{:T(128)S(6)} %select_n.151, ...), kind=kLoop, calls=%fused_computation.46 | loop fusion | flops 3440640 | bytes 2310796 | tf_op jit(solution)/shard_map/add | solution.py:413
  62.0 15.4 %main.1 = (bf16[128,1536]{1,0:T(8,128)(2,1)S(1)}, bf16[128,3072]{1,0:T(8,128)(2,1)S(1)}, bf16[8,128,384]{2,1,0:T(8,128)(2,1)}) custom-call(s32[5]{0:T(128)S(1)} %stack.60.bounds_ref, s32[4]{0:T(128)S(1)} %pad_add_fusion.1.at_ref, s32[1]{0:T(128)} %bitcast.9.core_ref, f32[8,128]{1,0:T(8,128)S(1)} %slice.48.corner_ref, bf16[192,1536]{1,0:T(8,128)(2,1)S(1)} %copy-done.10, ...), custom_call_target="tpu_custom_call" | custom-call | flops 6000000000 | bytes 12000000 | tf_op jit(solution)/shard_map/main/pallas_call | solution.py:326
  80.9 4.2 %all-to-all-start = ((bf16[8,128,384]{2,1,0:T(8,128)(2,1)}), bf16[8,128,384]{2,1,0:T(8,128)(2,1)}, u32[]{:S(2)}, u32[]{:S(2)}) async-start(bf16[8,128,384]{2,1,0:T(8,128)(2,1)} %get-tuple-element.44), calls=%async_computation | async-start | bytes 1572864 | tf_op jit(solution)/shard_map/all_to_all | solution.py:535
  88.8 8.6 %all-to-all-done = bf16[8,128,384]{2,1,0:T(8,128)(2,1)} async-done(((bf16[8,128,384]{2,1,0:T(8,128)(2,1)}), bf16[8,128,384]{2,1,0:T(8,128)(2,1)}, u32[]{:S(2)}, u32[]{:S(2)}) %all-to-all-start) | async-done | bytes 786464 | tf_op jit(solution)/shard_map/all_to_all | solution.py:535
  99.2 2.6 %collective-permute-start.19 = (bf16[384,384]{1,0:T(8,128)(2,1)S(1)}, bf16[384,384]{1,0:T(8,128)(2,1)S(1)}, u32[]{:S(2)}, u32[]{:S(2)}) collective-permute-start(bf16[384,384]{1,0:T(8,128)(2,1)S(1)} %convolution_convert_fusion), channel_id=1, source_target_pairs={{0,6},{2,0},{4,2},{6,4},{1,7},{3,1},{5,3},{7,5},{8,14},{10,8},{12,... | collective-permute-start | bytes 884744 | tf_op jit(solution)/shard_map/ppermute | solution.py:371
  101.8 1.7 %convolution_convert_fusion.1 = bf16[384,384]{1,0:T(8,128)(2,1)S(1)} fusion(bf16[1024,384]{1,0:T(8,128)(2,1)} %bitcast.24, bf16[1024,1536]{1,0:T(8,128)(2,1)S(1)} %bitcast.46, s32[]{:T(128)S(6)} %select_n.162), kind=kOutput, calls=%fused_computation.19 | convolution fusion | flops 302137344 | bytes 1867780 | tf_op jit(solution)/shard_map/dot_general | solution.py:471
  103.6 1.7 %convolution_convert_fusion.2 = bf16[384,384]{1,0:T(8,128)(2,1)S(1)} fusion(bf16[1024,384]{1,0:T(8,128)(2,1)} %bitcast.24, bf16[1024,1536]{1,0:T(8,128)(2,1)S(1)} %bitcast.47, s32[]{:T(128)S(6)} %select_n.161), kind=kOutput, calls=%fused_computation.20 | convolution fusion | flops 302137344 | bytes 1867780 | tf_op jit(solution)/shard_map/dot_general | solution.py:471
  107.6 3.7 %collective-permute-start.14 = (bf16[64,1536]{1,0:T(8,128)(2,1)}, bf16[64,1536]{1,0:T(8,128)(2,1)}, u32[]{:S(2)}, u32[]{:S(2)}) collective-permute-start(bf16[64,1536]{1,0:T(8,128)(2,1)} %get-tuple-element.52), channel_id=1, source_target_pairs={{0,8},{8,16},{16,24},{24,32},{32,40},{40,48},{48,56},{56,64},{64,7... | collective-permute-start | bytes 589832 | tf_op jit(solution)/shard_map/ppermute | solution.py:24
  114.3 2.9 %collective-permute-done.17 = bf16[384,384]{1,0:T(8,128)(2,1)S(1)} collective-permute-done((bf16[384,384]{1,0:T(8,128)(2,1)S(1)}, bf16[384,384]{1,0:T(8,128)(2,1)S(1)}, u32[]{:S(2)}, u32[]{:S(2)}) %collective-permute-start.17) | collective-permute-done | bytes 294944 | tf_op jit(solution)/shard_map/ppermute | solution.py:371
  118.3 13.6 %all-to-all-start.1 = ((bf16[64,6,384]{2,1,0:T(8,128)(2,1)}), bf16[64,6,384]{2,1,0:T(8,128)(2,1)S(1)}, u32[]{:S(2)}, u32[]{:S(2)}) async-start(bf16[64,6,384]{2,1,0:T(8,128)(2,1)} %reshape.132), calls=%async_computation.1 | async-start | bytes 786432 | tf_op jit(solution)/shard_map/all_to_all | solution.py:483
  131.9 10.1 %frame_back.1 = bf16[128,1536]{1,0:T(8,128)(2,1)} custom-call(s32[4]{0:T(128)} %copy-done.7, s32[1]{0:T(128)} %bitcast.9.core_ref, bf16[128,1536]{1,0:T(8,128)(2,1)} %bitcast.40, bf16[128,3072]{1,0:T(8,128)(2,1)} %copy-done.4, bf16[192,3072]{1,0:T(8,128)(2,1)} %rest_0_.3, bf16[192,3072]{1,0:T(8,128)(2,1)} %collective-permute-done.1.rest_1_, ...), custom_call_target="tpu_custom_call" | custom-call | flops 2000000000 | bytes 11000000 | tf_op jit(solution)/shard_map/frame_back/pallas_call | solution.py:353
  142.0 2.4 %fusion.14 = bf16[1,256,1536]{2,1,0:T(8,128)(2,1)} fusion(s32[]{:T(128)S(6)} %select_n.152, bf16[64,1536]{1,0:T(8,128)(2,1)} %collective-permute-done.14, bf16[128,1536]{1,0:T(8,128)(2,1)S(1)} %get-tuple-element.38, bf16[64,1536]{1,0:T(8,128)(2,1)} %collective-permute-done.15, pred[256]{0:T(512)(128)(4,1)S(1)} %iota_compare_fusion.4, ...), kind=kLoop, calls=%fused_computation.36 | loop fusion | flops 3538944 | bytes 1573636 | tf_op jit(solution)/shard_map/broadcast_in_dim | solution.py:542
  144.5 2.5 %all-to-all-done.1 = bf16[64,6,384]{2,1,0:T(8,128)(2,1)S(1)} async-done(((bf16[64,6,384]{2,1,0:T(8,128)(2,1)}), bf16[64,6,384]{2,1,0:T(8,128)(2,1)S(1)}, u32[]{:S(2)}, u32[]{:S(2)}) %all-to-all-start.1) | async-done | bytes 294944 | tf_op jit(solution)/shard_map/all_to_all | solution.py:483
  (101 shorter events, 34.4 us)
Async XLA Ops:
  0.6 27.5 %collective-permute-start = (bf16[192,3072]{1,0:T(8,128)(2,1)}, bf16[192,3072]{1,0:T(8,128)(2,1)S(1)}, u32[]{:S(2)}, u32[]{:S(2)}) collective-permute-start(bf16[192,3072]{1,0:T(8,128)(2,1)} %rest_0_.3), channel_id=1, source_target_pairs={{0,2},{2,4},{4,6},{6,0},{1,3},{3,5},{5,7},{7,1},{8,10},{10,12},{12... | collective-permute-start | bytes 3538952 | tf_op jit(solution)/shard_map/ppermute | solution.py:371
  2.8 13.3 %collective-permute-start.1 = (bf16[192,3072]{1,0:T(8,128)(2,1)}, bf16[192,3072]{1,0:T(8,128)(2,1)}, u32[]{:S(2)}, u32[]{:S(2)}) collective-permute-start(bf16[192,3072]{1,0:T(8,128)(2,1)} %rest_0_.3), channel_id=1, source_target_pairs={{0,1},{1,0},{2,3},{3,2},{4,5},{5,4},{6,7},{7,6},{8,9},{9,8},{10,11... | collective-permute-start | bytes 3538952 | tf_op jit(solution)/shard_map/ppermute | solution.py:375
  4.1 28.6 %collective-permute-start.6 = (bf16[192,3072]{1,0:T(8,128)(2,1)}, bf16[192,3072]{1,0:T(8,128)(2,1)S(1)}, u32[]{:S(2)}, u32[]{:S(2)}) collective-permute-start(bf16[192,3072]{1,0:T(8,128)(2,1)} %rest_0_.3), channel_id=1, source_target_pairs={{0,6},{2,0},{4,2},{6,4},{1,7},{3,1},{5,3},{7,5},{8,14},{10,8},{12,... | collective-permute-start | bytes 3538952 | tf_op jit(solution)/shard_map/ppermute | solution.py:371
  12.9 9.0 %collective-permute-start.2 = (bf16[112,1536]{1,0:T(8,128)(2,1)S(1)}, bf16[112,1536]{1,0:T(8,128)(2,1)S(1)}, u32[]{:S(2)}, u32[]{:S(2)}) collective-permute-start(bf16[112,1536]{1,0:T(8,128)(2,1)S(1)} %pad_maximum_fusion.1), channel_id=1, source_target_pairs={{0,8},{8,16},{16,24},{24,32},{32,40},{40,48},{48,56},{56,64},{64,7... | collective-permute-start | bytes 1032200 | tf_op jit(solution)/shard_map/ppermute | solution.py:24
  14.8 11.3 %collective-permute-start.3 = (bf16[112,1536]{1,0:T(8,128)(2,1)S(1)}, bf16[112,1536]{1,0:T(8,128)(2,1)S(1)}, u32[]{:S(2)}, u32[]{:S(2)}) collective-permute-start(bf16[112,1536]{1,0:T(8,128)(2,1)S(1)} %pad_maximum_fusion.2), channel_id=1, source_target_pairs={{8,0},{16,8},{24,16},{32,24},{40,32},{48,40},{56,48},{64,56},{72,6... | collective-permute-start | bytes 1032200 | tf_op jit(solution)/shard_map/ppermute | solution.py:24
  28.1 22.4 %copy-start.1 = (bf16[192,3072]{1,0:T(8,128)(2,1)}, bf16[192,3072]{1,0:T(8,128)(2,1)S(1)}, u32[]{:S(2)}) copy-start(bf16[192,3072]{1,0:T(8,128)(2,1)S(1)} %collective-permute-done.rest_2_) | copy-start | bytes 3538948
  28.2 12.2 %collective-permute-start.8 = (bf16[192,3072]{1,0:T(8,128)(2,1)S(1)}, bf16[192,3072]{1,0:T(8,128)(2,1)}, u32[]{:S(2)}, u32[]{:S(2)}) collective-permute-start(bf16[192,3072]{1,0:T(8,128)(2,1)S(1)} %collective-permute-done.rest_2_), channel_id=1, source_target_pairs={{0,1},{1,0},{2,3},{3,2},{4,5},{5,4},{6,7},{7,6},{8,9},{9,8},{10,11... | collective-permute-start | bytes 3538952 | tf_op jit(solution)/shard_map/ppermute | solution.py:375
  32.6 7.7 %collective-permute-start.9 = (bf16[192,3072]{1,0:T(8,128)(2,1)S(1)}, bf16[192,3072]{1,0:T(8,128)(2,1)}, u32[]{:S(2)}, u32[]{:S(2)}) collective-permute-start(bf16[192,3072]{1,0:T(8,128)(2,1)S(1)} %collective-permute-done.6.rest_4_), channel_id=1, source_target_pairs={{0,1},{1,0},{2,3},{3,2},{4,5},{5,4},{6,7},{7,6},{8,9},{9,8},{10,11... | collective-permute-start | bytes 3538952 | tf_op jit(solution)/shard_map/ppermute | solution.py:375
  34.3 17.8 %collective-permute-start.5 = (bf16[96,3072]{1,0:T(8,128)(2,1)}, bf16[96,3072]{1,0:T(8,128)(2,1)}, u32[]{:S(2)}, u32[]{:S(2)}) collective-permute-start(bf16[96,3072]{1,0:T(8,128)(2,1)} %slice.46), channel_id=1, source_target_pairs={{0,2},{2,4},{4,6},{6,0},{1,3},{3,5},{5,7},{7,1},{8,10},{10,12},{12... | collective-permute-start | bytes 1769480 | tf_op jit(solution)/shard_map/ppermute | solution.py:371
  35.5 16.6 %collective-permute-start.7 = (bf16[96,3072]{1,0:T(8,128)(2,1)}, bf16[96,3072]{1,0:T(8,128)(2,1)}, u32[]{:S(2)}, u32[]{:S(2)}) collective-permute-start(bf16[96,3072]{1,0:T(8,128)(2,1)} %slice.55), channel_id=1, source_target_pairs={{0,6},{2,0},{4,2},{6,4},{1,7},{3,1},{5,3},{7,5},{8,14},{10,8},{12,... | collective-permute-start | bytes 1769480 | tf_op jit(solution)/shard_map/ppermute | solution.py:371
  38.5 13.6 %collective-permute-start.10 = (bf16[128,1536]{1,0:T(8,128)(2,1)}, bf16[128,1536]{1,0:T(8,128)(2,1)S(1)}, u32[]{:S(2)}, u32[]{:S(2)}) collective-permute-start(bf16[128,1536]{1,0:T(8,128)(2,1)} %fusion.5), channel_id=1, source_target_pairs={{0,128},{64,192},{128,0},{192,64},{1,129},{65,193},{129,1},{193,65... | collective-permute-start | bytes 1179656 | tf_op jit(solution)/shard_map/ppermute | solution.py:371
  52.1 8.3 %collective-permute-start.12 = (bf16[96,3072]{1,0:T(8,128)(2,1)}, bf16[96,3072]{1,0:T(8,128)(2,1)S(1)}, u32[]{:S(2)}, u32[]{:S(2)}) collective-permute-start(bf16[96,3072]{1,0:T(8,128)(2,1)} %collective-permute-done.5.rest_0_.rest_6_), channel_id=1, source_target_pairs={{0,1},{1,0},{2,3},{3,2},{4,5},{5,4},{6,7},{7,6},{8,9},{9,8},{10,11... | collective-permute-start | bytes 1769480 | tf_op jit(solution)/shard_map/ppermute | solution.py:375
  53.1 7.4 %collective-permute-start.13 = (bf16[96,3072]{1,0:T(8,128)(2,1)}, bf16[96,3072]{1,0:T(8,128)(2,1)S(1)}, u32[]{:S(2)}, u32[]{:S(2)}) collective-permute-start(bf16[96,3072]{1,0:T(8,128)(2,1)} %collective-permute-done.7.rest_1_.rest_7_), channel_id=1, source_target_pairs={{0,1},{1,0},{2,3},{3,2},{4,5},{5,4},{6,7},{7,6},{8,9},{9,8},{10,11... | collective-permute-start | bytes 1769480 | tf_op jit(solution)/shard_map/ppermute | solution.py:375
  53.3 24.1 %copy-start.7 = (s32[4]{0:T(128)}, s32[4]{0:T(128)S(1)}, u32[]{:S(2)}) copy-start(s32[4]{0:T(128)S(1)} %pad_add_fusion.1.at_ref) | copy-start | bytes 52
  56.6 20.8 %collective-permute-start.4 = (bf16[128,1536]{1,0:T(8,128)(2,1)}, bf16[128,1536]{1,0:T(8,128)(2,1)S(1)}, u32[]{:S(2)}, u32[]{:S(2)}) collective-permute-start(bf16[128,1536]{1,0:T(8,128)(2,1)} %fusion.5), channel_id=1, source_target_pairs={{0,192},{64,0},{128,64},{192,128},{1,193},{65,1},{129,65},{193,129... | collective-permute-start | bytes 1179656 | tf_op jit(solution)/shard_map/ppermute | solution.py:371
  57.5 19.9 %collective-permute-start.11 = (bf16[128,1536]{1,0:T(8,128)(2,1)}, bf16[128,1536]{1,0:T(8,128)(2,1)S(1)}, u32[]{:S(2)}, u32[]{:S(2)}) collective-permute-start(bf16[128,1536]{1,0:T(8,128)(2,1)} %fusion.5), channel_id=1, source_target_pairs={{0,64},{64,128},{128,192},{192,0},{1,65},{65,129},{129,193},{193,1... | collective-permute-start | bytes 1179656 | tf_op jit(solution)/shard_map/ppermute | solution.py:371
  78.9 6.1 %collective-permute-start.16 = (bf16[4,128,1536]{2,1,0:T(8,128)(2,1)}, bf16[4,128,1536]{2,1,0:T(8,128)(2,1)}, u32[]{:S(2)}, u32[]{:S(2)}) collective-permute-start(bf16[4,128,1536]{2,1,0:T(8,128)(2,1)} %pad_maximum_fusion), channel_id=1, source_target_pairs={{0,1},{1,0},{2,3},{3,2},{4,5},{5,4},{6,7},{7,6},{8,9},{9,8},{10,11... | collective-permute-start | bytes 4718600 | tf_op jit(solution)/shard_map/ppermute | solution.py:375
  80.9 16.5 %all-to-all-start = ((bf16[8,128,384]{2,1,0:T(8,128)(2,1)}), bf16[8,128,384]{2,1,0:T(8,128)(2,1)}, u32[]{:S(2)}, u32[]{:S(2)}) async-start(bf16[8,128,384]{2,1,0:T(8,128)(2,1)} %get-tuple-element.44), calls=%async_computation | async-start | bytes 1572864 | tf_op jit(solution)/shard_map/all_to_all | solution.py:535
  99.2 18.2 %collective-permute-start.19 = (bf16[384,384]{1,0:T(8,128)(2,1)S(1)}, bf16[384,384]{1,0:T(8,128)(2,1)S(1)}, u32[]{:S(2)}, u32[]{:S(2)}) collective-permute-start(bf16[384,384]{1,0:T(8,128)(2,1)S(1)} %convolution_convert_fusion), channel_id=1, source_target_pairs={{0,6},{2,0},{4,2},{6,4},{1,7},{3,1},{5,3},{7,5},{8,14},{10,8},{12,... | collective-permute-start | bytes 884744 | tf_op jit(solution)/shard_map/ppermute | solution.py:371
  103.5 13.8 %collective-permute-start.18 = (bf16[384,384]{1,0:T(8,128)(2,1)S(1)}, bf16[384,384]{1,0:T(8,128)(2,1)S(1)}, u32[]{:S(2)}, u32[]{:S(2)}) collective-permute-start(bf16[384,384]{1,0:T(8,128)(2,1)S(1)} %convolution_convert_fusion.1), channel_id=1, source_target_pairs={{0,2},{2,4},{4,6},{6,0},{1,3},{3,5},{5,7},{7,1},{8,10},{10,12},{12... | collective-permute-start | bytes 884744 | tf_op jit(solution)/shard_map/ppermute | solution.py:371
  105.4 11.9 %collective-permute-start.17 = (bf16[384,384]{1,0:T(8,128)(2,1)S(1)}, bf16[384,384]{1,0:T(8,128)(2,1)S(1)}, u32[]{:S(2)}, u32[]{:S(2)}) collective-permute-start(bf16[384,384]{1,0:T(8,128)(2,1)S(1)} %convolution_convert_fusion.2), channel_id=1, source_target_pairs={{0,4},{2,6},{4,0},{6,2},{1,5},{3,7},{5,1},{7,3},{8,12},{10,14},{12... | collective-permute-start | bytes 884744 | tf_op jit(solution)/shard_map/ppermute | solution.py:371
  107.6 34.4 %collective-permute-start.14 = (bf16[64,1536]{1,0:T(8,128)(2,1)}, bf16[64,1536]{1,0:T(8,128)(2,1)}, u32[]{:S(2)}, u32[]{:S(2)}) collective-permute-start(bf16[64,1536]{1,0:T(8,128)(2,1)} %get-tuple-element.52), channel_id=1, source_target_pairs={{0,8},{8,16},{16,24},{24,32},{32,40},{40,48},{48,56},{56,64},{64,7... | collective-permute-start | bytes 589832 | tf_op jit(solution)/shard_map/ppermute | solution.py:24
  111.3 30.7 %collective-permute-start.15 = (bf16[64,1536]{1,0:T(8,128)(2,1)}, bf16[64,1536]{1,0:T(8,128)(2,1)}, u32[]{:S(2)}, u32[]{:S(2)}) collective-permute-start(bf16[64,1536]{1,0:T(8,128)(2,1)} %get-tuple-element.51), channel_id=1, source_target_pairs={{8,0},{16,8},{24,16},{32,24},{40,32},{48,40},{56,48},{64,56},{72,6... | collective-permute-start | bytes 589832 | tf_op jit(solution)/shard_map/ppermute | solution.py:24
  118.3 28.6 %all-to-all-start.1 = ((bf16[64,6,384]{2,1,0:T(8,128)(2,1)}), bf16[64,6,384]{2,1,0:T(8,128)(2,1)S(1)}, u32[]{:S(2)}, u32[]{:S(2)}) async-start(bf16[64,6,384]{2,1,0:T(8,128)(2,1)} %reshape.132), calls=%async_computation.1 | async-start | bytes 786432 | tf_op jit(solution)/shard_map/all_to_all | solution.py:483
  (16 other events, 139.9 us)

commit v5 on v4

--- a/solution.py
+++ b/solution.py
@@ -309,7 +309,7 @@
         in_specs=[SMEM, SMEM, VMEM, VMEM, VMEM] + [ANY] * len(pieces),
         out_specs=(VMEM, VMEM),
         scratch_shapes=[
-            pltpu.VMEM((chips.shape[0], depth, mixed_width), bf16),
+            pltpu.VMEM((NEAR, depth, mixed_width), bf16),
             pltpu.SemaphoreType.DMA((len(pieces),)),
         ],
         compiler_params=limit(44),
@@ -504,27 +504,30 @@
     from_prev, from_next, own_window, first, load = exchange_edges(
         rows_in, cotangent[0], bounds_row, device, edge
     )
-    rows_late, own_other = lax.optimization_barrier((rows_in, own_other))
-    hidden_sent = by_receiver(normalize_rows(rows_late)[0].astype(bf16))
-    below, hidden_sent, from_prev, from_next = lax.optimization_barrier(
-        (below, hidden_sent, from_prev, from_next)
-    )
-    upstream = upstream_window(own_window, from_prev, from_next, first, load)
-    half = below.shape[0] // 2
-    far = [ring(below[:half], "y", 1), ring(above[half:], "y", -1)]
-    near = [w_in, own_other, below, other_core(below), above, other_core(above)]
-    order = jnp.stack([chip, (chip + chips - 1) % chips, (chip + 1) % chips, (chip + 2) % chips])
-    blocks = hidden_blocks(hidden_sent)
-
     bounds = [rows * device - edge, jnp.int32(frame_total)]
     utt_end = jnp.int32(0)
     for utt in range(lengths.shape[1] - 1):
         utt_end = utt_end + lengths[0, utt]
         bounds.append(utt_end)
     bounds = jnp.stack(bounds).astype(jnp.int32)
-
-    hidden, part = run_part(order[:3], core, from_prev, rows_in, from_next, near, halo)
-    far, corner, blocks[1] = lax.optimization_barrier((far, part[:8, :LANES], blocks[1]))
+    order = jnp.stack([chip, *(lax.rem(chip + steps, chips) for steps in (chips - 1, 1, 2))])
+    rows_late, own_other = lax.optimization_barrier((rows_in, own_other))
+    hidden_sent = by_receiver(normalize_rows(rows_late)[0].astype(bf16))
+    below, hidden_sent, from_prev, from_next, first, load, bounds, order = (
+        lax.optimization_barrier(
+            (below, hidden_sent, from_prev, from_next, first, load, bounds, order)
+        )
+    )
+    upstream = upstream_window(own_window, from_prev, from_next, first, load)
+    half = below.shape[0] // 2
+    far = [ring(below[:half], "y", 1), ring(above[half:], "y", -1)]
+    near = [w_in, own_other, below, other_core(below), above, other_core(above)]
+    blocks = hidden_blocks(hidden_sent)
+
+    hidden, part = run_part(order, core, from_prev, rows_in, from_next, near, halo)
+    far, corner, blocks[1], upstream = lax.optimization_barrier(
+        (far, part[:8, :LANES], blocks[1], upstream)
+    )
     far = far + [other_core(piece) for piece in far]
     shares = lax.axis_size(("x", "c"))
     output, d_mixed, d_shares = run_main(

time: 148 us -> 143 us (0.966)
  waiting for transfers between devices: 24.1 us -> 21.6 us
  local copies, waits for them, and re-layouts: 12.1 us -> 10.1 us
  starting transfers between devices: 48.4 us -> 46.7 us
    ppermute x4, waiting for transfers between devices: 6.76 us -> 3.02 us  [passed_along(): lax.ppermute(value, axis, [(source, source + steps) for source in range(i...]
  transfers between devices with their start and end apart: 22 -> 22, of which waited for: 7 -> 8; matrix products, arithmetic and copies ran while one was open for 19% -> 19% of each run, Pallas kernels for 23% -> 24%
where the time goes in v5:
time: 143 us; the launch traced here: 142 us
  starting transfers between devices  46.7 us (33%)
  Pallas kernels  34.3 us (24%)
  waiting for transfers between devices  21.6 us (15%)
  other arithmetic  13.9 us (10%)
  local copies, waits for them, and re-layouts  10.1 us (7%)
  matrix products  9.79 us (7%)
  between operations  5.79 us (4%)
    ppermute x10, starting transfers between devices, ring(): lax.ppermute(value, axis, [(i, (i + steps) % count) for i in range(count)])  15.8 us
    pallas_call x1, Pallas kernels, run_main(): pl.pallas_call(functools.partial(main_kernel, rows, edge), out_shape=(jax...  15.4 us
    all_to_all x1, starting transfers between devices, weight_gradient(): pieces = lax.all_to_all(pieces, last, 0, 0, tiled=True).astype(f32)  12.4 us
    pallas_call x1, Pallas kernels, run_frame(): pl.pallas_call(frame_kernel, out_shape=jax.ShapeDtypeStruct((rows, width)...  10.1 us
    pallas_call x1, Pallas kernels, run_part(): pl.pallas_call(functools.partial(part_kernel, halo), out_shape=(jax.Shape...  8.9 us
    all_to_all x1, waiting for transfers between devices, on_device(): mixed_share = lax.all_to_all(d_shares, ('x', 'c'), 0, 0, tiled=True)  8.61 us
    ppermute x4, starting transfers between devices, passed_along(): lax.ppermute(value, axis, [(source, source + steps) for source in range(i...  7.4 us
    dot_general x4, matrix products, product(): lax.dot_general(columns, mixed_share, (((0,), (0,)), ((), ())), preferred...  6.97 us
  transfers between devices with their start and end apart: 22, of which 8 were waited for; matrix products, arithmetic and copies ran while one was open for 19% of the time, Pallas kernels for 24%

profile of v5, /device:TPU:1, one launch (start us, length us, event | category | flops | bytes accessed | tf_op | source)
XLA Modules:
  0.0 142.3 jit_solution(9191180734144482097)
XLA Ops:
  0.6 2.2 %collective-permute-start = (bf16[192,3072]{1,0:T(8,128)(2,1)}, bf16[192,3072]{1,0:T(8,128)(2,1)S(1)}, u32[]{:S(2)}, u32[]{:S(2)}) collective-permute-start(bf16[192,3072]{1,0:T(8,128)(2,1)} %rest_0_.3), channel_id=1, source_target_pairs={{0,2},{2,4},{4,6},{6,0},{1,3},{3,5},{5,7},{7,1},{8,10},{10,12},{12... | collective-permute-start | bytes 3538952 | tf_op jit(solution)/shard_map/ppermute | solution.py:371
  4.1 2.9 %collective-permute-start.6 = (bf16[192,3072]{1,0:T(8,128)(2,1)}, bf16[192,3072]{1,0:T(8,128)(2,1)S(1)}, u32[]{:S(2)}, u32[]{:S(2)}) collective-permute-start(bf16[192,3072]{1,0:T(8,128)(2,1)} %rest_0_.3), channel_id=1, source_target_pairs={{0,6},{2,0},{4,2},{6,4},{1,7},{3,1},{5,3},{7,5},{8,14},{10,8},{12,... | collective-permute-start | bytes 3538952 | tf_op jit(solution)/shard_map/ppermute | solution.py:371
  12.6 1.8 %collective-permute-start.2 = (bf16[112,1536]{1,0:T(8,128)(2,1)}, bf16[112,1536]{1,0:T(8,128)(2,1)S(1)}, u32[]{:S(2)}, u32[]{:S(2)}) collective-permute-start(bf16[112,1536]{1,0:T(8,128)(2,1)} %pad_maximum_fusion.1), channel_id=1, source_target_pairs={{0,8},{8,16},{16,24},{24,32},{32,40},{40,48},{48,56},{56,64},{64,7... | collective-permute-start | bytes 1032200 | tf_op jit(solution)/shard_map/ppermute | solution.py:24
  20.8 2.8 %fusion.5 = bf16[128,1536]{1,0:T(8,128)(2,1)} fusion(s32[1536]{0:T(1024)S(1)} %fusion.40, bf16[128,1536]{1,0:T(8,128)(2,1)S(1)} %bitcast.43, f32[128]{0:T(128)S(1)} %add_rsqrt_fusion, f32[128]{0:T(128)S(1)} %broadcast_multiply_fusion.1), kind=kOutput, calls=%fused_computation.10 | convolution fusion | flops 607322112 | bytes 793600 | tf_op jit(solution)/shard_map/dot_general | solution.py:441
  23.6 3.0 %collective-permute-done.3.next_ref = bf16[112,1536]{1,0:T(8,128)(2,1)S(1)} collective-permute-done((bf16[112,1536]{1,0:T(8,128)(2,1)}, bf16[112,1536]{1,0:T(8,128)(2,1)S(1)}, u32[]{:S(2)}, u32[]{:S(2)}) %collective-permute-start.3) | collective-permute-done | bytes 344096 | tf_op jit(solution)/shard_map/ppermute | solution.py:24
  28.1 3.3 %collective-permute-start.8 = (bf16[192,3072]{1,0:T(8,128)(2,1)S(1)}, bf16[192,3072]{1,0:T(8,128)(2,1)}, u32[]{:S(2)}, u32[]{:S(2)}) collective-permute-start(bf16[192,3072]{1,0:T(8,128)(2,1)S(1)} %collective-permute-done.rest_2_), channel_id=1, source_target_pairs={{0,1},{1,0},{2,3},{3,2},{4,5},{5,4},{6,7},{7,6},{8,9},{9,8},{10,11... | collective-permute-start | bytes 3538952 | tf_op jit(solution)/shard_map/ppermute | solution.py:375
  35.5 3.0 %collective-permute-start.7 = (bf16[96,3072]{1,0:T(8,128)(2,1)}, bf16[96,3072]{1,0:T(8,128)(2,1)}, u32[]{:S(2)}, u32[]{:S(2)}) collective-permute-start(bf16[96,3072]{1,0:T(8,128)(2,1)} %slice.53), channel_id=1, source_target_pairs={{0,6},{2,0},{4,2},{6,4},{1,7},{3,1},{5,3},{7,5},{8,14},{10,8},{12,... | collective-permute-start | bytes 1769480 | tf_op jit(solution)/shard_map/ppermute | solution.py:371
  39.7 2.4 %fusion.21.up_ref = bf16[160,1536]{1,0:T(8,128)(2,1)S(1)} fusion(s32[]{:T(128)S(6)} %select_n.140, bf16[112,1536]{1,0:T(8,128)(2,1)S(1)} %collective-permute-done.2.prev_ref, s32[]{:T(128)S(6)} %select_n.141, bf16[112,1536]{1,0:T(8,128)(2,1)S(1)} %broadcast_in_dim.40, bf16[256,1536]{1,0:T(8,128)(2,1)} %copy-done.10, s32[]{:T(128)S(6)} %select_n.142, ...), kind=kLoop, calls=%fused_computation.46 | loop fusion | flops 3440640 | bytes 2310796 | tf_op jit(solution)/shard_map/add | solution.py:413
  42.2 8.9 %forward_part.1 = (bf16[192,1536]{1,0:T(8,128)(2,1)S(1)}, f32[192,3072]{1,0:T(8,128)}) custom-call(s32[4]{0:T(128)S(1)} %pad_add_fusion.at_ref, s32[1]{0:T(128)} %bitcast.14.core_ref, bf16[112,1536]{1,0:T(8,128)(2,1)S(1)} %collective-permute-done.2.prev_ref, bf16[128,1536]{1,0:T(8,128)(2,1)S(1)} %bitcast.44, ...), custom_call_target="tpu_custom_call" | custom-call | flops 2000000000 | bytes 8000000 | tf_op jit(solution)/shard_map/forward_part/pallas_call | solution.py:303
  55.5 1.9 %copy-done.8 = f32[192,3072]{1,0:T(8,128)S(1)} copy-done((f32[192,3072]{1,0:T(8,128)S(1)}, f32[192,3072]{1,0:T(8,128)}, u32[]{:S(2)}) %copy-start.8) | copy-done | bytes 2359320
  57.3 15.4 %main.1 = (bf16[128,1536]{1,0:T(8,128)(2,1)S(1)}, bf16[128,3072]{1,0:T(8,128)(2,1)S(1)}, bf16[8,128,384]{2,1,0:T(8,128)(2,1)}) custom-call(s32[5]{0:T(128)S(1)} %stack.54.bounds_ref, s32[4]{0:T(128)S(1)} %pad_add_fusion.at_ref, s32[1]{0:T(128)} %bitcast.14.core_ref, f32[8,128]{1,0:T(8,128)S(1)} %slice.49.corner_ref, ...), custom_call_target="tpu_custom_call" | custom-call | flops 6000000000 | bytes 12000000 | tf_op jit(solution)/shard_map/main/pallas_call | solution.py:326
  75.7 4.2 %all-to-all-start = ((bf16[8,128,384]{2,1,0:T(8,128)(2,1)}), bf16[8,128,384]{2,1,0:T(8,128)(2,1)}, u32[]{:S(2)}, u32[]{:S(2)}) async-start(bf16[8,128,384]{2,1,0:T(8,128)(2,1)} %get-tuple-element.54), calls=%async_computation | async-start | bytes 1572864 | tf_op jit(solution)/shard_map/all_to_all | solution.py:538
  80.0 1.8 %select_bitcast_fusion = (bf16[4,1,128,1536]{3,2,0,1:T(8,128)(2,1)S(1)}, bf16[4,1,128,1536]{3,2,0,1:T(8,128)(2,1)S(1)}) fusion(bf16[4,128,1536]{2,1,0:T(8,128)(2,1)} %collective-permute-done.16, pred[]{:T(512)S(6)} %eq.30, bf16[1,128,1536]{2,1,0:T(8,128)(2,1)S(1)} %bitcast.50, bf16[1,128,1536]{2,1,0:T(8,128)(2,1)S(1)} %bitcast.54, ...), kind=kLoop, calls=%fused_computation.13 | loop fusion | flops 3932160 | bytes 6291457 | tf_op jit(solution)/shard_map/stack | solution.py:453
  83.8 8.6 %all-to-all-done = bf16[8,128,384]{2,1,0:T(8,128)(2,1)} async-done(((bf16[8,128,384]{2,1,0:T(8,128)(2,1)}), bf16[8,128,384]{2,1,0:T(8,128)(2,1)}, u32[]{:S(2)}, u32[]{:S(2)}) %all-to-all-start) | async-done | bytes 786464 | tf_op jit(solution)/shard_map/all_to_all | solution.py:538
  92.4 1.7 %convolution_convert_fusion = bf16[384,384]{1,0:T(8,128)(2,1)S(1)} fusion(bf16[1024,384]{1,0:T(8,128)(2,1)} %bitcast.24, bf16[1024,1536]{1,0:T(8,128)(2,1)S(1)} %bitcast.45, s32[]{:T(128)S(6)} %select_n.157), kind=kOutput, calls=%fused_computation.18 | convolution fusion | flops 302137344 | bytes 1867780 | tf_op jit(solution)/shard_map/dot_general | solution.py:471
  94.1 3.1 %collective-permute-start.19 = (bf16[384,384]{1,0:T(8,128)(2,1)S(1)}, bf16[384,384]{1,0:T(8,128)(2,1)S(1)}, u32[]{:S(2)}, u32[]{:S(2)}) collective-permute-start(bf16[384,384]{1,0:T(8,128)(2,1)S(1)} %convolution_convert_fusion), channel_id=1, source_target_pairs={{0,6},{2,0},{4,2},{6,4},{1,7},{3,1},{5,3},{7,5},{8,14},{10,8},{12,... | collective-permute-start | bytes 884744 | tf_op jit(solution)/shard_map/ppermute | solution.py:371
  97.2 1.7 %convolution_convert_fusion.1 = bf16[384,384]{1,0:T(8,128)(2,1)S(1)} fusion(bf16[1024,384]{1,0:T(8,128)(2,1)} %bitcast.24, bf16[1024,1536]{1,0:T(8,128)(2,1)S(1)} %bitcast.46, s32[]{:T(128)S(6)} %select_n.155), kind=kOutput, calls=%fused_computation.19 | convolution fusion | flops 302137344 | bytes 1867780 | tf_op jit(solution)/shard_map/dot_general | solution.py:471
  99.1 1.8 %convolution_convert_fusion.2 = bf16[384,384]{1,0:T(8,128)(2,1)S(1)} fusion(bf16[1024,384]{1,0:T(8,128)(2,1)} %bitcast.24, bf16[1024,1536]{1,0:T(8,128)(2,1)S(1)} %bitcast.47, s32[]{:T(128)S(6)} %select_n.153), kind=kOutput, calls=%fused_computation.20 | convolution fusion | flops 302137344 | bytes 1867780 | tf_op jit(solution)/shard_map/dot_general | solution.py:471
  103.3 3.0 %collective-permute-start.14 = (bf16[64,1536]{1,0:T(8,128)(2,1)}, bf16[64,1536]{1,0:T(8,128)(2,1)}, u32[]{:S(2)}, u32[]{:S(2)}) collective-permute-start(bf16[64,1536]{1,0:T(8,128)(2,1)} %get-tuple-element.62), channel_id=1, source_target_pairs={{0,8},{8,16},{16,24},{24,32},{32,40},{40,48},{48,56},{56,64},{64,7... | collective-permute-start | bytes 589832 | tf_op jit(solution)/shard_map/ppermute | solution.py:24
  109.4 3.6 %collective-permute-done.17 = bf16[384,384]{1,0:T(8,128)(2,1)S(1)} collective-permute-done((bf16[384,384]{1,0:T(8,128)(2,1)S(1)}, bf16[384,384]{1,0:T(8,128)(2,1)S(1)}, u32[]{:S(2)}, u32[]{:S(2)}) %collective-permute-start.17) | collective-permute-done | bytes 294944 | tf_op jit(solution)/shard_map/ppermute | solution.py:371
  114.1 12.4 %all-to-all-start.1 = ((bf16[64,6,384]{2,1,0:T(8,128)(2,1)}), bf16[64,6,384]{2,1,0:T(8,128)(2,1)S(1)}, u32[]{:S(2)}, u32[]{:S(2)}) async-start(bf16[64,6,384]{2,1,0:T(8,128)(2,1)} %reshape.132), calls=%async_computation.1 | async-start | bytes 786432 | tf_op jit(solution)/shard_map/all_to_all | solution.py:483
  126.5 10.1 %frame_back.1 = bf16[128,1536]{1,0:T(8,128)(2,1)} custom-call(s32[4]{0:T(128)} %copy-done.7, s32[1]{0:T(128)} %bitcast.14.core_ref, bf16[128,1536]{1,0:T(8,128)(2,1)} %bitcast.40, bf16[128,3072]{1,0:T(8,128)(2,1)} %copy-done.4, bf16[192,3072]{1,0:T(8,128)(2,1)} %rest_0_.3, bf16[192,3072]{1,0:T(8,128)(2,1)} %collective-permute-done.1.rest_1_, ...), custom_call_target="tpu_custom_call" | custom-call | flops 2000000000 | bytes 11000000 | tf_op jit(solution)/shard_map/frame_back/pallas_call | solution.py:353
  136.6 2.4 %fusion.14 = bf16[1,256,1536]{2,1,0:T(8,128)(2,1)} fusion(s32[]{:T(128)S(6)} %select_n.143, bf16[64,1536]{1,0:T(8,128)(2,1)} %collective-permute-done.14, bf16[128,1536]{1,0:T(8,128)(2,1)S(1)} %get-tuple-element.48, bf16[64,1536]{1,0:T(8,128)(2,1)} %collective-permute-done.15, pred[256]{0:T(512)(128)(4,1)S(1)} %iota_compare_fusion.4, ...), kind=kLoop, calls=%fused_computation.36 | loop fusion | flops 3538944 | bytes 1573636 | tf_op jit(solution)/shard_map/broadcast_in_dim | solution.py:545
  139.0 2.5 %all-to-all-done.1 = bf16[64,6,384]{2,1,0:T(8,128)(2,1)S(1)} async-done(((bf16[64,6,384]{2,1,0:T(8,128)(2,1)}), bf16[64,6,384]{2,1,0:T(8,128)(2,1)S(1)}, u32[]{:S(2)}, u32[]{:S(2)}) %all-to-all-start.1) | async-done | bytes 294944 | tf_op jit(solution)/shard_map/all_to_all | solution.py:483
  (100 shorter events, 31.9 us)
Async XLA Ops:
  0.6 27.5 %collective-permute-start = (bf16[192,3072]{1,0:T(8,128)(2,1)}, bf16[192,3072]{1,0:T(8,128)(2,1)S(1)}, u32[]{:S(2)}, u32[]{:S(2)}) collective-permute-start(bf16[192,3072]{1,0:T(8,128)(2,1)} %rest_0_.3), channel_id=1, source_target_pairs={{0,2},{2,4},{4,6},{6,0},{1,3},{3,5},{5,7},{7,1},{8,10},{10,12},{12... | collective-permute-start | bytes 3538952 | tf_op jit(solution)/shard_map/ppermute | solution.py:371
  2.8 17.6 %collective-permute-start.1 = (bf16[192,3072]{1,0:T(8,128)(2,1)}, bf16[192,3072]{1,0:T(8,128)(2,1)}, u32[]{:S(2)}, u32[]{:S(2)}) collective-permute-start(bf16[192,3072]{1,0:T(8,128)(2,1)} %rest_0_.3), channel_id=1, source_target_pairs={{0,1},{1,0},{2,3},{3,2},{4,5},{5,4},{6,7},{7,6},{8,9},{9,8},{10,11... | collective-permute-start | bytes 3538952 | tf_op jit(solution)/shard_map/ppermute | solution.py:375
  4.1 28.6 %collective-permute-start.6 = (bf16[192,3072]{1,0:T(8,128)(2,1)}, bf16[192,3072]{1,0:T(8,128)(2,1)S(1)}, u32[]{:S(2)}, u32[]{:S(2)}) collective-permute-start(bf16[192,3072]{1,0:T(8,128)(2,1)} %rest_0_.3), channel_id=1, source_target_pairs={{0,6},{2,0},{4,2},{6,4},{1,7},{3,1},{5,3},{7,5},{8,14},{10,8},{12,... | collective-permute-start | bytes 3538952 | tf_op jit(solution)/shard_map/ppermute | solution.py:371
  12.6 11.1 %collective-permute-start.2 = (bf16[112,1536]{1,0:T(8,128)(2,1)}, bf16[112,1536]{1,0:T(8,128)(2,1)S(1)}, u32[]{:S(2)}, u32[]{:S(2)}) collective-permute-start(bf16[112,1536]{1,0:T(8,128)(2,1)} %pad_maximum_fusion.1), channel_id=1, source_target_pairs={{0,8},{8,16},{16,24},{24,32},{32,40},{40,48},{48,56},{56,64},{64,7... | collective-permute-start | bytes 1032200 | tf_op jit(solution)/shard_map/ppermute | solution.py:24
  15.2 11.5 %collective-permute-start.3 = (bf16[112,1536]{1,0:T(8,128)(2,1)}, bf16[112,1536]{1,0:T(8,128)(2,1)S(1)}, u32[]{:S(2)}, u32[]{:S(2)}) collective-permute-start(bf16[112,1536]{1,0:T(8,128)(2,1)} %pad_maximum_fusion.2), channel_id=1, source_target_pairs={{8,0},{16,8},{24,16},{32,24},{40,32},{48,40},{56,48},{64,56},{72,6... | collective-permute-start | bytes 1032200 | tf_op jit(solution)/shard_map/ppermute | solution.py:24
  20.4 35.1 %copy-start.7 = (s32[4]{0:T(128)}, s32[4]{0:T(128)S(1)}, u32[]{:S(2)}) copy-start(s32[4]{0:T(128)S(1)} %pad_add_fusion.at_ref) | copy-start | bytes 52
  28.1 14.0 %collective-permute-start.8 = (bf16[192,3072]{1,0:T(8,128)(2,1)S(1)}, bf16[192,3072]{1,0:T(8,128)(2,1)}, u32[]{:S(2)}, u32[]{:S(2)}) collective-permute-start(bf16[192,3072]{1,0:T(8,128)(2,1)S(1)} %collective-permute-done.rest_2_), channel_id=1, source_target_pairs={{0,1},{1,0},{2,3},{3,2},{4,5},{5,4},{6,7},{7,6},{8,9},{9,8},{10,11... | collective-permute-start | bytes 3538952 | tf_op jit(solution)/shard_map/ppermute | solution.py:375
  32.6 9.5 %collective-permute-start.9 = (bf16[192,3072]{1,0:T(8,128)(2,1)S(1)}, bf16[192,3072]{1,0:T(8,128)(2,1)}, u32[]{:S(2)}, u32[]{:S(2)}) collective-permute-start(bf16[192,3072]{1,0:T(8,128)(2,1)S(1)} %collective-permute-done.6.rest_4_), channel_id=1, source_target_pairs={{0,1},{1,0},{2,3},{3,2},{4,5},{5,4},{6,7},{7,6},{8,9},{9,8},{10,11... | collective-permute-start | bytes 3538952 | tf_op jit(solution)/shard_map/ppermute | solution.py:375
  34.3 17.5 %collective-permute-start.5 = (bf16[96,3072]{1,0:T(8,128)(2,1)}, bf16[96,3072]{1,0:T(8,128)(2,1)}, u32[]{:S(2)}, u32[]{:S(2)}) collective-permute-start(bf16[96,3072]{1,0:T(8,128)(2,1)} %slice.47), channel_id=1, source_target_pairs={{0,2},{2,4},{4,6},{6,0},{1,3},{3,5},{5,7},{7,1},{8,10},{10,12},{12... | collective-permute-start | bytes 1769480 | tf_op jit(solution)/shard_map/ppermute | solution.py:371
  35.5 16.3 %collective-permute-start.7 = (bf16[96,3072]{1,0:T(8,128)(2,1)}, bf16[96,3072]{1,0:T(8,128)(2,1)}, u32[]{:S(2)}, u32[]{:S(2)}) collective-permute-start(bf16[96,3072]{1,0:T(8,128)(2,1)} %slice.53), channel_id=1, source_target_pairs={{0,6},{2,0},{4,2},{6,4},{1,7},{3,1},{5,3},{7,5},{8,14},{10,8},{12,... | collective-permute-start | bytes 1769480 | tf_op jit(solution)/shard_map/ppermute | solution.py:371
  38.5 13.3 %collective-permute-start.10 = (bf16[128,1536]{1,0:T(8,128)(2,1)}, bf16[128,1536]{1,0:T(8,128)(2,1)}, u32[]{:S(2)}, u32[]{:S(2)}) collective-permute-start(bf16[128,1536]{1,0:T(8,128)(2,1)} %fusion.5), channel_id=1, source_target_pairs={{0,128},{64,192},{128,0},{192,64},{1,129},{65,193},{129,1},{193,65... | collective-permute-start | bytes 1179656 | tf_op jit(solution)/shard_map/ppermute | solution.py:371
  51.8 2.8 %collective-permute-start.12 = (bf16[96,3072]{1,0:T(8,128)(2,1)}, bf16[96,3072]{1,0:T(8,128)(2,1)S(1)}, u32[]{:S(2)}, u32[]{:S(2)}) collective-permute-start(bf16[96,3072]{1,0:T(8,128)(2,1)} %collective-permute-done.5.rest_0_.rest_6_), channel_id=1, source_target_pairs={{0,1},{1,0},{2,3},{3,2},{4,5},{5,4},{6,7},{7,6},{8,9},{9,8},{10,11... | collective-permute-start | bytes 1769480 | tf_op jit(solution)/shard_map/ppermute | solution.py:375
  52.8 2.7 %collective-permute-start.13 = (bf16[96,3072]{1,0:T(8,128)(2,1)}, bf16[96,3072]{1,0:T(8,128)(2,1)S(1)}, u32[]{:S(2)}, u32[]{:S(2)}) collective-permute-start(bf16[96,3072]{1,0:T(8,128)(2,1)} %collective-permute-done.7.rest_1_.rest_7_), channel_id=1, source_target_pairs={{0,1},{1,0},{2,3},{3,2},{4,5},{5,4},{6,7},{7,6},{8,9},{9,8},{10,11... | collective-permute-start | bytes 1769480 | tf_op jit(solution)/shard_map/ppermute | solution.py:375
  52.9 19.9 %collective-permute-start.4 = (bf16[128,1536]{1,0:T(8,128)(2,1)S(1)}, bf16[128,1536]{1,0:T(8,128)(2,1)S(1)}, u32[]{:S(2)}, u32[]{:S(2)}) collective-permute-start(bf16[128,1536]{1,0:T(8,128)(2,1)S(1)} %copy-done.11), channel_id=1, source_target_pairs={{0,192},{64,0},{128,64},{192,128},{1,193},{65,1},{129,65},{193,129... | collective-permute-start | bytes 1179656 | tf_op jit(solution)/shard_map/ppermute | solution.py:371
  54.0 18.8 %collective-permute-start.11 = (bf16[128,1536]{1,0:T(8,128)(2,1)S(1)}, bf16[128,1536]{1,0:T(8,128)(2,1)S(1)}, u32[]{:S(2)}, u32[]{:S(2)}) collective-permute-start(bf16[128,1536]{1,0:T(8,128)(2,1)S(1)} %copy-done.11), channel_id=1, source_target_pairs={{0,64},{64,128},{128,192},{192,0},{1,65},{65,129},{129,193},{193,1... | collective-permute-start | bytes 1179656 | tf_op jit(solution)/shard_map/ppermute | solution.py:371
  54.6 18.1 %copy-start.5 = (bf16[96,3072]{1,0:T(8,128)(2,1)}, bf16[96,3072]{1,0:T(8,128)(2,1)S(1)}, u32[]{:S(2)}) copy-start(bf16[96,3072]{1,0:T(8,128)(2,1)S(1)} %collective-permute-done.12.rest_2_.rest_8_) | copy-start | bytes 1769476
  74.4 5.6 %collective-permute-start.16 = (bf16[4,128,1536]{2,1,0:T(8,128)(2,1)S(1)}, bf16[4,128,1536]{2,1,0:T(8,128)(2,1)}, u32[]{:S(2)}, u32[]{:S(2)}) collective-permute-start(bf16[4,128,1536]{2,1,0:T(8,128)(2,1)S(1)} %pad_maximum_fusion), channel_id=1, source_target_pairs={{0,1},{1,0},{2,3},{3,2},{4,5},{5,4},{6,7},{7,6},{8,9},{9,8},{10,11... | collective-permute-start | bytes 4718600 | tf_op jit(solution)/shard_map/ppermute | solution.py:375
  75.7 16.7 %all-to-all-start = ((bf16[8,128,384]{2,1,0:T(8,128)(2,1)}), bf16[8,128,384]{2,1,0:T(8,128)(2,1)}, u32[]{:S(2)}, u32[]{:S(2)}) async-start(bf16[8,128,384]{2,1,0:T(8,128)(2,1)} %get-tuple-element.54), calls=%async_computation | async-start | bytes 1572864 | tf_op jit(solution)/shard_map/all_to_all | solution.py:538
  94.1 18.9 %collective-permute-start.19 = (bf16[384,384]{1,0:T(8,128)(2,1)S(1)}, bf16[384,384]{1,0:T(8,128)(2,1)S(1)}, u32[]{:S(2)}, u32[]{:S(2)}) collective-permute-start(bf16[384,384]{1,0:T(8,128)(2,1)S(1)} %convolution_convert_fusion), channel_id=1, source_target_pairs={{0,6},{2,0},{4,2},{6,4},{1,7},{3,1},{5,3},{7,5},{8,14},{10,8},{12,... | collective-permute-start | bytes 884744 | tf_op jit(solution)/shard_map/ppermute | solution.py:371
  99.0 14.1 %collective-permute-start.18 = (bf16[384,384]{1,0:T(8,128)(2,1)S(1)}, bf16[384,384]{1,0:T(8,128)(2,1)S(1)}, u32[]{:S(2)}, u32[]{:S(2)}) collective-permute-start(bf16[384,384]{1,0:T(8,128)(2,1)S(1)} %convolution_convert_fusion.1), channel_id=1, source_target_pairs={{0,2},{2,4},{4,6},{6,0},{1,3},{3,5},{5,7},{7,1},{8,10},{10,12},{12... | collective-permute-start | bytes 884744 | tf_op jit(solution)/shard_map/ppermute | solution.py:371
  100.8 12.2 %collective-permute-start.17 = (bf16[384,384]{1,0:T(8,128)(2,1)S(1)}, bf16[384,384]{1,0:T(8,128)(2,1)S(1)}, u32[]{:S(2)}, u32[]{:S(2)}) collective-permute-start(bf16[384,384]{1,0:T(8,128)(2,1)S(1)} %convolution_convert_fusion.2), channel_id=1, source_target_pairs={{0,4},{2,6},{4,0},{6,2},{1,5},{3,7},{5,1},{7,3},{8,12},{10,14},{12... | collective-permute-start | bytes 884744 | tf_op jit(solution)/shard_map/ppermute | solution.py:371
  103.3 33.2 %collective-permute-start.14 = (bf16[64,1536]{1,0:T(8,128)(2,1)}, bf16[64,1536]{1,0:T(8,128)(2,1)}, u32[]{:S(2)}, u32[]{:S(2)}) collective-permute-start(bf16[64,1536]{1,0:T(8,128)(2,1)} %get-tuple-element.62), channel_id=1, source_target_pairs={{0,8},{8,16},{16,24},{24,32},{32,40},{40,48},{48,56},{56,64},{64,7... | collective-permute-start | bytes 589832 | tf_op jit(solution)/shard_map/ppermute | solution.py:24
  106.4 30.2 %collective-permute-start.15 = (bf16[64,1536]{1,0:T(8,128)(2,1)}, bf16[64,1536]{1,0:T(8,128)(2,1)}, u32[]{:S(2)}, u32[]{:S(2)}) collective-permute-start(bf16[64,1536]{1,0:T(8,128)(2,1)} %get-tuple-element.61), channel_id=1, source_target_pairs={{8,0},{16,8},{24,16},{32,24},{40,32},{48,40},{56,48},{64,56},{72,6... | collective-permute-start | bytes 589832 | tf_op jit(solution)/shard_map/ppermute | solution.py:24
  114.1 27.5 %all-to-all-start.1 = ((bf16[64,6,384]{2,1,0:T(8,128)(2,1)}), bf16[64,6,384]{2,1,0:T(8,128)(2,1)S(1)}, u32[]{:S(2)}, u32[]{:S(2)}) async-start(bf16[64,6,384]{2,1,0:T(8,128)(2,1)} %reshape.132), calls=%async_computation.1 | async-start | bytes 786432 | tf_op jit(solution)/shard_map/all_to_all | solution.py:483
  (16 other events, 101.1 us)

commit v6 on v5

--- a/solution.py
+++ b/solution.py
@@ -312,7 +312,7 @@
             pltpu.VMEM((NEAR, depth, mixed_width), bf16),
             pltpu.SemaphoreType.DMA((len(pieces),)),
         ],
-        compiler_params=limit(44),
+        compiler_params=limit(32),
         cost_estimate=pl.CostEstimate(flops=2 * 10**9, bytes_accessed=8 * 10**6, transcendentals=0),
         name="forward_part",
     )(chips, core, from_prev, rows_in, from_next, *pieces)
@@ -342,7 +342,7 @@
             pltpu.VMEM((taps, wide, LANES), f32),
             pltpu.SemaphoreType.DMA((len(pieces),)),
         ],
-        compiler_params=limit(44),
+        compiler_params=limit(32),
         cost_estimate=pl.CostEstimate(flops=6 * 10**9, bytes_accessed=12 * 10**6, transcendentals=0),
         name="main",
     )(bounds, chips, core, corner, hidden, part, upstream, kernel, *pieces)

time: 143 us -> 142 us (level)
  local copies, waits for them, and re-layouts: 10.1 us -> 7.53 us
  starting transfers between devices: 46.7 us -> 48.5 us
    unnamed x36 -> x34, local copies, waits for them, and re-layouts: 2.67 us -> 0.79 us
  transfers between devices with their start and end apart: 22 -> 22, of which waited for: 8 -> 10; matrix products, arithmetic and copies ran while one was open for 19% -> 19% of each run, Pallas kernels for 24% -> 23%
where the time goes in v6:
time: 142 us; the launch traced here: 141 us
  starting transfers between devices  48.5 us (34%)
  Pallas kernels  32.9 us (23%)
  waiting for transfers between devices  22.4 us (16%)
  other arithmetic  13.9 us (10%)
  matrix products  9.79 us (7%)
  local copies, waits for them, and re-layouts  7.53 us (5%)
  between operations  5.52 us (4%)
    ppermute x10, starting transfers between devices, ring(): lax.ppermute(value, axis, [(i, (i + steps) % count) for i in range(count)])  16 us
    pallas_call x1, Pallas kernels, run_main(): pl.pallas_call(functools.partial(main_kernel, rows, edge), out_shape=(jax...  15.4 us
    all_to_all x1, starting transfers between devices, weight_gradient(): pieces = lax.all_to_all(pieces, last, 0, 0, tiled=True).astype(f32)  13 us
    pallas_call x1, Pallas kernels, run_frame(): pl.pallas_call(frame_kernel, out_shape=jax.ShapeDtypeStruct((rows, width)...  10.1 us
    all_to_all x1, waiting for transfers between devices, on_device(): mixed_share = lax.all_to_all(d_shares, ('x', 'c'), 0, 0, tiled=True)  8.59 us
    ppermute x4, starting transfers between devices, passed_along(): lax.ppermute(value, axis, [(source, source + steps) for source in range(i...  8.51 us
    pallas_call x1, Pallas kernels, run_part(): pl.pallas_call(functools.partial(part_kernel, halo), out_shape=(jax.Shape...  7.48 us
    ppermute x10, waiting for transfers between devices, ring(): lax.ppermute(value, axis, [(i, (i + steps) % count) for i in range(count)])  7.22 us
  transfers between devices with their start and end apart: 22, of which 10 were waited for; matrix products, arithmetic and copies ran while one was open for 19% of the time, Pallas kernels for 23%

profile of v6, /device:TPU:1, one launch (start us, length us, event | category | flops | bytes accessed | tf_op | source)
XLA Modules:
  0.0 140.5 jit_solution(8964185533270128075)
XLA Ops:
  0.6 2.2 %collective-permute-start = (bf16[192,3072]{1,0:T(8,128)(2,1)}, bf16[192,3072]{1,0:T(8,128)(2,1)S(1)}, u32[]{:S(2)}, u32[]{:S(2)}) collective-permute-start(bf16[192,3072]{1,0:T(8,128)(2,1)} %rest_0_.3), channel_id=1, source_target_pairs={{0,2},{2,4},{4,6},{6,0},{1,3},{3,5},{5,7},{7,1},{8,10},{10,12},{12... | collective-permute-start | bytes 3538952 | tf_op jit(solution)/shard_map/ppermute | solution.py:371
  4.1 2.9 %collective-permute-start.6 = (bf16[192,3072]{1,0:T(8,128)(2,1)}, bf16[192,3072]{1,0:T(8,128)(2,1)S(1)}, u32[]{:S(2)}, u32[]{:S(2)}) collective-permute-start(bf16[192,3072]{1,0:T(8,128)(2,1)} %rest_0_.3), channel_id=1, source_target_pairs={{0,6},{2,0},{4,2},{6,4},{1,7},{3,1},{5,3},{7,5},{8,14},{10,8},{12,... | collective-permute-start | bytes 3538952 | tf_op jit(solution)/shard_map/ppermute | solution.py:371
  12.4 1.8 %collective-permute-start.2 = (bf16[112,1536]{1,0:T(8,128)(2,1)}, bf16[112,1536]{1,0:T(8,128)(2,1)S(1)}, u32[]{:S(2)}, u32[]{:S(2)}) collective-permute-start(bf16[112,1536]{1,0:T(8,128)(2,1)} %pad_maximum_fusion.1), channel_id=1, source_target_pairs={{0,8},{8,16},{16,24},{24,32},{32,40},{40,48},{48,56},{56,64},{64,7... | collective-permute-start | bytes 1032200 | tf_op jit(solution)/shard_map/ppermute | solution.py:24
  20.7 2.8 %fusion.5 = bf16[128,1536]{1,0:T(8,128)(2,1)} fusion(s32[1536]{0:T(1024)S(1)} %fusion.40, bf16[128,1536]{1,0:T(8,128)(2,1)S(1)} %bitcast.43, f32[128]{0:T(128)S(1)} %add_rsqrt_fusion, f32[128]{0:T(128)S(1)} %broadcast_multiply_fusion.1), kind=kOutput, calls=%fused_computation.10 | convolution fusion | flops 607322112 | bytes 793600 | tf_op jit(solution)/shard_map/dot_general | solution.py:441
  23.5 3.0 %collective-permute-done.3.next_ref = bf16[112,1536]{1,0:T(8,128)(2,1)S(1)} collective-permute-done((bf16[112,1536]{1,0:T(8,128)(2,1)}, bf16[112,1536]{1,0:T(8,128)(2,1)S(1)}, u32[]{:S(2)}, u32[]{:S(2)}) %collective-permute-start.3) | collective-permute-done | bytes 344096 | tf_op jit(solution)/shard_map/ppermute | solution.py:24
  28.1 3.3 %collective-permute-start.8 = (bf16[192,3072]{1,0:T(8,128)(2,1)S(1)}, bf16[192,3072]{1,0:T(8,128)(2,1)}, u32[]{:S(2)}, u32[]{:S(2)}) collective-permute-start(bf16[192,3072]{1,0:T(8,128)(2,1)S(1)} %collective-permute-done.rest_2_), channel_id=1, source_target_pairs={{0,1},{1,0},{2,3},{3,2},{4,5},{5,4},{6,7},{7,6},{8,9},{9,8},{10,11... | collective-permute-start | bytes 3538952 | tf_op jit(solution)/shard_map/ppermute | solution.py:375
  35.4 3.0 %collective-permute-start.7 = (bf16[96,3072]{1,0:T(8,128)(2,1)}, bf16[96,3072]{1,0:T(8,128)(2,1)}, u32[]{:S(2)}, u32[]{:S(2)}) collective-permute-start(bf16[96,3072]{1,0:T(8,128)(2,1)} %slice.53), channel_id=1, source_target_pairs={{0,6},{2,0},{4,2},{6,4},{1,7},{3,1},{5,3},{7,5},{8,14},{10,8},{12,... | collective-permute-start | bytes 1769480 | tf_op jit(solution)/shard_map/ppermute | solution.py:371
  39.7 2.4 %fusion.21.up_ref = bf16[160,1536]{1,0:T(8,128)(2,1)S(1)} fusion(s32[]{:T(128)S(6)} %select_n.140, bf16[112,1536]{1,0:T(8,128)(2,1)S(1)} %collective-permute-done.2.prev_ref, s32[]{:T(128)S(6)} %select_n.141, bf16[112,1536]{1,0:T(8,128)(2,1)S(1)} %broadcast_in_dim.40, bf16[256,1536]{1,0:T(8,128)(2,1)} %copy-done.9, s32[]{:T(128)S(6)} %select_n.142, ...), kind=kLoop, calls=%fused_computation.46 | loop fusion | flops 3440640 | bytes 2310796 | tf_op jit(solution)/shard_map/add | solution.py:413
  42.2 7.5 %forward_part.1 = (bf16[192,1536]{1,0:T(8,128)(2,1)S(1)}, f32[192,3072]{1,0:T(8,128)S(1)}) custom-call(s32[4]{0:T(128)S(1)} %pad_add_fusion.at_ref, s32[1]{0:T(128)} %bitcast.14.core_ref, bf16[112,1536]{1,0:T(8,128)(2,1)S(1)} %collective-permute-done.2.prev_ref, bf16[128,1536]{1,0:T(8,128)(2,1)S(1)} %bitcast.44, ...), custom_call_target="tpu_custom_call" | custom-call | flops 2000000000 | bytes 8000000 | tf_op jit(solution)/shard_map/forward_part/pallas_call | solution.py:303
  55.0 15.4 %main.1 = (bf16[128,1536]{1,0:T(8,128)(2,1)S(1)}, bf16[128,3072]{1,0:T(8,128)(2,1)S(1)}, bf16[8,128,384]{2,1,0:T(8,128)(2,1)}) custom-call(s32[5]{0:T(128)S(1)} %stack.54.bounds_ref, s32[4]{0:T(128)S(1)} %pad_add_fusion.at_ref, s32[1]{0:T(128)} %bitcast.14.core_ref, f32[8,128]{1,0:T(8,128)S(1)} %slice.49.corner_ref, ...), custom_call_target="tpu_custom_call" | custom-call | flops 6000000000 | bytes 12000000 | tf_op jit(solution)/shard_map/main/pallas_call | solution.py:326
  73.3 4.4 %all-to-all-start = ((bf16[8,128,384]{2,1,0:T(8,128)(2,1)}), bf16[8,128,384]{2,1,0:T(8,128)(2,1)}, u32[]{:S(2)}, u32[]{:S(2)}) async-start(bf16[8,128,384]{2,1,0:T(8,128)(2,1)} %get-tuple-element.54), calls=%async_computation | async-start | bytes 1572864 | tf_op jit(solution)/shard_map/all_to_all | solution.py:538
  77.7 1.8 %select_bitcast_fusion = (bf16[4,1,128,1536]{3,2,0,1:T(8,128)(2,1)S(1)}, bf16[4,1,128,1536]{3,2,0,1:T(8,128)(2,1)S(1)}) fusion(bf16[4,128,1536]{2,1,0:T(8,128)(2,1)} %collective-permute-done.16, pred[]{:T(512)S(6)} %eq.30, bf16[1,128,1536]{2,1,0:T(8,128)(2,1)S(1)} %bitcast.50, bf16[1,128,1536]{2,1,0:T(8,128)(2,1)S(1)} %bitcast.54, ...), kind=kLoop, calls=%fused_computation.13 | loop fusion | flops 3932160 | bytes 6291457 | tf_op jit(solution)/shard_map/stack | solution.py:453
  81.5 8.6 %all-to-all-done = bf16[8,128,384]{2,1,0:T(8,128)(2,1)} async-done(((bf16[8,128,384]{2,1,0:T(8,128)(2,1)}), bf16[8,128,384]{2,1,0:T(8,128)(2,1)}, u32[]{:S(2)}, u32[]{:S(2)}) %all-to-all-start) | async-done | bytes 786464 | tf_op jit(solution)/shard_map/all_to_all | solution.py:538
  90.1 1.7 %convolution_convert_fusion = bf16[384,384]{1,0:T(8,128)(2,1)S(1)} fusion(bf16[1024,384]{1,0:T(8,128)(2,1)} %bitcast.24, bf16[1024,1536]{1,0:T(8,128)(2,1)S(1)} %bitcast.45, s32[]{:T(128)S(6)} %select_n.157), kind=kOutput, calls=%fused_computation.18 | convolution fusion | flops 302137344 | bytes 1867780 | tf_op jit(solution)/shard_map/dot_general | solution.py:471
  91.8 3.4 %collective-permute-start.19 = (bf16[384,384]{1,0:T(8,128)(2,1)S(1)}, bf16[384,384]{1,0:T(8,128)(2,1)S(1)}, u32[]{:S(2)}, u32[]{:S(2)}) collective-permute-start(bf16[384,384]{1,0:T(8,128)(2,1)S(1)} %convolution_convert_fusion), channel_id=1, source_target_pairs={{0,6},{2,0},{4,2},{6,4},{1,7},{3,1},{5,3},{7,5},{8,14},{10,8},{12,... | collective-permute-start | bytes 884744 | tf_op jit(solution)/shard_map/ppermute | solution.py:371
  95.2 1.7 %convolution_convert_fusion.1 = bf16[384,384]{1,0:T(8,128)(2,1)S(1)} fusion(bf16[1024,384]{1,0:T(8,128)(2,1)} %bitcast.24, bf16[1024,1536]{1,0:T(8,128)(2,1)S(1)} %bitcast.46, s32[]{:T(128)S(6)} %select_n.155), kind=kOutput, calls=%fused_computation.19 | convolution fusion | flops 302137344 | bytes 1867780 | tf_op jit(solution)/shard_map/dot_general | solution.py:471
  97.0 1.7 %convolution_convert_fusion.2 = bf16[384,384]{1,0:T(8,128)(2,1)S(1)} fusion(bf16[1024,384]{1,0:T(8,128)(2,1)} %bitcast.24, bf16[1024,1536]{1,0:T(8,128)(2,1)S(1)} %bitcast.47, s32[]{:T(128)S(6)} %select_n.153), kind=kOutput, calls=%fused_computation.20 | convolution fusion | flops 302137344 | bytes 1867780 | tf_op jit(solution)/shard_map/dot_general | solution.py:471
  101.0 4.1 %collective-permute-start.14 = (bf16[64,1536]{1,0:T(8,128)(2,1)}, bf16[64,1536]{1,0:T(8,128)(2,1)}, u32[]{:S(2)}, u32[]{:S(2)}) collective-permute-start(bf16[64,1536]{1,0:T(8,128)(2,1)} %get-tuple-element.62), channel_id=1, source_target_pairs={{0,8},{8,16},{16,24},{24,32},{32,40},{40,48},{48,56},{56,64},{64,7... | collective-permute-start | bytes 589832 | tf_op jit(solution)/shard_map/ppermute | solution.py:24
  106.4 1.7 %fusion.18 = f32[384,384]{1,0:T(8,128)S(1)} fusion(bf16[1024,384]{1,0:T(8,128)(2,1)} %bitcast.24, bf16[1024,1536]{1,0:T(8,128)(2,1)S(1)} %bitcast.48, s32[]{:T(128)S(6)} %select_n.151), kind=kOutput, calls=%fused_computation.42 | convolution fusion | flops 301989888 | bytes 2162692 | tf_op jit(solution)/shard_map/dot_general | solution.py:471
  108.2 2.5 %collective-permute-done.17 = bf16[384,384]{1,0:T(8,128)(2,1)S(1)} collective-permute-done((bf16[384,384]{1,0:T(8,128)(2,1)S(1)}, bf16[384,384]{1,0:T(8,128)(2,1)S(1)}, u32[]{:S(2)}, u32[]{:S(2)}) %collective-permute-start.17) | collective-permute-done | bytes 294944 | tf_op jit(solution)/shard_map/ppermute | solution.py:371
  111.8 13.0 %all-to-all-start.1 = ((bf16[64,6,384]{2,1,0:T(8,128)(2,1)}), bf16[64,6,384]{2,1,0:T(8,128)(2,1)S(1)}, u32[]{:S(2)}, u32[]{:S(2)}) async-start(bf16[64,6,384]{2,1,0:T(8,128)(2,1)} %reshape.132), calls=%async_computation.1 | async-start | bytes 786432 | tf_op jit(solution)/shard_map/all_to_all | solution.py:483
  124.7 10.1 %frame_back.1 = bf16[128,1536]{1,0:T(8,128)(2,1)} custom-call(s32[4]{0:T(128)} %copy-done.7, s32[1]{0:T(128)} %bitcast.14.core_ref, bf16[128,1536]{1,0:T(8,128)(2,1)} %bitcast.40, bf16[128,3072]{1,0:T(8,128)(2,1)} %copy-done.4, bf16[192,3072]{1,0:T(8,128)(2,1)} %rest_0_.3, bf16[192,3072]{1,0:T(8,128)(2,1)} %collective-permute-done.1.rest_1_, ...), custom_call_target="tpu_custom_call" | custom-call | flops 2000000000 | bytes 11000000 | tf_op jit(solution)/shard_map/frame_back/pallas_call | solution.py:353
  134.8 2.4 %fusion.14 = bf16[1,256,1536]{2,1,0:T(8,128)(2,1)} fusion(s32[]{:T(128)S(6)} %select_n.143, bf16[64,1536]{1,0:T(8,128)(2,1)} %collective-permute-done.14, bf16[128,1536]{1,0:T(8,128)(2,1)S(1)} %get-tuple-element.48, bf16[64,1536]{1,0:T(8,128)(2,1)} %collective-permute-done.15, pred[256]{0:T(512)(128)(4,1)S(1)} %iota_compare_fusion.4, ...), kind=kLoop, calls=%fused_computation.36 | loop fusion | flops 3538944 | bytes 1573636 | tf_op jit(solution)/shard_map/broadcast_in_dim | solution.py:545
  137.3 2.5 %all-to-all-done.1 = bf16[64,6,384]{2,1,0:T(8,128)(2,1)S(1)} async-done(((bf16[64,6,384]{2,1,0:T(8,128)(2,1)}), bf16[64,6,384]{2,1,0:T(8,128)(2,1)S(1)}, u32[]{:S(2)}, u32[]{:S(2)}) %all-to-all-start.1) | async-done | bytes 294944 | tf_op jit(solution)/shard_map/all_to_all | solution.py:483
  (98 shorter events, 31.1 us)
Async XLA Ops:
  0.6 27.5 %collective-permute-start = (bf16[192,3072]{1,0:T(8,128)(2,1)}, bf16[192,3072]{1,0:T(8,128)(2,1)S(1)}, u32[]{:S(2)}, u32[]{:S(2)}) collective-permute-start(bf16[192,3072]{1,0:T(8,128)(2,1)} %rest_0_.3), channel_id=1, source_target_pairs={{0,2},{2,4},{4,6},{6,0},{1,3},{3,5},{5,7},{7,1},{8,10},{10,12},{12... | collective-permute-start | bytes 3538952 | tf_op jit(solution)/shard_map/ppermute | solution.py:371
  2.8 17.4 %collective-permute-start.1 = (bf16[192,3072]{1,0:T(8,128)(2,1)}, bf16[192,3072]{1,0:T(8,128)(2,1)}, u32[]{:S(2)}, u32[]{:S(2)}) collective-permute-start(bf16[192,3072]{1,0:T(8,128)(2,1)} %rest_0_.3), channel_id=1, source_target_pairs={{0,1},{1,0},{2,3},{3,2},{4,5},{5,4},{6,7},{7,6},{8,9},{9,8},{10,11... | collective-permute-start | bytes 3538952 | tf_op jit(solution)/shard_map/ppermute | solution.py:375
  4.1 28.6 %collective-permute-start.6 = (bf16[192,3072]{1,0:T(8,128)(2,1)}, bf16[192,3072]{1,0:T(8,128)(2,1)S(1)}, u32[]{:S(2)}, u32[]{:S(2)}) collective-permute-start(bf16[192,3072]{1,0:T(8,128)(2,1)} %rest_0_.3), channel_id=1, source_target_pairs={{0,6},{2,0},{4,2},{6,4},{1,7},{3,1},{5,3},{7,5},{8,14},{10,8},{12,... | collective-permute-start | bytes 3538952 | tf_op jit(solution)/shard_map/ppermute | solution.py:371
  12.4 11.1 %collective-permute-start.2 = (bf16[112,1536]{1,0:T(8,128)(2,1)}, bf16[112,1536]{1,0:T(8,128)(2,1)S(1)}, u32[]{:S(2)}, u32[]{:S(2)}) collective-permute-start(bf16[112,1536]{1,0:T(8,128)(2,1)} %pad_maximum_fusion.1), channel_id=1, source_target_pairs={{0,8},{8,16},{16,24},{24,32},{32,40},{40,48},{48,56},{56,64},{64,7... | collective-permute-start | bytes 1032200 | tf_op jit(solution)/shard_map/ppermute | solution.py:24
  15.0 11.5 %collective-permute-start.3 = (bf16[112,1536]{1,0:T(8,128)(2,1)}, bf16[112,1536]{1,0:T(8,128)(2,1)S(1)}, u32[]{:S(2)}, u32[]{:S(2)}) collective-permute-start(bf16[112,1536]{1,0:T(8,128)(2,1)} %pad_maximum_fusion.2), channel_id=1, source_target_pairs={{8,0},{16,8},{24,16},{32,24},{40,32},{48,40},{56,48},{64,56},{72,6... | collective-permute-start | bytes 1032200 | tf_op jit(solution)/shard_map/ppermute | solution.py:24
  20.2 34.8 %copy-start.7 = (s32[4]{0:T(128)}, s32[4]{0:T(128)S(1)}, u32[]{:S(2)}) copy-start(s32[4]{0:T(128)S(1)} %pad_add_fusion.at_ref) | copy-start | bytes 52
  28.1 14.0 %collective-permute-start.8 = (bf16[192,3072]{1,0:T(8,128)(2,1)S(1)}, bf16[192,3072]{1,0:T(8,128)(2,1)}, u32[]{:S(2)}, u32[]{:S(2)}) collective-permute-start(bf16[192,3072]{1,0:T(8,128)(2,1)S(1)} %collective-permute-done.rest_2_), channel_id=1, source_target_pairs={{0,1},{1,0},{2,3},{3,2},{4,5},{5,4},{6,7},{7,6},{8,9},{9,8},{10,11... | collective-permute-start | bytes 3538952 | tf_op jit(solution)/shard_map/ppermute | solution.py:375
  32.6 9.5 %collective-permute-start.9 = (bf16[192,3072]{1,0:T(8,128)(2,1)S(1)}, bf16[192,3072]{1,0:T(8,128)(2,1)}, u32[]{:S(2)}, u32[]{:S(2)}) collective-permute-start(bf16[192,3072]{1,0:T(8,128)(2,1)S(1)} %collective-permute-done.6.rest_4_), channel_id=1, source_target_pairs={{0,1},{1,0},{2,3},{3,2},{4,5},{5,4},{6,7},{7,6},{8,9},{9,8},{10,11... | collective-permute-start | bytes 3538952 | tf_op jit(solution)/shard_map/ppermute | solution.py:375
  34.3 17.2 %collective-permute-start.5 = (bf16[96,3072]{1,0:T(8,128)(2,1)}, bf16[96,3072]{1,0:T(8,128)(2,1)}, u32[]{:S(2)}, u32[]{:S(2)}) collective-permute-start(bf16[96,3072]{1,0:T(8,128)(2,1)} %slice.47), channel_id=1, source_target_pairs={{0,2},{2,4},{4,6},{6,0},{1,3},{3,5},{5,7},{7,1},{8,10},{10,12},{12... | collective-permute-start | bytes 1769480 | tf_op jit(solution)/shard_map/ppermute | solution.py:371
  35.4 16.1 %collective-permute-start.7 = (bf16[96,3072]{1,0:T(8,128)(2,1)}, bf16[96,3072]{1,0:T(8,128)(2,1)}, u32[]{:S(2)}, u32[]{:S(2)}) collective-permute-start(bf16[96,3072]{1,0:T(8,128)(2,1)} %slice.53), channel_id=1, source_target_pairs={{0,6},{2,0},{4,2},{6,4},{1,7},{3,1},{5,3},{7,5},{8,14},{10,8},{12,... | collective-permute-start | bytes 1769480 | tf_op jit(solution)/shard_map/ppermute | solution.py:371
  38.5 12.2 %collective-permute-start.10 = (bf16[128,1536]{1,0:T(8,128)(2,1)}, bf16[128,1536]{1,0:T(8,128)(2,1)}, u32[]{:S(2)}, u32[]{:S(2)}) collective-permute-start(bf16[128,1536]{1,0:T(8,128)(2,1)} %fusion.5), channel_id=1, source_target_pairs={{0,128},{64,192},{128,0},{192,64},{1,129},{65,193},{129,1},{193,65... | collective-permute-start | bytes 1179656 | tf_op jit(solution)/shard_map/ppermute | solution.py:371
  51.5 2.7 %collective-permute-start.12 = (bf16[96,3072]{1,0:T(8,128)(2,1)}, bf16[96,3072]{1,0:T(8,128)(2,1)S(1)}, u32[]{:S(2)}, u32[]{:S(2)}) collective-permute-start(bf16[96,3072]{1,0:T(8,128)(2,1)} %collective-permute-done.5.rest_0_.rest_6_), channel_id=1, source_target_pairs={{0,1},{1,0},{2,3},{3,2},{4,5},{5,4},{6,7},{7,6},{8,9},{9,8},{10,11... | collective-permute-start | bytes 1769480 | tf_op jit(solution)/shard_map/ppermute | solution.py:375
  52.3 2.7 %collective-permute-start.13 = (bf16[96,3072]{1,0:T(8,128)(2,1)}, bf16[96,3072]{1,0:T(8,128)(2,1)S(1)}, u32[]{:S(2)}, u32[]{:S(2)}) collective-permute-start(bf16[96,3072]{1,0:T(8,128)(2,1)} %collective-permute-done.7.rest_1_.rest_7_), channel_id=1, source_target_pairs={{0,1},{1,0},{2,3},{3,2},{4,5},{5,4},{6,7},{7,6},{8,9},{9,8},{10,11... | collective-permute-start | bytes 1769480 | tf_op jit(solution)/shard_map/ppermute | solution.py:375
  52.3 18.1 %collective-permute-start.4 = (bf16[128,1536]{1,0:T(8,128)(2,1)S(1)}, bf16[128,1536]{1,0:T(8,128)(2,1)S(1)}, u32[]{:S(2)}, u32[]{:S(2)}) collective-permute-start(bf16[128,1536]{1,0:T(8,128)(2,1)S(1)} %copy-done.10), channel_id=1, source_target_pairs={{0,192},{64,0},{128,64},{192,128},{1,193},{65,1},{129,65},{193,129... | collective-permute-start | bytes 1179656 | tf_op jit(solution)/shard_map/ppermute | solution.py:371
  54.0 16.5 %collective-permute-start.11 = (bf16[128,1536]{1,0:T(8,128)(2,1)S(1)}, bf16[128,1536]{1,0:T(8,128)(2,1)S(1)}, u32[]{:S(2)}, u32[]{:S(2)}) collective-permute-start(bf16[128,1536]{1,0:T(8,128)(2,1)S(1)} %copy-done.10), channel_id=1, source_target_pairs={{0,64},{64,128},{128,192},{192,0},{1,65},{65,129},{129,193},{193,1... | collective-permute-start | bytes 1179656 | tf_op jit(solution)/shard_map/ppermute | solution.py:371
  54.2 16.3 %copy-start.5 = (bf16[96,3072]{1,0:T(8,128)(2,1)}, bf16[96,3072]{1,0:T(8,128)(2,1)S(1)}, u32[]{:S(2)}) copy-start(bf16[96,3072]{1,0:T(8,128)(2,1)S(1)} %collective-permute-done.12.rest_2_.rest_8_) | copy-start | bytes 1769476
  72.0 5.7 %collective-permute-start.16 = (bf16[4,128,1536]{2,1,0:T(8,128)(2,1)S(1)}, bf16[4,128,1536]{2,1,0:T(8,128)(2,1)}, u32[]{:S(2)}, u32[]{:S(2)}) collective-permute-start(bf16[4,128,1536]{2,1,0:T(8,128)(2,1)S(1)} %pad_maximum_fusion), channel_id=1, source_target_pairs={{0,1},{1,0},{2,3},{3,2},{4,5},{5,4},{6,7},{7,6},{8,9},{9,8},{10,11... | collective-permute-start | bytes 4718600 | tf_op jit(solution)/shard_map/ppermute | solution.py:375
  73.3 16.8 %all-to-all-start = ((bf16[8,128,384]{2,1,0:T(8,128)(2,1)}), bf16[8,128,384]{2,1,0:T(8,128)(2,1)}, u32[]{:S(2)}, u32[]{:S(2)}) async-start(bf16[8,128,384]{2,1,0:T(8,128)(2,1)} %get-tuple-element.54), calls=%async_computation | async-start | bytes 1572864 | tf_op jit(solution)/shard_map/all_to_all | solution.py:538
  91.8 18.9 %collective-permute-start.19 = (bf16[384,384]{1,0:T(8,128)(2,1)S(1)}, bf16[384,384]{1,0:T(8,128)(2,1)S(1)}, u32[]{:S(2)}, u32[]{:S(2)}) collective-permute-start(bf16[384,384]{1,0:T(8,128)(2,1)S(1)} %convolution_convert_fusion), channel_id=1, source_target_pairs={{0,6},{2,0},{4,2},{6,4},{1,7},{3,1},{5,3},{7,5},{8,14},{10,8},{12,... | collective-permute-start | bytes 884744 | tf_op jit(solution)/shard_map/ppermute | solution.py:371
  96.9 13.8 %collective-permute-start.18 = (bf16[384,384]{1,0:T(8,128)(2,1)S(1)}, bf16[384,384]{1,0:T(8,128)(2,1)S(1)}, u32[]{:S(2)}, u32[]{:S(2)}) collective-permute-start(bf16[384,384]{1,0:T(8,128)(2,1)S(1)} %convolution_convert_fusion.1), channel_id=1, source_target_pairs={{0,2},{2,4},{4,6},{6,0},{1,3},{3,5},{5,7},{7,1},{8,10},{10,12},{12... | collective-permute-start | bytes 884744 | tf_op jit(solution)/shard_map/ppermute | solution.py:371
  98.8 11.9 %collective-permute-start.17 = (bf16[384,384]{1,0:T(8,128)(2,1)S(1)}, bf16[384,384]{1,0:T(8,128)(2,1)S(1)}, u32[]{:S(2)}, u32[]{:S(2)}) collective-permute-start(bf16[384,384]{1,0:T(8,128)(2,1)S(1)} %convolution_convert_fusion.2), channel_id=1, source_target_pairs={{0,4},{2,6},{4,0},{6,2},{1,5},{3,7},{5,1},{7,3},{8,12},{10,14},{12... | collective-permute-start | bytes 884744 | tf_op jit(solution)/shard_map/ppermute | solution.py:371
  101.0 33.8 %collective-permute-start.14 = (bf16[64,1536]{1,0:T(8,128)(2,1)}, bf16[64,1536]{1,0:T(8,128)(2,1)}, u32[]{:S(2)}, u32[]{:S(2)}) collective-permute-start(bf16[64,1536]{1,0:T(8,128)(2,1)} %get-tuple-element.62), channel_id=1, source_target_pairs={{0,8},{8,16},{16,24},{24,32},{32,40},{40,48},{48,56},{56,64},{64,7... | collective-permute-start | bytes 589832 | tf_op jit(solution)/shard_map/ppermute | solution.py:24
  105.2 29.7 %collective-permute-start.15 = (bf16[64,1536]{1,0:T(8,128)(2,1)}, bf16[64,1536]{1,0:T(8,128)(2,1)}, u32[]{:S(2)}, u32[]{:S(2)}) collective-permute-start(bf16[64,1536]{1,0:T(8,128)(2,1)} %get-tuple-element.61), channel_id=1, source_target_pairs={{8,0},{16,8},{24,16},{32,24},{40,32},{48,40},{56,48},{64,56},{72,6... | collective-permute-start | bytes 589832 | tf_op jit(solution)/shard_map/ppermute | solution.py:24
  111.8 28.1 %all-to-all-start.1 = ((bf16[64,6,384]{2,1,0:T(8,128)(2,1)}), bf16[64,6,384]{2,1,0:T(8,128)(2,1)S(1)}, u32[]{:S(2)}, u32[]{:S(2)}) async-start(bf16[64,6,384]{2,1,0:T(8,128)(2,1)} %reshape.132), calls=%async_computation.1 | async-start | bytes 786432 | tf_op jit(solution)/shard_map/all_to_all | solution.py:483
  (15 other events, 96.2 us)
